TPU v7x, 32 devices: a whole 2x2x4 slice. The times are simulated.
32 devices in a mesh: dp: 8 (over y, x, core), tensor: 4 (over z).
Axes of the slice: x: 2, y: 2, z: 4, core: 2. Of those that a mesh axis runs over, the one named last changes fastest.
Arguments:
- block_input: bfloat16 [8192, 2048], P(('dp', 'tensor')), may hold values from -6 to 6
- cotangent: bfloat16 [8192, 2048], P(('dp', 'tensor')), may hold values from -6 to 6
- noise_embed: bfloat16 [32, 2048], P('dp'), may hold values from -6 to 6
- image_sizes: int32 [8, 4], P('dp'), may hold values from 0 to 1024, as said below
- attend_weight: bfloat16 [2048, 6144], P('dp', 'tensor'), may hold values from -0.125 to 0.125
- merge_weight: bfloat16 [2048, 2048], P('tensor', 'dp'), may hold values from -1 to 1
- up_weight: bfloat16 [2048, 8192], P('dp', 'tensor'), may hold values from -0.125 to 0.125
- down_weight: bfloat16 [8192, 2048], P('tensor', 'dp'), may hold values from -0.125 to 0.125
- modulate_weight: bfloat16 [2048, 12288], P('dp', 'tensor'), may hold values from -0.1875 to 0.1875
Outputs:
- block_output: bfloat16 [8192, 2048], P(('dp', 'tensor'))
- input_grad: bfloat16 [8192, 2048], P(('dp', 'tensor'))
- noise_grad: float32 [32, 2048], P('dp')
- attend_grad: float32 [2048, 6144], P('dp', 'tensor')
- merge_grad: float32 [2048, 2048], P('tensor', 'dp')
- up_grad: float32 [2048, 8192], P('dp', 'tensor')
- down_grad: float32 [8192, 2048], P('tensor', 'dp')
- modulate_grad: float32 [2048, 12288], P('dp', 'tensor')
Inputs may be any that keep to these rules, and one draw needn't show every extreme that they name: `image_sizes`: each row lists the token counts of one bucket's images in order, each a multiple of 256, the first one nonzero; a row sums to at most 1024, and some row holds one image of 1024 tokens and empty slots.
All inputs are finite; a program needn't handle non-finite values.
Results may differ from a plain program's by a relative error of at most 0.02.
The roundings to bfloat16 on the way count: a program that leaves them out, or rounds other values in their place, can miss the bound.
Values may be sent and summed in bfloat16 or wider, within the bound.
A program may use at most 320 MiB of HBM per device.

v0:
```python
import jax
import jax.numpy as jnp
from jax import lax
from jax.sharding import PartitionSpec as P

HEAD_DIM = 128


exact_mode = lax.Precision.HIGHEST
masked_score = -1e30


def normalize(values):
    return values * lax.rsqrt(jnp.mean(values * values, axis=-1, keepdims=True) + 1e-06)


def modulate_rows(values, scale_part, shift_part):
    return normalize(values) * (1.0 + scale_part) + shift_part


def gelu_exact(values):
    return jax.nn.gelu(values, approximate=False)


def block_scores(query_part, keys, image_of, first_row, block_rows, score_scale):
    scores = (
        jnp.einsum("qhd,khd->hqk", query_part, keys, preferred_element_type=jnp.float32)
        * score_scale
    )
    same_image = image_of[first_row : first_row + block_rows, None] == image_of[None, :]
    return jnp.where(same_image[None], scores, masked_score)


def attention_forward(queries, keys, values, image_of, block_rows, score_scale):
    outputs = []
    log_parts = []
    for number in range(queries.shape[0] // block_rows):
        first_row = number * block_rows
        query_part = queries[first_row : first_row + block_rows]
        scores = block_scores(query_part, keys, image_of, first_row, block_rows, score_scale)
        highest = jnp.max(scores, axis=-1, keepdims=True)
        powers = jnp.exp(scores - highest)
        totals = jnp.sum(powers, axis=-1, keepdims=True)
        probs = powers / totals
        log_parts.append(highest + jnp.log(totals))
        outputs.append(
            jnp.einsum(
                "hqk,khd->qhd",
                probs.astype(jnp.bfloat16),
                values,
                preferred_element_type=jnp.float32,
            ).astype(jnp.bfloat16)
        )
    return (jnp.concatenate(outputs, axis=0), log_parts)


def attention_backward(
    queries, keys, values, grad_out, image_of, log_parts, block_rows, score_scale
):
    key_grad = jnp.zeros(keys.shape, jnp.float32)
    value_grad = jnp.zeros(values.shape, jnp.float32)
    query_grads = []
    for number in range(queries.shape[0] // block_rows):
        first_row = number * block_rows
        query_part = queries[first_row : first_row + block_rows]
        grad_part = grad_out[first_row : first_row + block_rows]
        scores = block_scores(query_part, keys, image_of, first_row, block_rows, score_scale)
        probs = jnp.exp(scores - log_parts[number])
        grad_probs = jnp.einsum(
            "qhd,khd->hqk", grad_part, values, preferred_element_type=jnp.float32
        )
        inner = jnp.sum(probs * grad_probs, axis=-1, keepdims=True)
        grad_scores = (probs * (grad_probs - inner)).astype(jnp.bfloat16)
        query_grads.append(
            (
                jnp.einsum("hqk,khd->qhd", grad_scores, keys, preferred_element_type=jnp.float32)
                * score_scale
            ).astype(jnp.bfloat16)
        )
        key_grad = (
            key_grad
            + jnp.einsum(
                "hqk,qhd->khd", grad_scores, query_part, preferred_element_type=jnp.float32
            )
            * score_scale
        )
        value_grad = value_grad + jnp.einsum(
            "hqk,qhd->khd",
            probs.astype(jnp.bfloat16),
            grad_part,
            preferred_element_type=jnp.float32,
        )
    query_all = jnp.concatenate(query_grads, axis=0)
    stacked = jnp.stack(
        [query_all, key_grad.astype(jnp.bfloat16), value_grad.astype(jnp.bfloat16)], axis=2
    )
    return stacked.reshape(queries.shape[0], -1)


def on_device(
    block_input,
    cotangent,
    noise_embed,
    image_sizes,
    attend_weight,
    merge_weight,
    up_weight,
    down_weight,
    modulate_weight,
):
    whole_input, whole_cotan = (
        lax.all_gather(block_input, "tensor", axis=0, tiled=True),
        lax.all_gather(cotangent, "tensor", axis=0, tiled=True),
    )
    attend_full, merge_full, up_full, down_full, modulate_full = (
        lax.all_gather(attend_weight, "dp", axis=0, tiled=True),
        lax.all_gather(merge_weight, "dp", axis=1, tiled=True),
        lax.all_gather(up_weight, "dp", axis=0, tiled=True),
        lax.all_gather(down_weight, "dp", axis=1, tiled=True),
        lax.all_gather(modulate_weight, "dp", axis=0, tiled=True),
    )
    tokens = whole_input.shape[0]
    width = whole_input.shape[1]
    own_rows = block_input.shape[0]
    first_own = lax.axis_index("tensor") * own_rows
    sizes_row = image_sizes[0]
    images = sizes_row.shape[0]
    ends = jnp.cumsum(sizes_row)
    places = jnp.arange(tokens, dtype=jnp.int32)
    image_of = jnp.sum((places[:, None] >= ends[None, :]).astype(jnp.int32), axis=1)
    select = (image_of[:, None] == jnp.arange(images, dtype=jnp.int32)[None, :]).astype(jnp.float32)

    def own_part(values):
        return lax.dynamic_slice_in_dim(values, first_own, own_rows, 0)

    noise_full = noise_embed.astype(jnp.float32)
    noise_act, silu_back = jax.vjp(jax.nn.silu, noise_full)
    noise_low = noise_act.astype(jnp.bfloat16)
    modulation_cols = jnp.dot(noise_low, modulate_full, preferred_element_type=jnp.float32)
    modulation = lax.all_gather(modulation_cols, "tensor", axis=1, tiled=True)
    token_parts = [
        jnp.dot(select, modulation[:, number * width : (number + 1) * width], precision=exact_mode)
        for number in range(6)
    ]
    shift_first, scale_first, gate_first, shift_second, scale_second, gate_second = token_parts
    inputs_full = whole_input.astype(jnp.float32)
    hidden_first_f, back_first = jax.vjp(modulate_rows, inputs_full, scale_first, shift_first)
    hidden_first = hidden_first_f.astype(jnp.bfloat16)
    heads_local = attend_full.shape[1] // (3 * HEAD_DIM)
    packed = jnp.dot(hidden_first, attend_full, preferred_element_type=jnp.float32)
    packed = packed.reshape(tokens, heads_local, 3, HEAD_DIM).astype(jnp.bfloat16)
    queries = packed[:, :, 0]
    keys = packed[:, :, 1]
    values = packed[:, :, 2]
    block_rows = min(512, tokens)
    score_scale = HEAD_DIM ** (-0.5)
    attended3, log_parts = attention_forward(
        queries, keys, values, image_of, block_rows, score_scale
    )
    attended = attended3.reshape(tokens, heads_local * HEAD_DIM)
    attn_out = lax.psum(jnp.dot(attended, merge_full, preferred_element_type=jnp.float32), "tensor")
    middle = inputs_full + gate_first * attn_out
    hidden_second_f, back_second = jax.vjp(modulate_rows, middle, scale_second, shift_second)
    hidden_second = hidden_second_f.astype(jnp.bfloat16)
    pre_act = jnp.dot(hidden_second, up_full, preferred_element_type=jnp.float32)
    activated_f, gelu_back = jax.vjp(gelu_exact, pre_act)
    activated = activated_f.astype(jnp.bfloat16)
    mlp_terms = jnp.dot(activated, down_full, preferred_element_type=jnp.float32)
    grad_full = whole_cotan.astype(jnp.float32)
    mlp_out = lax.psum(mlp_terms.astype(jnp.bfloat16), "tensor").astype(jnp.float32)
    block_output = own_part(middle + gate_second * mlp_out).astype(jnp.bfloat16)
    d_gate_second = grad_full * mlp_out
    d_mlp = (gate_second * grad_full).astype(jnp.bfloat16)
    down_local = jnp.dot(activated.T, d_mlp, preferred_element_type=jnp.float32)
    d_act = jnp.dot(d_mlp, down_full.T, preferred_element_type=jnp.float32)
    d_pre = gelu_back(d_act)[0].astype(jnp.bfloat16)
    up_local = jnp.dot(hidden_second.T, d_pre, preferred_element_type=jnp.float32)
    d_hidden_second = lax.psum(
        jnp.dot(d_pre, up_full.T, preferred_element_type=jnp.float32).astype(jnp.bfloat16), "tensor"
    ).astype(jnp.float32)
    d_mid_norm, d_scale_second, d_shift_second = back_second(d_hidden_second)
    d_middle = grad_full + d_mid_norm
    d_gate_first = d_middle * attn_out
    d_attn = (gate_first * d_middle).astype(jnp.bfloat16)
    merge_local = jnp.dot(attended.T, d_attn, preferred_element_type=jnp.float32)
    d_attended = jnp.dot(d_attn, merge_full.T, preferred_element_type=jnp.float32).astype(
        jnp.bfloat16
    )
    d_attended3 = d_attended.reshape(tokens, heads_local, HEAD_DIM)
    d_qkv = attention_backward(
        queries, keys, values, d_attended3, image_of, log_parts, block_rows, score_scale
    )
    attend_local = jnp.dot(hidden_first.T, d_qkv, preferred_element_type=jnp.float32)
    d_first_terms = jnp.dot(d_qkv, attend_full.T, preferred_element_type=jnp.float32)

    def image_sum(part_grad, chosen):
        return jnp.dot(chosen.T, part_grad, precision=exact_mode)

    d_hidden_first = lax.psum(d_first_terms.astype(jnp.bfloat16), "tensor").astype(jnp.float32)
    d_in_norm, d_scale_first, d_shift_first = back_first(d_hidden_first)
    input_grad = own_part(d_middle + d_in_norm).astype(jnp.bfloat16)
    token_grads = [
        d_shift_first,
        d_scale_first,
        d_gate_first,
        d_shift_second,
        d_scale_second,
        d_gate_second,
    ]
    d_modulation = jnp.concatenate(
        [image_sum(part_grad, select) for part_grad in token_grads], axis=1
    ).astype(jnp.bfloat16)
    own_cols = modulate_weight.shape[1]
    d_mod_cols = lax.dynamic_slice_in_dim(
        d_modulation, lax.axis_index("tensor") * own_cols, own_cols, 1
    )
    modulate_local = jnp.dot(noise_low.T, d_mod_cols, preferred_element_type=jnp.float32)
    noise_sum = lax.psum(
        jnp.dot(d_mod_cols, modulate_full.T, preferred_element_type=jnp.float32).astype(
            jnp.bfloat16
        ),
        "tensor",
    ).astype(jnp.float32)
    noise_grad = silu_back(noise_sum)[0]
    attend_part, merge_part, up_part, down_part, modulate_part = (
        lax.psum_scatter(
            attend_local.astype(jnp.bfloat16), "dp", scatter_dimension=0, tiled=True
        ).astype(jnp.float32),
        lax.psum_scatter(
            merge_local.astype(jnp.bfloat16), "dp", scatter_dimension=1, tiled=True
        ).astype(jnp.float32),
        lax.psum_scatter(
            up_local.astype(jnp.bfloat16), "dp", scatter_dimension=0, tiled=True
        ).astype(jnp.float32),
        lax.psum_scatter(
            down_local.astype(jnp.bfloat16), "dp", scatter_dimension=1, tiled=True
        ).astype(jnp.float32),
        lax.psum_scatter(
            modulate_local.astype(jnp.bfloat16), "dp", scatter_dimension=0, tiled=True
        ).astype(jnp.float32),
    )
    return (
        block_output,
        input_grad,
        noise_grad,
        attend_part,
        merge_part,
        up_part,
        down_part,
        modulate_part,
    )


def solution(mesh):
    in_specs = (
        P(("dp", "tensor"), None),
        P(("dp", "tensor"), None),
        P("dp", None),
        P("dp", None),
        P("dp", "tensor"),
        P("tensor", "dp"),
        P("dp", "tensor"),
        P("tensor", "dp"),
        P("dp", "tensor"),
    )
    out_specs = (
        P(("dp", "tensor"), None),
        P(("dp", "tensor"), None),
        P("dp", None),
        P("dp", "tensor"),
        P("tensor", "dp"),
        P("dp", "tensor"),
        P("tensor", "dp"),
        P("dp", "tensor"),
    )
    return jax.shard_map(
        on_device, mesh=mesh, in_specs=in_specs, out_specs=out_specs, check_vma=False
    )
```

profile of v0, /device:TPU:0, one launch (start us, length us, event | category | flops | bytes accessed | tf_op | source)
XLA Modules:
  0.0 1653.7 jit_solution(14905621734195895460)
XLA Ops:
  12.6 80.6 %all-gather.8.cloned.1.call-done = bf16[1024,2048]{1,0:T(8,128)(2,1)} async-done(((bf16[256,2048]{1,0:T(8,128)(2,1)}), bf16[1024,2048]{1,0:T(8,128)(2,1)}) %all-gather.8.cloned.1.call-update) | async-done | bytes 4194320 | tf_op jit(solution)/shard_map/all_gather | solution.py:112
  96.8 68.9 %all-gather.10.cloned.1.call-done = bf16[2048,3072]{1,0:T(8,128)(2,1)} async-done(((bf16[256,3072]{1,0:T(8,128)(2,1)}), bf16[2048,3072]{1,0:T(8,128)(2,1)}) %all-gather.10.cloned.1.call-update) | async-done | bytes 12582928 | tf_op jit(solution)/shard_map/all_gather | solution.py:120
  172.0 13.8 all_gather.26
  199.5 13.7 all-gather.12.cloned.1.call-done
  213.2 11.2 convolution_convert_fusion.5
  264.1 277.2 %all-reduce.5.cloned.1.call-done = f32[1024,2048]{1,0:T(8,128)} async-done(((f32[1024,2048]{1,0:T(8,128)}), f32[1024,2048]{1,0:T(8,128)}) %all-reduce.5.cloned.1.call-update) | async-done | bytes 8388624 | tf_op jit(solution)/shard_map/psum | solution.py:161
  560.5 36.0 %all-gather.16.cloned.1.call-done = bf16[2048,2048]{1,0:T(8,128)(2,1)} async-done(((bf16[256,2048]{1,0:T(8,128)(2,1)}), bf16[2048,2048]{1,0:T(8,128)(2,1)}) %all-gather.16.cloned.1.call-update) | async-done | bytes 8388624 | tf_op jit(solution)/shard_map/all_gather | solution.py:118
  596.5 31.3 %multiply_convert_fusion.3 = (bf16[1024,2048]{1,0:T(8,128)(2,1)}, f32[1024,2048]{1,0:T(8,128)}, f32[1024,2048]{1,0:T(8,128)}) fusion(bf16[1024,2048]{1,0:T(8,128)(2,1)} %add_convert_fusion.1, bf16[2048,2048]{1,0:T(8,128)(2,1)} %all-gather.16.cloned.1.call-done), kind=kOutput, calls=%fused_computation.27 | convolution fusion | flops 8726249472 | bytes 33554432 | tf_op jit(solution)/shard_map/dot_general | solution.py:165
  627.8 51.1 %all-gather.20.cloned.1.call-done = bf16[1024,2048]{1,0:T(8,128)(2,1)} async-done(((bf16[256,2048]{1,0:T(8,128)(2,1)}), bf16[1024,2048]{1,0:T(8,128)(2,1)}) %all-gather.20.cloned.1.call-update) | async-done | bytes 4194320 | tf_op jit(solution)/shard_map/all_gather | solution.py:113
  678.9 56.4 %all-gather.18.cloned.1.call-done = bf16[2048,2048]{1,0:T(8,128)(2,1)} async-done(((bf16[2048,256]{1,0:T(8,128)(2,1)}), bf16[2048,2048]{1,0:T(8,128)(2,1)}) %all-gather.18.cloned.1.call-update) | async-done | bytes 8388624 | tf_op jit(solution)/shard_map/all_gather | solution.py:119
  735.3 22.0 %add_convert_fusion = bf16[1024,2048]{1,0:T(8,128)(2,1)} fusion(f32[1024,2048]{1,0:T(8,128)} %get-tuple-element.15, f32[1024,2048]{1,0:T(8,128)} %get-tuple-element.29, bf16[2048,2048]{1,0:T(8,128)(2,1)} %all-gather.18.cloned.1.call-done, f32[1024,2048]{1,0:T(8,128)} %fusion.62, bf16[1024,2048]{1,0:T(8,128)(2,1)} %all-gather.20.cloned.1.call-done), kind=kOutput, calls=%fused_computation.26 | convolution fusion | flops 8625586176 | bytes 41943040 | tf_op jit(solution)/shard_map/dot_general | solution.py:175
  757.3 13.9 convolution_convert_fusion.6
  771.3 14.3 convolution_convert_fusion.7
  785.6 140.8 %all-reduce.7.cloned.1.call-done = bf16[1024,2048]{1,0:T(8,128)(2,1)} async-done(((bf16[1024,2048]{1,0:T(8,128)(2,1)}), bf16[1024,2048]{1,0:T(8,128)(2,1)}) %all-reduce.7.cloned.1.call-update) | async-done | bytes 4194320 | tf_op jit(solution)/shard_map/psum | solution.py:178
  934.9 18.3 %multiply_convert_fusion.2 = (bf16[1024,2048]{1,0:T(8,128)(2,1)}, f32[1024,2048]{1,0:T(8,128)}) fusion(f32[1024,2048]{1,0:T(8,128)} %get-tuple-element.28, f32[1024,2048]{1,0:T(8,128)} %copy-done, f32[1024]{0:T(1024)S(1)} %multiply_multiply_fusion.6, f32[1024]{0:T(1024)S(1)} %fusion.93, f32[1024,2048]{1,0:T(8,128)} %fusion.61, ...), kind=kLoop, calls=%fused_computation.23 | loop fusion | flops 23068672 | bytes 46145536 | tf_op jit(solution)/shard_map/convert_element_type | solution.py:184
  1003.5 14.4 convolution_convert_fusion.2
  1018.0 15.4 convolution_convert_fusion.1
  1033.5 11.2 convolution_convert_fusion.3
  1044.8 243.1 %all-reduce.9.cloned.1.call-done = (bf16[1024,2048]{1,0:T(8,128)(2,1)}, bf16[1024,2048]{1,0:T(8,128)(2,1)}) async-done(((bf16[1024,2048]{1,0:T(8,128)(2,1)}, bf16[1024,2048]{1,0:T(8,128)(2,1)}), (bf16[1024,2048]{1,0:T(8,128)(2,1)}, bf16[1024,2048]{1,0:T(8,128)(2,1)})) %all-reduce.9.cloned.1.call-update) | async-done | bytes 8388624 | tf_op jit(solution)/shard_map/psum | solution.py:170
  1350.3 56.8 %reduce-scatter.10.cloned.1.call-done = bf16[256,2048]{1,0:T(8,128)(2,1)} async-done(((bf16[2048,2048]{1,0:T(8,128)(2,1)}), bf16[256,2048]{1,0:T(8,128)(2,1)}) %reduce-scatter.10.cloned.1.call-update) | async-done | bytes 1048592 | tf_op jit(solution)/shard_map/reduce_scatter | solution.py:232
  1409.9 72.4 %reduce-scatter.12.cloned.1.call-done = bf16[2048,256]{1,0:T(8,128)(2,1)} async-done(((bf16[2048,2048]{1,0:T(8,128)(2,1)}), bf16[2048,256]{1,0:T(8,128)(2,1)}) %reduce-scatter.12.cloned.1.call-update) | async-done | bytes 1048592 | tf_op jit(solution)/shard_map/reduce_scatter | solution.py:235
  1492.9 18.7 %psum.39 = bf16[4,2048]{1,0:T(4,128)(2,1)S(1)} all-reduce(bf16[4,2048]{1,0:T(4,128)(2,1)S(1)} %convolution_convert_fusion.9), channel_id=1, replica_groups=mesh['dp'=8,'tensor'=4] {'tensor'}, use_global_device_ids=true, to_apply=%region_16.17 | all-reduce | flops 8192 | bytes 32768 | tf_op jit(solution)/shard_map/psum | solution.py:218
  1519.1 28.2 %reduce-scatter.6.cloned.1.call-done = bf16[256,1536]{1,0:T(8,128)(2,1)} async-done(((bf16[2048,1536]{1,0:T(8,128)(2,1)}), bf16[256,1536]{1,0:T(8,128)(2,1)}) %reduce-scatter.6.cloned.1.call-update) | async-done | bytes 786448 | tf_op jit(solution)/shard_map/reduce_scatter | solution.py:226
  1549.7 93.7 %reduce-scatter.14.cloned.1.call-done = bf16[256,3072]{1,0:T(8,128)(2,1)} async-done(((bf16[2048,3072]{1,0:T(8,128)(2,1)}), bf16[256,3072]{1,0:T(8,128)(2,1)}) %reduce-scatter.14.cloned.1.call-update) | async-done | bytes 1572880 | tf_op jit(solution)/shard_map/reduce_scatter | solution.py:238
  (171 shorter events, 235.5 us)
Async XLA Ops:
  7.2 158.5 %copy-start.21 = (bf16[4,2048]{1,0:T(4,128)(2,1)S(1)}, bf16[4,2048]{1,0:T(4,128)(2,1)}, u32[]{:S(2)}) copy-start(bf16[4,2048]{1,0:T(4,128)(2,1)} %param.11) | copy-start | bytes 49156
  7.2 86.0 %all-gather.8.cloned.1.call-start = ((), (), s32[]{:S(2)}) async-start(), calls=%async_computation.5 | async-start | bytes 5242880 | tf_op jit(solution)/shard_map/all_gather | solution.py:112
  7.9 157.8 %all-gather.10.cloned.1.call-start = ((), (), s32[]{:S(2)}) async-start(), calls=%async_computation.6 | async-start | bytes 14155776 | tf_op jit(solution)/shard_map/all_gather | solution.py:120
  8.7 204.5 %all-gather.12.cloned.1.call-start = ((), (), s32[]{:S(2)}) async-start(), calls=%async_computation.7 | async-start | bytes 7077888 | tf_op jit(solution)/shard_map/all_gather | solution.py:116
  9.4 233.7 %all-gather.14.cloned.1.call-start = ((), (), s32[]{:S(2)}) async-start(), calls=%async_computation.8 | async-start | bytes 2359296 | tf_op jit(solution)/shard_map/all_gather | solution.py:117
  10.0 531.4 %all-reduce.5.cloned.1.call-start = ((), (), s32[]{:S(2)}) async-start(), calls=%async_computation.9 | async-start | bytes 16777216 | tf_op jit(solution)/shard_map/psum | solution.py:161
  10.9 540.4 %copy-start.16 = (s32[1024]{0:T(1024)}, s32[1024]{0:T(1024)S(1)}, u32[]{:S(2)}) copy-start(s32[1024]{0:T(1024)S(1)} %convert_reduce_fusion) | copy-start | bytes 12292
  96.8 92.5 %copy-start.23 = (f32[1024]{0:T(1024)}, f32[1024]{0:T(1024)S(1)}, u32[]{:S(2)}) copy-start(f32[1024]{0:T(1024)S(1)} %fusion.92) | copy-start | bytes 12292
  172.0 20.6 %copy-start.2 = (bf16[1024,2048]{1,0:T(8,128)(2,1)S(1)}, bf16[1024,2048]{1,0:T(8,128)(2,1)}, u32[]{:S(2)}) copy-start(bf16[1024,2048]{1,0:T(8,128)(2,1)} %all-gather.8.cloned.1.call-done) | copy-start | bytes 12582916
  250.4 346.1 %all-gather.16.cloned.1.call-start = ((), (), s32[]{:S(2)}) async-start(), calls=%async_computation.10 | async-start | bytes 9437184 | tf_op jit(solution)/shard_map/all_gather | solution.py:118
  250.9 427.9 %all-gather.20.cloned.1.call-start = ((), (), s32[]{:S(2)}) async-start(), calls=%async_computation.12 | async-start | bytes 5242880 | tf_op jit(solution)/shard_map/all_gather | solution.py:113
  251.7 483.6 %all-gather.18.cloned.1.call-start = ((), (), s32[]{:S(2)}) async-start(), calls=%async_computation.11 | async-start | bytes 9437184 | tf_op jit(solution)/shard_map/all_gather | solution.py:119
  252.4 674.0 %all-reduce.7.cloned.1.call-start = ((), (), s32[]{:S(2)}) async-start(), calls=%async_computation.13 | async-start | bytes 8388608 | tf_op jit(solution)/shard_map/psum | solution.py:178
  541.3 13.2 copy-start.1
  771.3 516.7 %all-reduce.9.cloned.1.call-start = ((), (), s32[]{:S(2)}) async-start(), calls=%async_computation.19 | async-start | bytes 16777216 | tf_op jit(solution)/shard_map/psum | solution.py:170
  926.4 32.2 %slice-start.2 = ((s8[8388608]{0:T(1024)(128)(4,1)}), s8[4194304]{0:T(1024)(128)(4,1)S(1)}, s32[]{:S(2)}) async-start(s8[8388608]{0:T(1024)(128)(4,1)} %bitcast.103), calls=%async_computation.22 | async-start | bytes 8388608
  934.9 23.6 %slice-start.3 = ((s8[8388608]{0:T(1024)(128)(4,1)}), s8[4194304]{0:T(1024)(128)(4,1)S(1)}, s32[]{:S(2)}) async-start(s8[8388608]{0:T(1024)(128)(4,1)} %bitcast.103), calls=%async_computation.23 | async-start | bytes 8388608
  997.2 335.2 %reduce-scatter.8.cloned.1.call-start = ((), (), s32[]{:S(2)}) async-start(), calls=%async_computation.15 | async-start | bytes 2359296 | tf_op jit(solution)/shard_map/reduce_scatter | solution.py:229
  1003.5 403.6 %reduce-scatter.10.cloned.1.call-start = ((), (), s32[]{:S(2)}) async-start(), calls=%async_computation.16 | async-start | bytes 9437184 | tf_op jit(solution)/shard_map/reduce_scatter | solution.py:232
  1018.0 464.2 %reduce-scatter.12.cloned.1.call-start = ((), (), s32[]{:S(2)}) async-start(), calls=%async_computation.17 | async-start | bytes 9437184 | tf_op jit(solution)/shard_map/reduce_scatter | solution.py:235
  1033.5 254.5 %copy-start.17 = (s32[1024]{0:T(1024)S(1)}, s32[1024]{0:T(1024)}, u32[]{:S(2)}) copy-start(s32[1024]{0:T(1024)} %copy-done.16) | copy-start | bytes 12292
  1033.5 513.8 %reduce-scatter.6.cloned.1.call-start = ((), (), s32[]{:S(2)}) async-start(), calls=%async_computation.14 | async-start | bytes 7077888 | tf_op jit(solution)/shard_map/reduce_scatter | solution.py:226
  1044.7 246.2 %copy-start.24 = (f32[1024]{0:T(1024)S(1)}, f32[1024]{0:T(1024)}, u32[]{:S(2)}) copy-start(f32[1024]{0:T(1024)} %copy-done.23) | copy-start | bytes 12292
  1044.8 598.7 %reduce-scatter.14.cloned.1.call-start = ((), (), s32[]{:S(2)}) async-start(), calls=%async_computation.18 | async-start | bytes 14155776 | tf_op jit(solution)/shard_map/reduce_scatter | solution.py:238
  (26 other events, 147.3 us)
Sparse Core Ops, SparseCore 0:
  9.6 83.5 all-gather.7
  95.0 70.6 all-gather.9
  167.6 45.5 all-gather.11
  214.9 28.1 all-gather.13
  250.5 290.8 all-reduce.4
  543.1 53.3 all-gather.15
  598.1 80.7 all-gather.19
  680.7 54.4 all-gather.17
  771.4 154.9 all-reduce.6
  997.4 290.5 all-reduce.8
  1292.2 40.2 reduce-scatter.7
  1335.8 71.2 reduce-scatter.9
  1410.9 71.2 reduce-scatter.11
  1485.5 61.7 reduce-scatter.5
  1551.0 92.4 reduce-scatter.13
where the time goes:
time: 1660 us; the launch traced here: 1650 us
  waiting for transfers between devices  1230 us (74%)
  matrix products  278 us (17%)
  other arithmetic  86.2 us (5%)
  blocking collectives  32.5 us (2%)
    psum x1, waiting for transfers between devices, on_device(): lax.psum(jnp.dot(attended, merge_full, preferred_element_type=jnp.float32...  277 us
    psum x1, waiting for transfers between devices, on_device(): lax.psum(mlp_terms.astype(jnp.bfloat16), 'tensor').astype(jnp.float32)  243 us
    psum x1, waiting for transfers between devices, on_device(): lax.psum(jnp.dot(d_pre, up_full.T, preferred_element_type=jnp.float32).as...  141 us
    reduce_scatter x1, waiting for transfers between devices, on_device(): lax.psum_scatter(modulate_local.astype(jnp.bfloat16), 'dp', scatter_dimen...  93.7 us
    all_gather x1, waiting for transfers between devices, on_device(): lax.all_gather(block_input, 'tensor', axis=0, tiled=True)  80.6 us
    reduce_scatter x1, waiting for transfers between devices, on_device(): lax.psum_scatter(down_local.astype(jnp.bfloat16), 'dp', scatter_dimension...  72.4 us
    all_gather x1, waiting for transfers between devices, on_device(): lax.all_gather(modulate_weight, 'dp', axis=0, tiled=True)  68.9 us
    reduce_scatter x1, waiting for transfers between devices, on_device(): lax.psum_scatter(up_local.astype(jnp.bfloat16), 'dp', scatter_dimension=0...  56.8 us
  transfers between devices with their start and end apart: 15, of which 15 were waited for; matrix products, arithmetic and copies ran while one was open for 15% of the time, Pallas kernels for 0%

commit v1 on v0

v1 whole, which is shorter than its diff:
```python
import jax
import jax.numpy as jnp
from jax import lax
from jax.sharding import PartitionSpec as P

HEAD_DIM = 128
MASKED = -1e30


def normalize(values):
    return values * lax.rsqrt(jnp.mean(values * values, axis=-1, keepdims=True) + 1e-06)


def modulate_rows(values, scale_part, shift_part):
    return normalize(values) * (1.0 + scale_part) + shift_part


def gelu_exact(values):
    return jax.nn.gelu(values, approximate=False)


def dot(a, b, dims=(((1,), (0,)), ((), ()))):
    return lax.dot_general(a, b, dims, preferred_element_type=jnp.float32)


ROWS_ROWS = (((0,), (0,)), ((), ()))
COLS_COLS = (((1,), (1,)), ((), ()))


def gather_line(own, n, i):
    to_right, to_left = own, own
    lefts, rights = [own], [own]
    for step in range(1, n):
        to_right = lax.ppermute(to_right, "tensor", [(j, j + 1) for j in range(step - 1, n - 1)])
        to_left = lax.ppermute(to_left, "tensor", [(j, j - 1) for j in range(1, n - step + 1)])
        lefts.append(to_right)
        rights.append(to_left)
    return [own] + [jnp.where(i >= s, lefts[s], rights[n - s]) for s in range(1, n)]


def scatter_line(parts, n):
    from_left = from_right = None
    for m in range(n - 1, 0, -1):
        right_part, left_part = parts[n - m], parts[m]
        if from_left is not None:
            right_part = right_part + from_left
            left_part = left_part + from_right
        from_left = lax.ppermute(
            right_part.astype(jnp.bfloat16), "tensor", [(j, j + 1) for j in range(n - m)]
        ).astype(jnp.float32)
        from_right = lax.ppermute(
            left_part.astype(jnp.bfloat16), "tensor", [(j, j - 1) for j in range(m, n)]
        ).astype(jnp.float32)
    return parts[0] + from_left + from_right if from_left is not None else parts[0]


def head_scores(query_part, keys, image_rows, image_of, score_scale):
    scores = (
        jnp.einsum("qhd,khd->hqk", query_part, keys, preferred_element_type=jnp.float32)
        * score_scale
    )
    same_image = image_rows[:, None] == image_of[None, :]
    return jnp.where(same_image[None], scores, MASKED)


def attention_forward(queries, keys, values, image_of, block_rows, score_scale):
    outputs = []
    log_parts = []
    for number in range(queries.shape[0] // block_rows):
        rows = slice(number * block_rows, (number + 1) * block_rows)
        scores = head_scores(queries[rows], keys, image_of[rows], image_of, score_scale)
        highest = jnp.max(scores, axis=-1, keepdims=True)
        powers = jnp.exp(scores - highest)
        totals = jnp.sum(powers, axis=-1, keepdims=True)
        probs = powers / totals
        log_parts.append(highest + jnp.log(totals))
        outputs.append(
            jnp.einsum(
                "hqk,khd->qhd",
                probs.astype(jnp.bfloat16),
                values,
                preferred_element_type=jnp.float32,
            ).astype(jnp.bfloat16)
        )
    return (jnp.concatenate(outputs, axis=0), log_parts)


def attention_backward(
    queries, keys, values, grad_out, image_of, log_parts, block_rows, score_scale
):
    key_grad = jnp.zeros(keys.shape, jnp.float32)
    value_grad = jnp.zeros(values.shape, jnp.float32)
    query_grads = []
    for number in range(queries.shape[0] // block_rows):
        rows = slice(number * block_rows, (number + 1) * block_rows)
        query_part = queries[rows]
        grad_part = grad_out[rows]
        scores = head_scores(query_part, keys, image_of[rows], image_of, score_scale)
        probs = jnp.exp(scores - log_parts[number])
        grad_probs = jnp.einsum(
            "qhd,khd->hqk", grad_part, values, preferred_element_type=jnp.float32
        )
        inner = jnp.sum(probs * grad_probs, axis=-1, keepdims=True)
        grad_scores = (probs * (grad_probs - inner)).astype(jnp.bfloat16)
        query_grads.append(
            (
                jnp.einsum("hqk,khd->qhd", grad_scores, keys, preferred_element_type=jnp.float32)
                * score_scale
            ).astype(jnp.bfloat16)
        )
        key_grad = (
            key_grad
            + jnp.einsum(
                "hqk,qhd->khd", grad_scores, query_part, preferred_element_type=jnp.float32
            )
            * score_scale
        )
        value_grad = value_grad + jnp.einsum(
            "hqk,qhd->khd",
            probs.astype(jnp.bfloat16),
            grad_part,
            preferred_element_type=jnp.float32,
        )
    query_all = jnp.concatenate(query_grads, axis=0)
    stacked = jnp.stack(
        [query_all, key_grad.astype(jnp.bfloat16), value_grad.astype(jnp.bfloat16)], axis=2
    )
    return stacked.reshape(queries.shape[0], -1)


def on_device(
    block_input,
    cotangent,
    noise_embed,
    image_sizes,
    attend_weight,
    merge_weight,
    up_weight,
    down_weight,
    modulate_weight,
):
    n = lax.axis_size("tensor")
    n_dp = lax.axis_size("dp")
    place = lax.axis_index("tensor")
    dp_place = lax.axis_index("dp")
    rows, width = block_input.shape
    tokens = n * rows
    images = image_sizes.shape[1]
    k_rows = modulate_weight.shape[0]

    noise_all = lax.all_gather(noise_embed, "dp", axis=0, tiled=True)
    noise_low_all = jax.nn.silu(noise_all.astype(jnp.float32)).astype(jnp.bfloat16)
    noise_low_cols = lax.dynamic_slice_in_dim(noise_low_all, dp_place * k_rows, k_rows, 1)
    modulation_terms = dot(noise_low_cols, modulate_weight)
    modulation_cols = lax.psum_scatter(modulation_terms, "dp", scatter_dimension=0, tiled=True)
    modulation = lax.all_gather(modulation_cols, "tensor", axis=1, tiled=True)

    attend_full = lax.all_gather(attend_weight, "dp", axis=0, tiled=True)
    merge_full = lax.all_gather(merge_weight, "dp", axis=1, tiled=True)
    up_full = lax.all_gather(up_weight, "dp", axis=0, tiled=True)
    down_full = lax.all_gather(down_weight, "dp", axis=1, tiled=True)

    sizes_row = image_sizes[0]
    ends = [sum(sizes_row[j] for j in range(last + 1)) for last in range(images)]

    def image_at(places):
        return sum((places >= end).astype(jnp.int32) for end in ends)

    blocks = [lax.rem(place - s + n, n) for s in range(n)]
    own_images = image_at(place * rows + jnp.arange(rows, dtype=jnp.int32))
    image_of = jnp.concatenate(
        [image_at(block * rows + jnp.arange(rows, dtype=jnp.int32)) for block in blocks]
    )
    select = [(own_images == j).astype(jnp.float32)[:, None] for j in range(images)]

    def per_slot(number):
        table = modulation[:, number * width : (number + 1) * width]
        return sum(select[j] * table[j : j + 1] for j in range(images))

    shift_first, scale_first, gate_first, shift_second, scale_second, gate_second = [
        per_slot(number) for number in range(6)
    ]
    inputs = block_input.astype(jnp.float32)
    grad_rows = cotangent.astype(jnp.float32)
    hidden_first_f, back_first = jax.vjp(modulate_rows, inputs, scale_first, shift_first)
    hidden_first = gather_line(hidden_first_f.astype(jnp.bfloat16), n, place)
    d_mlp = gather_line((gate_second * grad_rows).astype(jnp.bfloat16), n, place)

    heads_local = attend_full.shape[1] // (3 * HEAD_DIM)
    packed = jnp.concatenate([dot(part, attend_full).astype(jnp.bfloat16) for part in hidden_first])
    packed = packed.reshape(tokens, heads_local, 3, HEAD_DIM)
    queries, keys, values = packed[:, :, 0], packed[:, :, 1], packed[:, :, 2]
    block_rows = min(512, tokens)
    score_scale = HEAD_DIM ** (-0.5)
    attended3, log_parts = attention_forward(
        queries, keys, values, image_of, block_rows, score_scale
    )
    attended = attended3.reshape(tokens, heads_local * HEAD_DIM)

    def slots(array):
        return [array[s * rows : (s + 1) * rows] for s in range(n)]

    attn_out = scatter_line([dot(part, merge_full) for part in slots(attended)], n)
    middle = inputs + gate_first * attn_out
    hidden_second_f, back_second = jax.vjp(modulate_rows, middle, scale_second, shift_second)
    hidden_second = gather_line(hidden_second_f.astype(jnp.bfloat16), n, place)
    activated, mlp_terms, d_pre, d_hidden_terms = [], [], [], []
    for s in range(n):
        pre_act = dot(hidden_second[s], up_full)
        activated_f, gelu_back = jax.vjp(gelu_exact, pre_act)
        activated.append(activated_f.astype(jnp.bfloat16))
        mlp_terms.append(dot(activated[s], down_full))
        d_act = dot(d_mlp[s], down_full, COLS_COLS)
        d_pre.append(gelu_back(d_act)[0].astype(jnp.bfloat16))
        d_hidden_terms.append(dot(d_pre[s], up_full, COLS_COLS))
    d_hidden_second = scatter_line(d_hidden_terms, n)
    mlp_out = scatter_line(mlp_terms, n)
    block_output = (middle + gate_second * mlp_out).astype(jnp.bfloat16)
    d_gate_second = grad_rows * mlp_out
    d_mid_norm, d_scale_second, d_shift_second = back_second(d_hidden_second)
    d_middle = grad_rows + d_mid_norm
    d_gate_first = d_middle * attn_out
    d_attn_parts = gather_line((gate_first * d_middle).astype(jnp.bfloat16), n, place)
    d_attn = jnp.concatenate(d_attn_parts)

    down_local = dot(jnp.concatenate(activated), jnp.concatenate(d_mlp), ROWS_ROWS)
    up_local = dot(jnp.concatenate(hidden_second), jnp.concatenate(d_pre), ROWS_ROWS)
    down_part = lax.psum_scatter(
        down_local.astype(jnp.bfloat16), "dp", scatter_dimension=1, tiled=True
    ).astype(jnp.float32)
    up_part = lax.psum_scatter(
        up_local.astype(jnp.bfloat16), "dp", scatter_dimension=0, tiled=True
    ).astype(jnp.float32)

    merge_local = dot(attended, d_attn, ROWS_ROWS)
    merge_part = lax.psum_scatter(
        merge_local.astype(jnp.bfloat16), "dp", scatter_dimension=1, tiled=True
    ).astype(jnp.float32)
    d_attended = dot(d_attn, merge_full, COLS_COLS).astype(jnp.bfloat16)
    d_qkv = attention_backward(
        queries,
        keys,
        values,
        d_attended.reshape(tokens, heads_local, HEAD_DIM),
        image_of,
        log_parts,
        block_rows,
        score_scale,
    )
    attend_local = dot(jnp.concatenate(hidden_first), d_qkv, ROWS_ROWS)
    attend_part = lax.psum_scatter(
        attend_local.astype(jnp.bfloat16), "dp", scatter_dimension=0, tiled=True
    ).astype(jnp.float32)
    d_hidden_first = scatter_line([dot(part, attend_full, COLS_COLS) for part in slots(d_qkv)], n)
    d_in_norm, d_scale_first, d_shift_first = back_first(d_hidden_first)
    input_grad = (d_middle + d_in_norm).astype(jnp.bfloat16)

    token_grads = [
        d_shift_first,
        d_scale_first,
        d_gate_first,
        d_shift_second,
        d_scale_second,
        d_gate_second,
    ]
    image_rows = [
        jnp.concatenate(
            [jnp.sum(part * select[j], axis=0, keepdims=True) for part in token_grads], axis=1
        )
        for j in range(images)
    ]
    d_mod_terms = jnp.concatenate(image_rows, axis=0)
    d_mod_cols = lax.psum_scatter(
        d_mod_terms, "tensor", scatter_dimension=1, tiled=True
    ).astype(jnp.bfloat16)
    d_mod_all = lax.all_gather(d_mod_cols, "dp", axis=0, tiled=True)
    modulate_part = dot(noise_low_cols, d_mod_all, ROWS_ROWS)
    noise_terms = dot(d_mod_all, modulate_weight, COLS_COLS)
    noise_cols = lax.psum(noise_terms, "tensor")
    noise_sum = lax.all_to_all(noise_cols, "dp", split_axis=0, concat_axis=1, tiled=True)
    silu_back = jax.vjp(jax.nn.silu, noise_embed.astype(jnp.float32))[1]
    noise_grad = silu_back(noise_sum)[0]
    return (
        block_output,
        input_grad,
        noise_grad,
        attend_part,
        merge_part,
        up_part,
        down_part,
        modulate_part,
    )


def solution(mesh):
    whole_rows = P(("dp", "tensor"), None)
    by_dp = P("dp", None)
    tall = P("dp", "tensor")
    wide = P("tensor", "dp")
    return jax.shard_map(
        on_device,
        mesh=mesh,
        in_specs=(whole_rows, whole_rows, by_dp, by_dp, tall, wide, tall, wide, tall),
        out_specs=(whole_rows, whole_rows, by_dp, tall, wide, tall, wide, tall),
        check_vma=False,
    )
```

time: 1660 us -> 1100 us (0.66)
  waiting for transfers between devices: 1230 us -> 558 us
  starting transfers between devices: 0.6 us -> 151 us
  matrix products: 278 us -> 202 us
  blocking collectives: 32.5 us -> 53 us
    psum x3 -> x0, waiting for transfers between devices: 661 us -> none  [the longest x1 277 us: on_device(): lax.psum(jnp.dot(attended, merge_full, preferred_element_type=jnp.float32...]
    ppermute x0 -> x48, waiting for transfers between devices: none -> 365 us  [the longest x12 158 us: gather_line(): lax.ppermute(to_left, 'tensor', [(j, j - 1) for j in range(1, n - step +...]
    all_gather x7 -> x4, waiting for transfers between devices: 308 us -> 0.03 us  [the longest x1 0.02 us: on_device(): up_full = lax.all_gather(up_weight, 'dp', axis=0, tiled=True)]
    unnamed x15 -> x12, waiting for transfers between devices: 4.63 us -> 155 us
    ppermute x0 -> x48, starting transfers between devices: none -> 147 us  [the longest x12 74 us: scatter_line(): lax.ppermute(right_part.astype(jnp.bfloat16), 'tensor', [(j, j + 1) for j...]
    reduce_scatter x1 -> x0, waiting for transfers between devices: 93.7 us -> none  [on_device(): lax.psum_scatter(modulate_local.astype(jnp.bfloat16), 'dp', scatter_dimen...]
    dot_general x29 -> x38, matrix products: 252 us -> 178 us  [the longest x36 173 us: dot(): return lax.dot_general(a, b, dims, preferred_element_type=jnp.float32)]
    reduce_scatter x1, waiting for transfers between devices: 72.4 us -> 8.28 us  [on_device(): lax.psum_scatter(down_local.astype(jnp.bfloat16), 'dp', scatter_dimension...]
  transfers between devices with their start and end apart: 15 -> 59, of which waited for: 15 -> 32; matrix products, arithmetic and copies ran while one was open for 15% -> 26% of each run, Pallas kernels for 0% -> 0%
where the time goes in v1:
time: 1100 us; the launch traced here: 1090 us
  waiting for transfers between devices  558 us (51%)
  matrix products  202 us (18%)
  starting transfers between devices  151 us (14%)
  other arithmetic  80.3 us (7%)
  blocking collectives  53 us (5%)
  local copies, waits for them, and re-layouts  29 us (3%)
  between operations  20.4 us (2%)
    dot_general x36, matrix products, dot(): return lax.dot_general(a, b, dims, preferred_element_type=jnp.float32)  173 us
    ppermute x12, waiting for transfers between devices, gather_line(): lax.ppermute(to_left, 'tensor', [(j, j - 1) for j in range(1, n - step +...  158 us
    unnamed x12, waiting for transfers between devices  155 us
    ppermute x12, waiting for transfers between devices, scatter_line(): lax.ppermute(right_part.astype(jnp.bfloat16), 'tensor', [(j, j + 1) for j...  90.3 us
    ppermute x12, waiting for transfers between devices, scatter_line(): lax.ppermute(left_part.astype(jnp.bfloat16), 'tensor', [(j, j - 1) for j...  89.2 us
    ppermute x12, starting transfers between devices, scatter_line(): lax.ppermute(right_part.astype(jnp.bfloat16), 'tensor', [(j, j + 1) for j...  74 us
    ppermute x12, starting transfers between devices, gather_line(): lax.ppermute(to_right, 'tensor', [(j, j + 1) for j in range(step - 1, n -...  45.4 us
    ppermute x12, waiting for transfers between devices, gather_line(): lax.ppermute(to_right, 'tensor', [(j, j + 1) for j in range(step - 1, n -...  27.5 us
  transfers between devices with their start and end apart: 59, of which 32 were waited for; matrix products, arithmetic and copies ran while one was open for 26% of the time, Pallas kernels for 0%

profile of v1, /device:TPU:0, one launch (start us, length us, event | category | flops | bytes accessed | tf_op | source)
XLA Modules:
  0.0 1093.9 jit_solution(11330077114006807228)
XLA Ops:
  27.1 47.0 %all-reduce.3.cloned.1.call-done = f32[32,3072]{1,0:T(8,128)} async-done(((f32[32,3072]{1,0:T(8,128)}), f32[32,3072]{1,0:T(8,128)}) %all-reduce.3.cloned.1.call-update) | async-done | bytes 393232
  74.9 13.7 %all_gather.22 = f32[4,12288]{1,0:T(4,128)S(1)} all-gather(f32[4,3072]{1,0:T(4,128)S(1)} %constant_dynamic-slice_fusion), channel_id=1, replica_groups=mesh['dp'=8,'tensor'=4] {'tensor'}, dimensions={1}, use_global_device_ids=true | all-gather | bytes 245760 | tf_op jit(solution)/shard_map/all_gather | solution.py:156
  100.8 16.5 %collective-permute-done = bf16[256,2048]{1,0:T(8,128)(2,1)} collective-permute-done((bf16[256,2048]{1,0:T(8,128)(2,1)S(1)}, bf16[256,2048]{1,0:T(8,128)(2,1)}, u32[]{:S(2)}, u32[]{:S(2)}) %collective-permute-start) | collective-permute-done | bytes 1048608 | tf_op jit(solution)/shard_map/ppermute | solution.py:34
  128.4 17.6 %collective-permute-done.2 = bf16[256,2048]{1,0:T(8,128)(2,1)} collective-permute-done((bf16[256,2048]{1,0:T(8,128)(2,1)}, bf16[256,2048]{1,0:T(8,128)(2,1)}, u32[]{:S(2)}, u32[]{:S(2)}) %collective-permute-start.2) | collective-permute-done | bytes 1048608 | tf_op jit(solution)/shard_map/ppermute | solution.py:35
  152.0 15.3 %collective-permute-done.3 = bf16[256,2048]{1,0:T(8,128)(2,1)S(1)} collective-permute-done((bf16[256,2048]{1,0:T(8,128)(2,1)}, bf16[256,2048]{1,0:T(8,128)(2,1)S(1)}, u32[]{:S(2)}, u32[]{:S(2)}) %collective-permute-start.3) | collective-permute-done | bytes 1048608 | tf_op jit(solution)/shard_map/ppermute | solution.py:35
  227.3 15.3 %collective-permute-done.7 = bf16[256,2048]{1,0:T(8,128)(2,1)S(1)} collective-permute-done((bf16[256,2048]{1,0:T(8,128)(2,1)S(1)}, bf16[256,2048]{1,0:T(8,128)(2,1)S(1)}, u32[]{:S(2)}, u32[]{:S(2)}) %collective-permute-start.7) | collective-permute-done | bytes 1048608 | tf_op jit(solution)/shard_map/ppermute | solution.py:48
  251.5 12.7 %collective-permute-done.8 = bf16[256,2048]{1,0:T(8,128)(2,1)S(1)} collective-permute-done((bf16[256,2048]{1,0:T(8,128)(2,1)S(1)}, bf16[256,2048]{1,0:T(8,128)(2,1)S(1)}, u32[]{:S(2)}, u32[]{:S(2)}) %collective-permute-start.8) | collective-permute-done | bytes 1048608 | tf_op jit(solution)/shard_map/ppermute | solution.py:48
  264.2 38.2 %collective-permute-done.11 = bf16[256,2048]{1,0:T(8,128)(2,1)S(1)} collective-permute-done((bf16[256,2048]{1,0:T(8,128)(2,1)S(1)}, bf16[256,2048]{1,0:T(8,128)(2,1)S(1)}, u32[]{:S(2)}, u32[]{:S(2)}) %collective-permute-start.11) | collective-permute-done | bytes 1048608 | tf_op jit(solution)/shard_map/ppermute | solution.py:51
  341.3 21.2 %collective-permute-done.27 = bf16[256,2048]{1,0:T(8,128)(2,1)} collective-permute-done((bf16[256,2048]{1,0:T(8,128)(2,1)S(1)}, bf16[256,2048]{1,0:T(8,128)(2,1)}, u32[]{:S(2)}, u32[]{:S(2)}) %collective-permute-start.27) | collective-permute-done | bytes 1048608 | tf_op jit(solution)/shard_map/ppermute | solution.py:35
  386.3 21.2 %collective-permute-done.28 = bf16[256,2048]{1,0:T(8,128)(2,1)} collective-permute-done((bf16[256,2048]{1,0:T(8,128)(2,1)}, bf16[256,2048]{1,0:T(8,128)(2,1)}, u32[]{:S(2)}, u32[]{:S(2)}) %collective-permute-start.28) | collective-permute-done | bytes 1048608 | tf_op jit(solution)/shard_map/ppermute | solution.py:35
  483.7 11.4 %collective-permute-done.30 = bf16[256,2048]{1,0:T(8,128)(2,1)S(1)} collective-permute-done((bf16[256,2048]{1,0:T(8,128)(2,1)S(1)}, bf16[256,2048]{1,0:T(8,128)(2,1)S(1)}, u32[]{:S(2)}, u32[]{:S(2)}) %collective-permute-start.30) | collective-permute-done | bytes 1048608 | tf_op jit(solution)/shard_map/ppermute | solution.py:48
  523.8 12.9 %collective-permute-done.19 = bf16[256,2048]{1,0:T(8,128)(2,1)S(1)} collective-permute-done((bf16[256,2048]{1,0:T(8,128)(2,1)S(1)}, bf16[256,2048]{1,0:T(8,128)(2,1)S(1)}, u32[]{:S(2)}, u32[]{:S(2)}) %collective-permute-start.19) | collective-permute-done | bytes 1048608 | tf_op jit(solution)/shard_map/ppermute | solution.py:48
  549.1 29.7 %collective-permute-start.32 = (bf16[256,2048]{1,0:T(8,128)(2,1)S(1)}, bf16[256,2048]{1,0:T(8,128)(2,1)S(1)}, u32[]{:S(2)}, u32[]{:S(2)}) collective-permute-start(bf16[256,2048]{1,0:T(8,128)(2,1)S(1)} %get-tuple-element.81), channel_id=1, source_target_pairs={{0,1},{1,2},{2,3},{4,5},{5,6},{6,7},{8,9},{9,10},{10,11},{12,13},{... | collective-permute-start | bytes 3145736 | tf_op jit(solution)/shard_map/ppermute | solution.py:48
  597.9 13.5 %collective-permute-done.23 = bf16[256,2048]{1,0:T(8,128)(2,1)S(1)} collective-permute-done((bf16[256,2048]{1,0:T(8,128)(2,1)S(1)}, bf16[256,2048]{1,0:T(8,128)(2,1)S(1)}, u32[]{:S(2)}, u32[]{:S(2)}) %collective-permute-start.23) | collective-permute-done | bytes 1048608 | tf_op jit(solution)/shard_map/ppermute | solution.py:51
  619.2 21.0 %collective-permute-start.36 = (bf16[256,2048]{1,0:T(8,128)(2,1)S(1)}, bf16[256,2048]{1,0:T(8,128)(2,1)S(1)}, u32[]{:S(2)}, u32[]{:S(2)}) collective-permute-start(bf16[256,2048]{1,0:T(8,128)(2,1)S(1)} %get-tuple-element.52), channel_id=1, source_target_pairs={{0,1},{1,2},{2,3},{4,5},{5,6},{6,7},{8,9},{9,10},{10,11},{12,13},{... | collective-permute-start | bytes 3145736 | tf_op jit(solution)/shard_map/ppermute | solution.py:34
  653.2 20.8 %collective-permute-done.37 = bf16[256,2048]{1,0:T(8,128)(2,1)S(1)} collective-permute-done((bf16[256,2048]{1,0:T(8,128)(2,1)S(1)}, bf16[256,2048]{1,0:T(8,128)(2,1)S(1)}, u32[]{:S(2)}, u32[]{:S(2)}) %collective-permute-start.37) | collective-permute-done | bytes 1048608 | tf_op jit(solution)/shard_map/ppermute | solution.py:35
  676.2 18.4 %collective-permute-done.38 = bf16[256,2048]{1,0:T(8,128)(2,1)S(1)} collective-permute-done((bf16[256,2048]{1,0:T(8,128)(2,1)S(1)}, bf16[256,2048]{1,0:T(8,128)(2,1)S(1)}, u32[]{:S(2)}, u32[]{:S(2)}) %collective-permute-start.38) | collective-permute-done | bytes 1048608 | tf_op jit(solution)/shard_map/ppermute | solution.py:35
  696.2 15.1 %collective-permute-done.39 = bf16[256,2048]{1,0:T(8,128)(2,1)S(1)} collective-permute-done((bf16[256,2048]{1,0:T(8,128)(2,1)S(1)}, bf16[256,2048]{1,0:T(8,128)(2,1)S(1)}, u32[]{:S(2)}, u32[]{:S(2)}) %collective-permute-start.39) | collective-permute-done | bytes 1048608 | tf_op jit(solution)/shard_map/ppermute | solution.py:35
  716.2 14.1 %convolution_convert_fusion.1 = bf16[2048,2048]{1,0:T(8,128)(2,1)} fusion(bf16[256,2048]{1,0:T(8,128)(2,1)} %copy-done.50, bf16[256,2048]{1,0:T(8,128)(2,1)} %copy-done.48, bf16[256,2048]{1,0:T(8,128)(2,1)} %copy-done.49, bf16[256,2048]{1,0:T(8,128)(2,1)} %get-tuple-element.117, bf16[256,2048]{1,0:T(8,128)(2,1)} %get-tuple-element.58, ...), kind=kOutput, calls=%fused_computation.13 | convolution fusion | flops 8627683328 | bytes 16777216 | tf_op jit(solution)/shard_map/dot_general | solution.py:23
  775.4 13.0 %collective-permute-done.42 = bf16[256,2048]{1,0:T(8,128)(2,1)S(1)} collective-permute-done((bf16[256,2048]{1,0:T(8,128)(2,1)S(1)}, bf16[256,2048]{1,0:T(8,128)(2,1)S(1)}, u32[]{:S(2)}, u32[]{:S(2)}) %collective-permute-start.42) | collective-permute-done | bytes 1048608 | tf_op jit(solution)/shard_map/ppermute | solution.py:48
  837.1 32.7 %collective-permute-done.47 = bf16[256,2048]{1,0:T(8,128)(2,1)S(1)} collective-permute-done((bf16[256,2048]{1,0:T(8,128)(2,1)S(1)}, bf16[256,2048]{1,0:T(8,128)(2,1)S(1)}, u32[]{:S(2)}, u32[]{:S(2)}) %collective-permute-start.47) | collective-permute-done | bytes 1048608 | tf_op jit(solution)/shard_map/ppermute | solution.py:51
  911.7 106.5 %reduce-scatter.16.cloned.1.call-done = f32[3072,4]{1,0:T(8,128)} async-done(((f32[12288,4]{1,0:T(8,128)}), f32[3072,4]{1,0:T(8,128)}) %reduce-scatter.16.cloned.1.call-update) | async-done | bytes 49168
  1029.9 19.1 %psum.7 = f32[8,4,256]{2,1,0:T(4,128)} all-reduce(f32[8,4,256]{2,1,0:T(4,128)S(1)} %all_to_all.14), channel_id=1, replica_groups=mesh['dp'=8,'tensor'=4] {'tensor'}, use_global_device_ids=true, to_apply=%region_36.37 | all-reduce | flops 8192 | bytes 65536 | tf_op jit(solution)/shard_map/psum | solution.py:279
  1058.1 26.3 %reduce-scatter.8.cloned.1.call-done = bf16[256,1536]{1,0:T(8,128)(2,1)} async-done(((bf16[2048,1536]{1,0:T(8,128)(2,1)}), bf16[256,1536]{1,0:T(8,128)(2,1)}) %reduce-scatter.8.cloned.1.call-update) | async-done | bytes 786448 | tf_op jit(solution)/shard_map/reduce_scatter | solution.py:251
  (539 shorter events, 500.3 us)
Async XLA Ops:
  7.2 66.8 %all-reduce.3.cloned.1.call-start = ((), (), s32[]{:S(2)}) async-start(), calls=%async_computation.15 | async-start | bytes 786432
  19.4 149.0 %all-gather.7.cloned.1.call-start = ((), (), s32[]{:S(2)}) async-start(), calls=%async_computation.6 | async-start | bytes 7077888 | tf_op jit(solution)/shard_map/all_gather | solution.py:158
  20.2 177.8 %all-gather.9.cloned.1.call-start = ((), (), s32[]{:S(2)}) async-start(), calls=%async_computation.7 | async-start | bytes 2359296 | tf_op jit(solution)/shard_map/all_gather | solution.py:159
  20.9 303.7 %all-gather.11.cloned.1.call-start = ((), (), s32[]{:S(2)}) async-start(), calls=%async_computation.8 | async-start | bytes 9437184 | tf_op jit(solution)/shard_map/all_gather | solution.py:160
  21.5 345.7 %all-gather.13.cloned.1.call-start = ((), (), s32[]{:S(2)}) async-start(), calls=%async_computation.9 | async-start | bytes 9437184 | tf_op jit(solution)/shard_map/all_gather | solution.py:161
  123.9 768.2 %reduce-scatter.10.cloned.1.call-start = ((), (), s32[]{:S(2)}) async-start(), calls=%async_computation.11 | async-start | bytes 2359296 | tf_op jit(solution)/shard_map/reduce_scatter | solution.py:236
  250.2 52.3 %collective-permute-start.11 = (bf16[256,2048]{1,0:T(8,128)(2,1)S(1)}, bf16[256,2048]{1,0:T(8,128)(2,1)S(1)}, u32[]{:S(2)}, u32[]{:S(2)}) collective-permute-start(bf16[256,2048]{1,0:T(8,128)(2,1)S(1)} %add_convert_fusion.19), channel_id=1, source_target_pairs={{1,0},{2,1},{3,2},{5,4},{6,5},{7,6},{9,8},{10,9},{11,10},{13,12},{... | collective-permute-start | bytes 3145736 | tf_op jit(solution)/shard_map/ppermute | solution.py:51
  312.7 49.8 %collective-permute-start.27 = (bf16[256,2048]{1,0:T(8,128)(2,1)S(1)}, bf16[256,2048]{1,0:T(8,128)(2,1)}, u32[]{:S(2)}, u32[]{:S(2)}) collective-permute-start(bf16[256,2048]{1,0:T(8,128)(2,1)S(1)} %get-tuple-element.118), channel_id=1, source_target_pairs={{1,0},{2,1},{3,2},{5,4},{6,5},{7,6},{9,8},{10,9},{11,10},{13,12},{... | collective-permute-start | bytes 3145736 | tf_op jit(solution)/shard_map/ppermute | solution.py:35
  314.0 49.8 %collective-permute-start.12 = (bf16[256,2048]{1,0:T(8,128)(2,1)}, bf16[256,2048]{1,0:T(8,128)(2,1)}, u32[]{:S(2)}, u32[]{:S(2)}) collective-permute-start(bf16[256,2048]{1,0:T(8,128)(2,1)} %get-tuple-element.117), channel_id=1, source_target_pairs={{0,1},{1,2},{2,3},{4,5},{5,6},{6,7},{8,9},{9,10},{10,11},{12,13},{... | collective-permute-start | bytes 3145736 | tf_op jit(solution)/shard_map/ppermute | solution.py:34
  320.5 44.9 %collective-permute-start.24 = (bf16[256,2048]{1,0:T(8,128)(2,1)S(1)}, bf16[256,2048]{1,0:T(8,128)(2,1)}, u32[]{:S(2)}, u32[]{:S(2)}) collective-permute-start(bf16[256,2048]{1,0:T(8,128)(2,1)S(1)} %get-tuple-element.118), channel_id=1, source_target_pairs={{0,1},{1,2},{2,3},{4,5},{5,6},{6,7},{8,9},{9,10},{10,11},{12,13},{... | collective-permute-start | bytes 3145736 | tf_op jit(solution)/shard_map/ppermute | solution.py:34
  340.0 44.9 %collective-permute-start.16 = (bf16[256,2048]{1,0:T(8,128)(2,1)}, bf16[256,2048]{1,0:T(8,128)(2,1)}, u32[]{:S(2)}, u32[]{:S(2)}) collective-permute-start(bf16[256,2048]{1,0:T(8,128)(2,1)} %collective-permute-done.15), channel_id=1, source_target_pairs={{1,0},{2,1},{5,4},{6,5},{9,8},{10,9},{13,12},{14,13},{17,16},{18,1... | collective-permute-start | bytes 3145736 | tf_op jit(solution)/shard_map/ppermute | solution.py:35
  362.5 44.9 %collective-permute-start.28 = (bf16[256,2048]{1,0:T(8,128)(2,1)}, bf16[256,2048]{1,0:T(8,128)(2,1)}, u32[]{:S(2)}, u32[]{:S(2)}) collective-permute-start(bf16[256,2048]{1,0:T(8,128)(2,1)} %collective-permute-done.27), channel_id=1, source_target_pairs={{1,0},{2,1},{5,4},{6,5},{9,8},{10,9},{13,12},{14,13},{17,16},{18,1... | collective-permute-start | bytes 3145736 | tf_op jit(solution)/shard_map/ppermute | solution.py:35
  363.8 44.9 %collective-permute-start.13 = (bf16[256,2048]{1,0:T(8,128)(2,1)}, bf16[256,2048]{1,0:T(8,128)(2,1)}, u32[]{:S(2)}, u32[]{:S(2)}) collective-permute-start(bf16[256,2048]{1,0:T(8,128)(2,1)} %collective-permute-done.12), channel_id=1, source_target_pairs={{1,2},{2,3},{5,6},{6,7},{9,10},{10,11},{13,14},{14,15},{17,18},{18... | collective-permute-start | bytes 3145736 | tf_op jit(solution)/shard_map/ppermute | solution.py:34
  365.5 45.4 %collective-permute-start.25 = (bf16[256,2048]{1,0:T(8,128)(2,1)}, bf16[256,2048]{1,0:T(8,128)(2,1)}, u32[]{:S(2)}, u32[]{:S(2)}) collective-permute-start(bf16[256,2048]{1,0:T(8,128)(2,1)} %collective-permute-done.24), channel_id=1, source_target_pairs={{1,2},{2,3},{5,6},{6,7},{9,10},{10,11},{13,14},{14,15},{17,18},{18... | collective-permute-start | bytes 3145736 | tf_op jit(solution)/shard_map/ppermute | solution.py:34
  385.0 42.4 %collective-permute-start.17 = (bf16[256,2048]{1,0:T(8,128)(2,1)}, bf16[256,2048]{1,0:T(8,128)(2,1)S(1)}, u32[]{:S(2)}, u32[]{:S(2)}) collective-permute-start(bf16[256,2048]{1,0:T(8,128)(2,1)} %collective-permute-done.16), channel_id=1, source_target_pairs={{1,0},{5,4},{9,8},{13,12},{17,16},{21,20},{25,24},{29,28}} | collective-permute-start | bytes 3145736 | tf_op jit(solution)/shard_map/ppermute | solution.py:35
  408.7 52.9 %collective-permute-start.14 = (bf16[256,2048]{1,0:T(8,128)(2,1)}, bf16[256,2048]{1,0:T(8,128)(2,1)S(1)}, u32[]{:S(2)}, u32[]{:S(2)}) collective-permute-start(bf16[256,2048]{1,0:T(8,128)(2,1)} %collective-permute-done.13), channel_id=1, source_target_pairs={{2,3},{6,7},{10,11},{14,15},{18,19},{22,23},{26,27},{30,31}} | collective-permute-start | bytes 3145736 | tf_op jit(solution)/shard_map/ppermute | solution.py:34
  412.6 52.8 %collective-permute-start.26 = (bf16[256,2048]{1,0:T(8,128)(2,1)}, bf16[256,2048]{1,0:T(8,128)(2,1)S(1)}, u32[]{:S(2)}, u32[]{:S(2)}) collective-permute-start(bf16[256,2048]{1,0:T(8,128)(2,1)} %collective-permute-done.25), channel_id=1, source_target_pairs={{2,3},{6,7},{10,11},{14,15},{18,19},{22,23},{26,27},{30,31}} | collective-permute-start | bytes 3145736 | tf_op jit(solution)/shard_map/ppermute | solution.py:34
  454.6 48.6 %collective-permute-start.18 = (bf16[256,2048]{1,0:T(8,128)(2,1)S(1)}, bf16[256,2048]{1,0:T(8,128)(2,1)S(1)}, u32[]{:S(2)}, u32[]{:S(2)}) collective-permute-start(bf16[256,2048]{1,0:T(8,128)(2,1)S(1)} %get-tuple-element.137), channel_id=1, source_target_pairs={{0,1},{4,5},{8,9},{12,13},{16,17},{20,21},{24,25},{28,29}} | collective-permute-start | bytes 3145736 | tf_op jit(solution)/shard_map/ppermute | solution.py:48
  543.2 54.7 %collective-permute-start.20 = (bf16[256,2048]{1,0:T(8,128)(2,1)S(1)}, bf16[256,2048]{1,0:T(8,128)(2,1)S(1)}, u32[]{:S(2)}, u32[]{:S(2)}) collective-permute-start(bf16[256,2048]{1,0:T(8,128)(2,1)S(1)} %get-tuple-element.83), channel_id=1, source_target_pairs={{0,1},{1,2},{2,3},{4,5},{5,6},{6,7},{8,9},{9,10},{10,11},{12,13},{... | collective-permute-start | bytes 3145736 | tf_op jit(solution)/shard_map/ppermute | solution.py:48
  715.9 177.9 %reduce-scatter.12.cloned.1.call-start = ((), (), s32[]{:S(2)}) async-start(), calls=%async_computation.12 | async-start | bytes 9437184 | tf_op jit(solution)/shard_map/reduce_scatter | solution.py:231
  730.4 174.6 %reduce-scatter.14.cloned.1.call-start = ((), (), s32[]{:S(2)}) async-start(), calls=%async_computation.13 | async-start | bytes 9437184 | tf_op jit(solution)/shard_map/reduce_scatter | solution.py:228
  808.7 209.4 %reduce-scatter.16.cloned.1.call-start = ((), (), s32[]{:S(2)}) async-start(), calls=%async_computation.14 | async-start | bytes 7864320
  825.2 44.6 %collective-permute-start.47 = (bf16[256,2048]{1,0:T(8,128)(2,1)S(1)}, bf16[256,2048]{1,0:T(8,128)(2,1)S(1)}, u32[]{:S(2)}, u32[]{:S(2)}) collective-permute-start(bf16[256,2048]{1,0:T(8,128)(2,1)S(1)} %add_convert_fusion), channel_id=1, source_target_pairs={{1,0},{2,1},{3,2},{5,4},{6,5},{7,6},{9,8},{10,9},{11,10},{13,12},{... | collective-permute-start | bytes 3145736 | tf_op jit(solution)/shard_map/ppermute | solution.py:51
  880.8 203.7 %reduce-scatter.8.cloned.1.call-start = ((), (), s32[]{:S(2)}) async-start(), calls=%async_computation.10 | async-start | bytes 7077888 | tf_op jit(solution)/shard_map/reduce_scatter | solution.py:251
  (170 other events, 6531.1 us)
Sparse Core Ops, SparseCore 0:
  19.6 54.4 all-reduce.2
  75.9 44.8 all-gather.6
  122.7 28.1 all-gather.8
  152.6 54.3 all-gather.10
  208.8 55.9 all-gather.12
  716.1 38.9 reduce-scatter.9
  758.9 71.2 reduce-scatter.11
  833.7 71.2 reduce-scatter.13
  907.4 110.7 reduce-scatter.15
  1021.8 62.6 reduce-scatter.7

commit v2 on v1

v2 whole, which is shorter than its diff:
```python
import functools
import math

import jax
import jax.numpy as jnp
from jax import lax
from jax.experimental import pallas as pl
from jax.experimental.pallas import tpu as pltpu
from jax.sharding import PartitionSpec as P

HEAD_DIM = 128
MASKED = -1e30


def normalize(values):
    return values * lax.rsqrt(jnp.mean(values * values, axis=-1, keepdims=True) + 1e-06)


def modulate_rows(values, scale_part, shift_part):
    return normalize(values) * (1.0 + scale_part) + shift_part


def gelu_exact(values):
    return jax.nn.gelu(values, approximate=False)


def dot(a, b, dims=(((1,), (0,)), ((), ()))):
    return lax.dot_general(a, b, dims, preferred_element_type=jnp.float32)


ROWS_ROWS = (((0,), (0,)), ((), ()))
COLS_COLS = (((1,), (1,)), ((), ()))


MESH = pl.DeviceIdType.MESH
HBM = pl.BlockSpec(memory_space=pl.ANY)
VMEM = pl.BlockSpec(memory_space=pltpu.VMEM)
DMA = pltpu.SemaphoreType.DMA


def rows_of(j, rows):
    return pl.ds(pl.multiple_of(j * rows, rows), rows)


def beside(step):
    return (lax.axis_index("dp"), lax.axis_index("tensor") + step)


def greet_line(n, i):
    barrier = pltpu.get_barrier_semaphore()

    @pl.when(i > 0)
    def _():
        pl.semaphore_signal(barrier, inc=1, device_id=beside(-1), device_id_type=MESH)

    @pl.when(i < n - 1)
    def _():
        pl.semaphore_signal(barrier, inc=1, device_id=beside(1), device_id_type=MESH)

    pl.semaphore_wait(barrier, jnp.where(i > 0, 1, 0) + jnp.where(i < n - 1, 1, 0))


class LineGather:
    def __init__(self, n, i, rows, own, full, to_left, to_right, arrived):
        self.n, self.i, self.rows, self.own, self.full = n, i, rows, own, full
        self.to_left, self.to_right, self.arrived = to_left, to_right, arrived

    def copy(self, j, step, source=None):
        place = self.full.at[rows_of(j, self.rows)]
        return pltpu.make_async_remote_copy(
            src_ref=place if source is None else source,
            dst_ref=place,
            send_sem=(self.to_right if step > 0 else self.to_left).at[j],
            recv_sem=self.arrived.at[j],
            device_id=beside(step),
            device_id_type=MESH,
        )

    def start(self):
        @pl.when(self.i > 0)
        def _():
            self.copy(self.i, -1, self.own).start()

        @pl.when(self.i < self.n - 1)
        def _():
            self.copy(self.i, 1, self.own).start()

    def step(self, s):
        for side in (-1, 1):
            j = self.i + side * s
            there = (j >= 0) & (j < self.n)
            more = (self.i > 0) if side > 0 else (self.i < self.n - 1)

            @pl.when(there)
            def _():
                self.copy(j, side).wait_recv()

            @pl.when(there & more)
            def _():
                self.copy(j, -side).start()

    def finish(self):
        @pl.when(self.i > 0)
        def _():
            self.copy(self.i, -1, self.own).wait_send()

        @pl.when(self.i < self.n - 1)
        def _():
            self.copy(self.i, 1, self.own).wait_send()

        for j in range(self.n):

            @pl.when((j < self.i) & (self.i < self.n - 1))
            def _():
                self.copy(j, 1).wait_send()

            @pl.when((j > self.i) & (self.i > 0))
            def _():
                self.copy(j, -1).wait_send()


class LineScatter:
    def __init__(self, n, i, rows, width, part, got, sent, arrived):
        self.n, self.i, self.rows, self.width = n, i, rows, width
        self.part, self.got, self.sent, self.arrived = part, got, sent, arrived
        self.pieces = part.shape[1] // width

    def columns(self, c):
        return pl.ds(pl.multiple_of(c * self.width, self.width), self.width)

    def copy(self, j, slot, c, step):
        return pltpu.make_async_remote_copy(
            src_ref=self.part.at[rows_of(j, self.rows), self.columns(c)],
            dst_ref=self.got.at[rows_of(slot, self.rows), self.columns(c)],
            send_sem=self.sent.at[j, c],
            recv_sem=self.arrived.at[slot, c],
            device_id=beside(step),
            device_id_type=MESH,
        )

    def slot_there(self, j, step):
        if step > 0:
            return j
        return jnp.where(j == self.i - 1, self.n, j)

    def at_end(self, j, c):
        @pl.when((self.i == 0) & (j > 0))
        def _():
            self.copy(j, j, c, 1).start()

        @pl.when((self.i == self.n - 1) & (j < self.i))
        def _():
            self.copy(j, self.slot_there(j, -1), c, -1).start()

    def pass_on(self, t, c, near):
        n, i = self.n, self.i
        rightward = (2 * i < n - 1) if near else (2 * i >= n - 1)
        j = jnp.where(rightward, t, n - 1 - t)
        step = jnp.where(rightward, 1, -1)
        right = rightward & (i > 0) & (j > i)
        left = jnp.logical_not(rightward) & (i < n - 1) & (j < i)

        @pl.when(right | left)
        def _():
            self.add(j, j, c)
            slot = jnp.where(left & (j == i - 1), n, j)
            self.copy(j, slot, c, step).start()

    def add(self, j, slot, c):
        self.copy(j, slot, c, 1).wait_recv()
        here = (rows_of(j, self.rows), self.columns(c))
        there = (rows_of(slot, self.rows), self.columns(c))
        total = self.part[here].astype(jnp.float32) + self.got[there].astype(jnp.float32)
        self.part[here] = total.astype(self.part.dtype)

    def own(self, c, out):
        i, n = self.i, self.n
        columns = self.columns(c)
        out[:, columns] = self.part[rows_of(i, self.rows), columns].astype(out.dtype)

        @pl.when(i > 0)
        def _():
            self.copy(i, i, c, 1).wait_recv()
            out[:, columns] += self.got[rows_of(i, self.rows), columns].astype(out.dtype)

        @pl.when(i < n - 1)
        def _():
            self.copy(i, n, c, -1).wait_recv()
            out[:, columns] += self.got[rows_of(n, self.rows), columns].astype(out.dtype)

    def all_sent(self):
        def one(j, carry):
            @pl.when(j != self.i)
            def _():
                for c in range(self.pieces):
                    self.copy(j, 0, c, 1).wait_send()

            return carry

        lax.fori_loop(0, self.n, one, 0)


def mm(a, b):
    return lax.dot_general(a, b, (((1,), (0,)), ((), ())), preferred_element_type=jnp.float32)


def mm_nt(a, b):
    return lax.dot_general(a, b, (((1,), (1,)), ((), ())), preferred_element_type=jnp.float32)


def mm_tn(a, b):
    return lax.dot_general(a, b, (((0,), (0,)), ((), ())), preferred_element_type=jnp.float32)


def call(kernel, collective_id, name, in_specs, outs, out_specs, scratch, flops=0, limit=60):
    return pl.pallas_call(
        kernel,
        out_shape=outs,
        in_specs=in_specs,
        out_specs=out_specs,
        scratch_shapes=scratch,
        compiler_params=pltpu.CompilerParams(
            collective_id=collective_id,
            has_side_effects=True,
            vmem_limit_bytes=limit * 1024 * 1024,
        ),
        cost_estimate=pl.CostEstimate(flops=flops, bytes_accessed=1 << 20, transcendentals=0),
        name=name,
    )


def gather_kernel(n, rows, count, *refs):
    own, full = refs[:count], refs[count : 2 * count]
    to_left, to_right, arrived, local = refs[2 * count :]
    i = lax.axis_index("tensor")
    copies = [
        pltpu.make_async_copy(own[a], full[a].at[rows_of(i, rows)], local.at[a])
        for a in range(count)
    ]
    for copy in copies:
        copy.start()
    greet_line(n, i)
    lines = [
        LineGather(n, i, rows, own[a], full[a], to_left.at[a], to_right.at[a], arrived.at[a])
        for a in range(count)
    ]
    for line in lines:
        line.start()
        for s in range(1, n):
            line.step(s)
    for line in lines:
        line.finish()
    for copy in copies:
        copy.wait()


def gather_rows(n, arrays, collective_id):
    count = len(arrays)
    rows, width = arrays[0].shape
    sems = [DMA((count, n))] * 3 + [DMA((count,))]
    return call(
        functools.partial(gather_kernel, n, rows, count),
        collective_id,
        "gather_rows",
        [HBM] * count,
        [jax.ShapeDtypeStruct((n * rows, width), a.dtype) for a in arrays],
        [HBM] * count,
        sems,
    )(*arrays)


def scatter_kernel(n, rows, width, parts_in, out, part, got, sent, arrived, local):
    i = lax.axis_index("tensor")
    copy = pltpu.make_async_copy(parts_in, part, local)
    copy.start()
    greet_line(n, i)
    copy.wait()
    line = LineScatter(n, i, rows, width, part, got, sent, arrived)
    for t in range(n - 1, 0, -1):
        for j in (t, n - 1 - t):
            for c in range(line.pieces):
                if j == t:
                    pl.when(i == 0)(functools.partial(line.at_end, j, c))
                else:
                    pl.when(i == n - 1)(functools.partial(line.at_end, j, c))
    for t in range(n - 1, 1, -1):
        for near in (True, False):
            for c in range(line.pieces):
                line.pass_on(t, c, near)
    for c in range(line.pieces):
        line.own(c, out)
    line.all_sent()


def scatter_rows(n, parts, collective_id, pieces=4):
    total, columns = parts.shape
    rows = total // n
    width = columns // pieces
    return call(
        functools.partial(scatter_kernel, n, rows, width),
        collective_id,
        "scatter_rows",
        [HBM],
        jax.ShapeDtypeStruct((rows, columns), jnp.float32),
        VMEM,
        [
            pltpu.VMEM((total, columns), jnp.bfloat16),
            pltpu.VMEM((total + rows, columns), jnp.bfloat16),
            DMA((n, pieces)),
            DMA((n + 1, pieces)),
            DMA,
        ],
    )(parts)


def ffn_kernel(
    n,
    tile,
    grad_tile,
    own_hidden,
    table,
    d_mlp_hbm,
    up_hbm,
    down_hbm,
    d_hidden,
    mlp_part,
    up_grad,
    down_grad,
    up,
    down,
    d_mlp,
    hidden,
    activated,
    d_pre,
    part,
    got,
    stage,
    to_left,
    to_right,
    arrived,
    sent,
    came,
    local,
    stage_sem,
):
    i = lax.axis_index("tensor")
    rows, width = own_hidden.shape
    units = up.shape[1]
    loads = [
        pltpu.make_async_copy(source, target, local.at[k])
        for k, (source, target) in enumerate(((up_hbm, up), (d_mlp_hbm, d_mlp), (down_hbm, down)))
    ]
    for load in loads:
        load.start()
    greet_line(n, i)
    line = LineGather(n, i, rows, own_hidden, hidden, to_left, to_right, arrived)
    line.start()
    sums = LineScatter(n, i, rows, tile, part, got, sent, came)
    hidden[rows_of(i, rows), :] = own_hidden[...]
    for load in loads:
        load.wait()

    def one_block(j):
        here = rows_of(j, rows)

        def gated(c, carry):
            at = pl.ds(pl.multiple_of(c * tile, tile), tile)
            d_mlp[here, at] = (d_mlp[here, at].astype(jnp.float32) * table[j, 5:6, at]).astype(
                jnp.bfloat16
            )
            return carry

        lax.fori_loop(0, width // tile, gated, 0)

        def first(c, carry):
            at = pl.ds(pl.multiple_of(c * tile, tile), tile)
            pre = mm(hidden[here, :], up[:, at])
            d_act = mm_nt(d_mlp[here, :], down[at, :])
            cdf = 0.5 * (1.0 + lax.erf(pre * (0.5**0.5)))
            density = jnp.exp(-0.5 * pre * pre) * ((0.5 / math.pi) ** 0.5)
            activated[here, at] = (pre * cdf).astype(jnp.bfloat16)
            d_pre[here, at] = (d_act * (cdf + pre * density)).astype(jnp.bfloat16)
            return carry

        lax.fori_loop(0, units // tile, first, 0)

        def second(c, carry):
            at = pl.ds(pl.multiple_of(c * tile, tile), tile)
            part[here, at] = mm_nt(d_pre[here, :], up[at, :]).astype(jnp.bfloat16)
            sums.at_end(j, c)
            return carry

        lax.fori_loop(0, width // tile, second, 0)

        def third(c, carry):
            at = pl.ds(pl.multiple_of(c * tile, tile), tile)
            mlp_part[here, at] = mm(activated[here, :], down[:, at]).astype(jnp.bfloat16)
            return carry

        lax.fori_loop(0, width // tile, third, 0)

    def visit(q, carry):
        s = (q + 1) // 2
        side = 1 - 2 * (q % 2)
        j = i + s * side

        @pl.when(q % 2 == 1)
        def _():
            line.step(s)

        @pl.when((j >= 0) & (j < n))
        def _():
            one_block(j)

        return carry

    lax.fori_loop(0, 2 * n - 1, visit, 0)

    count = (width // grad_tile) * (units // grad_tile)
    turns = 2 * max(n - 2, 1) * sums.pieces
    per_turn = -(-2 * count // turns)

    def square(ref, row, column):
        return ref.at[
            pl.ds(pl.multiple_of(row * grad_tile, grad_tile), grad_tile),
            pl.ds(pl.multiple_of(column * grad_tile, grad_tile), grad_tile),
        ]

    def put(slot, target):
        return pltpu.make_async_copy(stage.at[slot], target, stage_sem.at[slot])

    def one_grad(k, left, right, target):
        wide = right.shape[1] // grad_tile
        row, column = k // wide, k % wide
        slot = k % 2

        @pl.when(k >= 2)
        def _():
            put(slot, square(target, 0, 0)).wait()

        a = left[:, pl.ds(pl.multiple_of(row * grad_tile, grad_tile), grad_tile)]
        b = right[:, pl.ds(pl.multiple_of(column * grad_tile, grad_tile), grad_tile)]
        stage[slot] = mm_tn(a, b).astype(jnp.bfloat16)
        put(slot, square(target, row, column)).start()

    def tail(k, carry):
        t, c = 2 + k // (2 * sums.pieces), k % sums.pieces
        for near in (True, False):

            @pl.when((k // sums.pieces) % 2 == (0 if near else 1))
            def _():
                sums.pass_on(t, c, near)

        for extra in range(per_turn):
            item = k * per_turn + extra

            @pl.when(item < count)
            def _():
                one_grad(item, hidden, d_pre, up_grad)

            @pl.when(item == count)
            def _():
                for slot in range(2):
                    put(slot, square(up_grad, 0, 0)).wait()

            @pl.when((item >= count) & (item < 2 * count))
            def _():
                one_grad(item - count, activated, d_mlp, down_grad)

        return carry

    lax.fori_loop(0, turns, tail, 0)
    for slot in range(2):
        put(slot, square(down_grad, 0, 0)).wait()
    for c in range(sums.pieces):
        sums.own(c, d_hidden)
    line.finish()
    sums.all_sent()


def ffn(n, own_hidden, table, cotangents, up, down, collective_id, tile=512, grad_tile=512):
    rows, width = own_hidden.shape
    units = up.shape[1]
    pieces = width // tile
    low = jnp.bfloat16
    return call(
        functools.partial(ffn_kernel, n, tile, grad_tile),
        collective_id,
        "ffn",
        [VMEM, VMEM, HBM, HBM, HBM],
        [
            jax.ShapeDtypeStruct((rows, width), jnp.float32),
            jax.ShapeDtypeStruct((n * rows, width), low),
            jax.ShapeDtypeStruct((width, units), low),
            jax.ShapeDtypeStruct((units, width), low),
        ],
        [VMEM, VMEM, HBM, HBM],
        [
            pltpu.VMEM((width, units), low),
            pltpu.VMEM((units, width), low),
            pltpu.VMEM((n * rows, width), low),
            pltpu.VMEM((n * rows, width), low),
            pltpu.VMEM((n * rows, units), low),
            pltpu.VMEM((n * rows, units), low),
            pltpu.VMEM((n * rows, width), low),
            pltpu.VMEM(((n + 1) * rows, width), low),
            pltpu.VMEM((2, grad_tile, grad_tile), low),
            DMA((n,)),
            DMA((n,)),
            DMA((n,)),
            DMA((n, pieces)),
            DMA((n + 1, pieces)),
            DMA((3,)),
            DMA((2,)),
        ],
        flops=12 * n * rows * width * units,
    )(own_hidden, table, cotangents, up, down)


class PlaneGather:
    def __init__(self, n_dp, d, own, view, height, sent, came):
        self.n_dp, self.d, self.own, self.view, self.height = n_dp, d, own, view, height
        self.sent, self.came = sent, came
        self.square = n_dp == 8
        self.peers = [2 * k for k in range(1, n_dp // 2)]

    def copy(self, k, source, target, peer):
        return pltpu.make_async_remote_copy(
            src_ref=source,
            dst_ref=target,
            send_sem=self.sent.at[k],
            recv_sem=self.came.at[k],
            device_id=(self.d ^ peer, lax.axis_index("tensor")),
            device_id_type=MESH,
        )

    def slab(self, flip, half=None):
        if half is None:
            return self.view(self.d ^ flip, 0, self.height)
        return self.view(self.d ^ flip, half * (self.height // 2), self.height // 2)

    def owns(self):
        peers = [2, 4] if self.square else self.peers
        return [
            self.copy(k, self.own, self.slab(0), peer) for k, peer in enumerate([1] + peers)
        ]

    def relay_of(self, k):
        flip, half, peer = ((2, 0, 4), (4, 1, 2))[k - 1]
        return self.copy(2 + k, self.slab(flip, half), self.slab(flip, half), peer)

    def across(self):
        return [
            self.copy(3, self.slab(6, 0), self.slab(6, 0), 4),
            self.copy(4, self.slab(6, 1), self.slab(6, 1), 2),
        ]

    def hand(self, flip):
        base = 5 if self.square else len(self.peers) + 1
        k = base + flip // 2 - 1
        return self.copy(k, self.slab(flip), self.slab(flip), 1)

    def handed(self, flip):
        base = 5 if self.square else len(self.peers) + 1
        k = base + flip // 2 - 1
        return self.copy(k, self.slab(flip ^ 1), self.slab(flip ^ 1), 1)

    def start(self):
        for copy in self.owns():
            copy.start()

    def relay(self):
        if not self.square:
            return
        for k, flip in ((1, 2), (2, 4)):
            self.copy(k, self.own, self.slab(flip), flip).wait_recv()
            self.relay_of(k).start()
            self.hand(flip).start()

    def close(self):
        if self.square:
            for copy in self.across():
                copy.wait_recv()
            self.hand(6).start()
        else:
            for k, flip in enumerate(self.peers):
                self.copy(k + 1, self.own, self.slab(flip), flip).wait_recv()
                self.hand(flip).start()
        self.copy(0, self.own, self.slab(1), 1).wait_recv()
        for flip in self.peers:
            self.handed(flip).wait_recv()

    def finish(self):
        for copy in self.owns():
            copy.wait_send()
        if self.square:
            for k in (1, 2):
                self.relay_of(k).wait_send()
        for flip in self.peers:
            self.hand(flip).wait_send()


def plane_sems(n_dp):
    return 8 if n_dp == 8 else n_dp - 1


def greet_all(n, n_dp, d, i):
    barrier = pltpu.get_barrier_semaphore()
    for flip in range(1, n_dp):
        pl.semaphore_signal(barrier, inc=1, device_id=(d ^ flip, i), device_id_type=MESH)
    for turn in range(1, n):
        pl.semaphore_signal(
            barrier, inc=1, device_id=(d, lax.rem(i + turn, n)), device_id_type=MESH
        )
    pl.semaphore_wait(barrier, n_dp + n - 2)


def front_kernel(
    n,
    n_dp,
    heads,
    tile,
    x_own,
    cot_own,
    noise,
    mod_w,
    chosen,
    bias,
    attend_w,
    merge_w,
    up_w,
    down_w,
    cot_full,
    hidden,
    qkv,
    lse,
    attended,
    att_rows,
    attn_out,
    middle,
    hidden_second,
    table,
    attend_full,
    merge_full,
    up_full,
    down_full,
    x_full,
    attend,
    merge,
    noise_all,
    terms,
    terms_all,
    columns,
    noise_sem,
    terms_sem,
    column_sem,
    x_sem,
    cot_sem,
    merge_sem,
    weight_sent,
    weight_came,
    out_sem,
    att_sem,
    local,
):
    d, i = lax.axis_index("dp"), lax.axis_index("tensor")
    rows, width = x_own.shape
    k_rows, own_cols = mod_w.shape
    head_cols = heads * HEAD_DIM
    low, f32 = jnp.bfloat16, jnp.float32
    merge_rows, merge_cols = merge_w.shape
    down_cols = down_w.shape[1]
    merge_slab = merge.at[:, pl.ds(pl.multiple_of(d * merge_cols, merge_cols), merge_cols)]

    def row_view(full, height):
        return lambda at, start, count: full.at[
            pl.ds(pl.multiple_of(at * height + start, 16), count), :
        ]

    def column_view(full, wide):
        return lambda at, start, count: full.at[
            pl.ds(start, count), pl.ds(pl.multiple_of(at * wide, wide), wide)
        ]

    weights = [
        PlaneGather(n_dp, d, own, view, height, weight_sent.at[k], weight_came.at[k])
        for k, (own, view, height) in enumerate(
            (
                (attend_w, row_view(attend, k_rows), k_rows),
                (merge_slab, column_view(merge, merge_cols), n * merge_rows),
                (up_w, row_view(up_full, k_rows), k_rows),
                (down_w, column_view(down_full, down_cols), down_w.shape[0]),
            )
        )
    ]
    attend_g, merge_g, up_g, down_g = weights
    copies = [
        pltpu.make_async_copy(source, target, local.at[k])
        for k, (source, target) in enumerate(
            (
                (cot_own, cot_full.at[rows_of(i, rows)]),
                (attend_w, attend_g.slab(0)),
                (merge_w, merge_slab.at[rows_of(i, merge_rows)]),
                (up_w, up_g.slab(0)),
                (down_w, down_g.slab(0)),
            )
        )
    ]
    for copy in copies:
        copy.start()
    greet_all(n, n_dp, d, i)

    def to_plane(source, target, sems, flip):
        return pltpu.make_async_remote_copy(
            src_ref=source.at[d ^ flip],
            dst_ref=target.at[d],
            send_sem=sems.at[0, flip],
            recv_sem=sems.at[1, flip],
            device_id=(d ^ flip, i),
            device_id_type=MESH,
        )

    def from_plane(target, sems, flip):
        return pltpu.make_async_remote_copy(
            src_ref=target.at[d ^ flip],
            dst_ref=target.at[d ^ flip],
            send_sem=sems.at[0, flip],
            recv_sem=sems.at[1, flip],
            device_id=(d ^ flip, i),
            device_id_type=MESH,
        )

    for flip in range(1, n_dp):
        to_plane(noise, noise_all, noise_sem, flip).start()
    merge_line = LineGather(
        n, i, merge_rows, merge_w, merge_slab, merge_sem.at[0], merge_sem.at[1], merge_sem.at[2]
    )
    x_line = LineGather(n, i, rows, x_own, x_full, x_sem.at[0], x_sem.at[1], x_sem.at[2])
    cot_line = LineGather(
        n, i, rows, cot_own, cot_full, cot_sem.at[0], cot_sem.at[1], cot_sem.at[2]
    )
    x_line.start()
    attend_g.start()
    merge_line.start()
    noise_all[d] = noise[d]
    x_full[rows_of(i, rows), :] = x_own[...]
    for flip in range(1, n_dp):
        from_plane(noise_all, noise_sem, flip).wait_recv()
    images = noise_all[...].reshape(n_dp * 8, k_rows).astype(low)
    for c in range(own_cols // tile):
        terms[:, :, c * tile : (c + 1) * tile] = mm(
            images, mod_w[:, c * tile : (c + 1) * tile]
        ).reshape(n_dp, 8, tile)
    for flip in range(1, n_dp):
        to_plane(terms, terms_all, terms_sem, flip).start()
    terms_all[d] = terms[d]
    for flip in range(1, n_dp):
        from_plane(terms_all, terms_sem, flip).wait_recv()
    columns[pl.ds(pl.multiple_of(i * 8, 8), 8), :] = jnp.sum(terms_all[...], axis=0)
    own_columns = columns.at[pl.ds(pl.multiple_of(i * 8, 8), 8)]
    column_line = LineGather(
        n, i, 8, own_columns, columns, column_sem.at[0], column_sem.at[1], column_sem.at[2]
    )
    column_line.start()
    for s in range(1, n):
        column_line.step(s)
    unit = math.gcd(width, own_cols)

    def fill(j, carry):
        for number in range(6):
            for start in range(0, width, unit):
                at = number * width + start
                part = columns[at // own_cols * 8 : at // own_cols * 8 + 8, pl.ds(at % own_cols, unit)]
                table[j, number : number + 1, start : start + unit] = jnp.sum(
                    part * chosen[j][:, :1], axis=0, keepdims=True
                )
        return carry

    lax.fori_loop(0, n, fill, 0)
    x_line.step(1)
    attend_g.relay()
    merge_line.step(1)
    for copy in copies:
        copy.wait()
    attend_g.close()
    up_g.start()
    keep_attend = pltpu.make_async_copy(attend, attend_full, out_sem.at[0])
    keep_merge = pltpu.make_async_copy(merge, merge_full, out_sem.at[1])
    keep_attend.start()

    def tiles(count):
        return [slice(c * tile, (c + 1) * tile) for c in range(count // tile)]

    def one_block(j):
        here = rows_of(j, rows)
        squares = jnp.zeros((rows, 1), f32)
        for at in tiles(width):
            v = x_full[here, at].astype(f32)
            squares += jnp.sum(v * v, axis=1, keepdims=True)
        root = lax.rsqrt(squares * (1.0 / width) + 1e-06)
        for at in tiles(width):
            v = x_full[here, at].astype(f32) * root
            hidden[here, at] = (v * (1.0 + table[j, 1:2, at]) + table[j, 0:1, at]).astype(low)
        wide = qkv.shape[1]
        step = math.gcd(wide, 512)
        for c in range(wide // step):
            at = slice(c * step, (c + 1) * step)
            qkv[here, at] = mm(hidden[here, :], attend[:, at]).astype(low)

    def visit(q, carry):
        s = (q + 1) // 2
        side = 1 - 2 * (q % 2)
        j = i + s * side

        @pl.when((q % 2 == 1) & (s + 1 < n))
        def _():
            x_line.step(s + 1)
            merge_line.step(s + 1)

        @pl.when(q == 2 * n - 5)
        def _():
            up_g.relay()
            merge_g.start()
            cot_line.start()

        @pl.when((j >= 0) & (j < n))
        def _():
            one_block(j)

        return carry

    lax.fori_loop(0, 2 * n - 1, visit, 0)

    area = min(256, n * rows)
    areas = n * rows // area
    owners = area // rows

    def to_owner(j):
        return pltpu.make_async_remote_copy(
            src_ref=attended.at[rows_of(j, rows), :],
            dst_ref=att_rows.at[:, pl.ds(pl.multiple_of(i * head_cols, head_cols), head_cols)],
            send_sem=att_sem.at[0, j],
            recv_sem=att_sem.at[1, i],
            device_id=(d, j),
            device_id_type=MESH,
        )

    def from_source(t):
        return pltpu.make_async_remote_copy(
            src_ref=attended.at[rows_of(t, rows), :],
            dst_ref=att_rows.at[:, pl.ds(pl.multiple_of(t * head_cols, head_cols), head_cols)],
            send_sem=att_sem.at[0, t],
            recv_sem=att_sem.at[1, t],
            device_id=(d, t),
            device_id_type=MESH,
        )

    def attend_area(turn, carry):
        here_at = lax.rem(i // owners + 1 + turn, areas)
        here = rows_of(here_at, area)
        for h in range(heads):
            first = h * 3 * HEAD_DIM
            q = qkv[here, first : first + HEAD_DIM]
            parts = []
            for b in range(areas):
                key = qkv[b * area : (b + 1) * area, first + HEAD_DIM : first + 2 * HEAD_DIM]
                parts.append(mm_nt(key, q) * HEAD_DIM ** (-0.5) + bias[here_at, b])
            highest = parts[0].max(axis=0, keepdims=True)
            for part in parts[1:]:
                highest = jnp.maximum(highest, part.max(axis=0, keepdims=True))
            parts = [jnp.exp(part - highest) for part in parts]
            totals = sum(jnp.sum(part, axis=0, keepdims=True) for part in parts)
            inverse = 1.0 / totals
            out = jnp.zeros((HEAD_DIM, area), f32)
            for b in range(areas):
                value = qkv[b * area : (b + 1) * area, first + 2 * HEAD_DIM : first + 3 * HEAD_DIM]
                out += mm_tn(value, (parts[b] * inverse).astype(low))
            attended[here, h * HEAD_DIM : (h + 1) * HEAD_DIM] = out.T.astype(low)
            lse[pl.ds(here_at * heads + h, 1), :] = highest + jnp.log(totals)
        for k in range(owners):
            j = here_at * owners + k

            @pl.when(j != i)
            def _():
                to_owner(j).start()

        @pl.when(turn == (areas - 1) // 2)
        def _():
            up_g.close()
            cot_line.step(1)

        @pl.when(turn == areas - 1)
        def _():
            merge_g.relay()
            down_g.start()

        return carry

    lax.fori_loop(0, areas, attend_area, 0)
    att_rows[:, pl.ds(pl.multiple_of(i * head_cols, head_cols), head_cols)] = attended[
        rows_of(i, rows), :
    ]
    if n > 2:
        cot_line.step(2)
    merge_g.close()
    keep_merge.start()
    for turn in range(1, n):
        from_source(lax.rem(i + turn, n)).wait_recv()
    squares = jnp.zeros((rows, 1), f32)
    for at in tiles(width):
        out = mm(att_rows[...], merge[:, at])
        attn_out[:, at] = out
        v = x_own[:, at].astype(f32) + table[i, 2:3, at] * out
        middle[:, at] = v
        squares += jnp.sum(v * v, axis=1, keepdims=True)
    root = lax.rsqrt(squares * (1.0 / width) + 1e-06)
    for at in tiles(width):
        v = middle[:, at] * root
        hidden_second[:, at] = (v * (1.0 + table[i, 4:5, at]) + table[i, 3:4, at]).astype(low)
    down_g.relay()
    for s in range(3, n):
        cot_line.step(s)
    down_g.close()
    keep_attend.wait()
    keep_merge.wait()
    for flip in range(1, n_dp):
        to_plane(noise, noise_all, noise_sem, flip).wait_send()
        to_plane(terms, terms_all, terms_sem, flip).wait_send()
    for line in (merge_line, x_line, column_line, cot_line):
        line.finish()
    for turn in range(1, n):
        to_owner(lax.rem(i + turn, n)).wait_send()
    for weight in weights:
        weight.finish()


def front(n, n_dp, x, cot, noise, mod_w, chosen, bias, attend_w, merge_w, up_w, down_w, number):
    rows, width = x.shape
    k_rows, own_cols = mod_w.shape
    wide = attend_w.shape[1]
    heads = wide // (3 * HEAD_DIM)
    total = n * rows
    areas = bias.shape[0]
    low, f32 = jnp.bfloat16, jnp.float32
    sds = jax.ShapeDtypeStruct
    count = plane_sems(n_dp)
    return call(
        functools.partial(front_kernel, n, n_dp, heads, 512),
        number,
        "front",
        [VMEM] * 5 + [pl.BlockSpec(memory_space=pltpu.SMEM)] + [VMEM] * 4,
        [
            sds((total, width), low),
            sds((total, width), low),
            sds((total, wide), low),
            sds((areas * heads, total // areas), f32),
            sds((total, heads * HEAD_DIM), low),
            sds((rows, width), low),
            sds((rows, width), f32),
            sds((rows, width), f32),
            sds((rows, width), low),
            sds((n, 8, width), f32),
            sds((n_dp * k_rows, wide), low),
            sds((n * merge_w.shape[0], n_dp * merge_w.shape[1]), low),
            sds((n_dp * k_rows, up_w.shape[1]), low),
            sds((down_w.shape[0], n_dp * down_w.shape[1]), low),
        ],
        [HBM] + [VMEM] * 9 + [HBM] * 4,
        [
            pltpu.VMEM((total, width), low),
            pltpu.VMEM((n_dp * k_rows, wide), low),
            pltpu.VMEM((n * merge_w.shape[0], n_dp * merge_w.shape[1]), low),
            pltpu.VMEM((n_dp, 8, k_rows), f32),
            pltpu.VMEM((n_dp, 8, own_cols), f32),
            pltpu.VMEM((n_dp, 8, own_cols), f32),
            pltpu.VMEM((n * 8, own_cols), f32),
            DMA((2, n_dp)),
            DMA((2, n_dp)),
            DMA((3, n)),
            DMA((3, n)),
            DMA((3, n)),
            DMA((3, n)),
            DMA((4, count)),
            DMA((4, count)),
            DMA((2,)),
            DMA((2, n)),
            DMA((5,)),
        ],
        flops=2 * total * width * wide,
    )(x, cot, noise, mod_w, chosen, bias, attend_w, merge_w, up_w, down_w)


def attention_backward(packed, grad_out, attended, lse, image_of, heads, score_scale):
    tokens = packed.shape[0]
    areas = lse.shape[0] // heads
    split = packed.reshape(tokens, heads, 3, HEAD_DIM)
    queries, keys, values = split[:, :, 0], split[:, :, 1], split[:, :, 2]
    grads = grad_out.reshape(tokens, heads, HEAD_DIM)
    logs = lse.reshape(areas, heads, -1).transpose(1, 0, 2).reshape(heads, tokens)
    scores = (
        jnp.einsum("qhd,khd->hqk", queries, keys, preferred_element_type=jnp.float32)
        * score_scale
    )
    same_image = image_of[:, None] == image_of[None, :]
    scores = jnp.where(same_image[None], scores, MASKED)
    probs = jnp.exp(scores - logs[:, :, None])
    grad_probs = jnp.einsum("qhd,khd->hqk", grads, values, preferred_element_type=jnp.float32)
    inner = jnp.sum(probs * grad_probs, axis=-1, keepdims=True)
    grad_scores = (probs * (grad_probs - inner)).astype(jnp.bfloat16)

    def product(form, a, b):
        return jnp.einsum(form, a, b, preferred_element_type=jnp.float32)

    d_queries = product("hqk,khd->qhd", grad_scores, keys) * score_scale
    d_keys = product("hqk,qhd->khd", grad_scores, queries) * score_scale
    d_values = product("hqk,qhd->khd", probs.astype(jnp.bfloat16), grads)
    return jnp.stack([d_queries, d_keys, d_values], axis=2).astype(jnp.bfloat16).reshape(tokens, -1)


def on_device(
    block_input,
    cotangent,
    noise_embed,
    image_sizes,
    attend_weight,
    merge_weight,
    up_weight,
    down_weight,
    modulate_weight,
):
    n = lax.axis_size("tensor")
    n_dp = lax.axis_size("dp")
    place = lax.axis_index("tensor")
    dp_place = lax.axis_index("dp")
    rows, width = block_input.shape
    tokens = n * rows
    images = image_sizes.shape[1]
    k_rows = modulate_weight.shape[0]

    sizes_row = image_sizes[0]
    ends = [sum(sizes_row[j] for j in range(last + 1)) for last in range(images)]

    def image_at(places):
        return sum((places >= end).astype(jnp.int32) for end in ends)

    image_of = image_at(jnp.arange(tokens, dtype=jnp.int32))
    block_images = image_at(jnp.arange(n, dtype=jnp.int32) * rows)
    chosen = (block_images[:, None] == jnp.arange(8, dtype=jnp.int32)[None, :]) & (
        jnp.arange(8) < images
    )[None]
    chosen = jnp.broadcast_to(chosen.astype(jnp.float32)[:, :, None], (n, 8, 128))
    area = min(256, tokens)
    area_images = image_at(jnp.arange(tokens // area, dtype=jnp.int32) * area)
    bias = jnp.where(area_images[:, None] == area_images[None, :], 0.0, MASKED)
    noise_low = jax.nn.silu(noise_embed.astype(jnp.float32)).astype(jnp.bfloat16)
    noise_slabs = noise_low.astype(jnp.float32).reshape(images, n_dp, k_rows).transpose(1, 0, 2)
    noise_slabs = jnp.pad(noise_slabs, ((0, 0), (0, 8 - images), (0, 0)))
    noise_low_cols = lax.dynamic_slice_in_dim(
        lax.all_gather(noise_low, "dp", axis=0, tiled=True), dp_place * k_rows, k_rows, 1
    )
    (
        cot_full,
        hidden_first,
        packed,
        lse,
        attended,
        att_rows,
        attn_out,
        middle,
        hidden_second,
        table,
        attend_full,
        merge_full,
        up_full,
        down_full,
    ) = front(
        n,
        n_dp,
        block_input,
        cotangent,
        noise_slabs,
        modulate_weight,
        chosen,
        bias,
        attend_weight,
        merge_weight,
        up_weight,
        down_weight,
        0,
    )
    heads_local = packed.shape[1] // (3 * HEAD_DIM)
    score_scale = HEAD_DIM ** (-0.5)
    own_table = lax.dynamic_index_in_dim(table, place, 0, keepdims=False)
    shift_first, scale_first, gate_first, shift_second, scale_second, gate_second = [
        own_table[number : number + 1] for number in range(6)
    ]
    inputs = block_input.astype(jnp.float32)
    grad_rows = cotangent.astype(jnp.float32)
    own_image = lax.dynamic_index_in_dim(block_images, place, 0, keepdims=False)

    def rows_back(values, scale_part):
        return jax.vjp(modulate_rows, values, jnp.broadcast_to(scale_part, values.shape), jnp.zeros_like(values))[1]

    back_first = rows_back(inputs, scale_first)
    back_second = rows_back(middle, scale_second)
    d_hidden_second, mlp_part, up_local, down_local = ffn(
        n, hidden_second, table, cot_full, up_full, down_full, 2
    )
    mlp_out = scatter_rows(n, mlp_part, 3)
    block_output = (middle + gate_second * mlp_out).astype(jnp.bfloat16)
    d_gate_second = grad_rows * mlp_out
    d_mid_norm, d_scale_second, d_shift_second = back_second(d_hidden_second)
    d_middle = grad_rows + d_mid_norm
    d_gate_first = d_middle * attn_out
    d_attn = gather_rows(n, [(gate_first * d_middle).astype(jnp.bfloat16)], 4)[0]

    down_part = lax.psum_scatter(
        down_local, "dp", scatter_dimension=1, tiled=True
    ).astype(jnp.float32)
    up_part = lax.psum_scatter(
        up_local, "dp", scatter_dimension=0, tiled=True
    ).astype(jnp.float32)

    own_heads = heads_local * HEAD_DIM
    merge_own = lax.dynamic_slice_in_dim(merge_full, place * own_heads, own_heads, 0)
    merge_local = dot(attended, d_attn, ROWS_ROWS)
    merge_part = lax.psum_scatter(
        merge_local.astype(jnp.bfloat16), "dp", scatter_dimension=1, tiled=True
    ).astype(jnp.float32)
    d_attended = dot(d_attn, merge_own, COLS_COLS).astype(jnp.bfloat16)
    d_qkv = attention_backward(
        packed, d_attended, attended, lse, image_of, heads_local, score_scale
    )
    attend_local = dot(hidden_first, d_qkv, ROWS_ROWS)
    attend_part = lax.psum_scatter(
        attend_local.astype(jnp.bfloat16), "dp", scatter_dimension=0, tiled=True
    ).astype(jnp.float32)
    d_hidden_first = scatter_rows(
        n, dot(d_qkv, attend_full, COLS_COLS).astype(jnp.bfloat16), 5
    )
    d_in_norm, d_scale_first, d_shift_first = back_first(d_hidden_first)
    input_grad = (d_middle + d_in_norm).astype(jnp.bfloat16)

    token_grads = [
        d_shift_first,
        d_scale_first,
        d_gate_first,
        d_shift_second,
        d_scale_second,
        d_gate_second,
    ]
    image_rows = [
        jnp.concatenate(
            [jnp.where(own_image == j, jnp.sum(part, axis=0, keepdims=True), 0.0) for part in token_grads], axis=1
        )
        for j in range(images)
    ]
    d_mod_terms = jnp.concatenate(image_rows, axis=0)
    d_mod_cols = lax.psum_scatter(
        d_mod_terms, "tensor", scatter_dimension=1, tiled=True
    ).astype(jnp.bfloat16)
    d_mod_all = lax.all_gather(d_mod_cols, "dp", axis=0, tiled=True)
    modulate_part = dot(noise_low_cols, d_mod_all, ROWS_ROWS)
    noise_terms = dot(d_mod_all, modulate_weight, COLS_COLS)
    noise_cols = lax.psum(noise_terms, "tensor")
    noise_sum = lax.all_to_all(noise_cols, "dp", split_axis=0, concat_axis=1, tiled=True)
    silu_back = jax.vjp(jax.nn.silu, noise_embed.astype(jnp.float32))[1]
    noise_grad = silu_back(noise_sum)[0]
    return (
        block_output,
        input_grad,
        noise_grad,
        attend_part,
        merge_part,
        up_part,
        down_part,
        modulate_part,
    )


def solution(mesh):
    whole_rows = P(("dp", "tensor"), None)
    by_dp = P("dp", None)
    tall = P("dp", "tensor")
    wide = P("tensor", "dp")
    return jax.shard_map(
        on_device,
        mesh=mesh,
        in_specs=(whole_rows, whole_rows, by_dp, by_dp, tall, wide, tall, wide, tall),
        out_specs=(whole_rows, whole_rows, by_dp, tall, wide, tall, wide, tall),
        check_vma=False,
    )
```

time: 1100 us -> 1040 us (0.945)
  Pallas kernels: 0 us -> 536 us
  waiting for transfers between devices: 558 us -> 295 us
  starting transfers between devices: 151 us -> 3.8 us
  matrix products: 202 us -> 79.9 us
  other arithmetic: 80.3 us -> 45.3 us
  blocking collectives: 53 us -> 36.9 us
  local copies, waits for them, and re-layouts: 29 us -> 17.8 us
    pallas_call x0 -> x5, Pallas kernels: none -> 536 us  [the longest x1 199 us: front(): call(functools.partial(front_kernel, n, n_dp, heads, 512), number, 'front...]
    ppermute x48 -> x0, waiting for transfers between devices: 365 us -> none  [the longest x12 158 us: gather_line(): lax.ppermute(to_left, 'tensor', [(j, j - 1) for j in range(1, n - step +...]
    ppermute x48 -> x0, starting transfers between devices: 147 us -> none  [the longest x12 74 us: scatter_line(): lax.ppermute(right_part.astype(jnp.bfloat16), 'tensor', [(j, j + 1) for j...]
    dot_general x36 -> x6, matrix products: 173 us -> 36.5 us  [dot(): return lax.dot_general(a, b, dims, preferred_element_type=jnp.float32)]
    reduce_scatter x2, waiting for transfers between devices: 8.29 us -> 144 us  [the longest x1 72.3 us: on_device(): lax.psum_scatter(up_local, 'dp', scatter_dimension=0, tiled=True)]
    unnamed x12 -> x6, waiting for transfers between devices: 155 us -> 79.3 us
    reduce_scatter x1, waiting for transfers between devices: 26.3 us -> 63.8 us  [on_device(): lax.psum_scatter(attend_local.astype(jnp.bfloat16), 'dp', scatter_dimensi...]
    convert_element_type x22 -> x4, other arithmetic: 25.2 us -> 6.31 us  [the longest x1 2.79 us: on_device(): up_part = lax.psum_scatter(up_local, 'dp', scatter_dimension=0, tiled=Tru...]
  transfers between devices with their start and end apart: 59 -> 6, of which waited for: 32 -> 6; matrix products, arithmetic and copies ran while one was open for 26% -> 3% of each run, Pallas kernels for 0% -> 0%
where the time goes in v2:
time: 1040 us; the launch traced here: 1030 us
  Pallas kernels  536 us (52%)
  waiting for transfers between devices  295 us (28%)
  matrix products  79.9 us (8%)
  other arithmetic  45.3 us (4%)
  blocking collectives  36.9 us (4%)
  between operations  19.6 us (2%)
  local copies, waits for them, and re-layouts  17.8 us (2%)
    pallas_call x1, Pallas kernels, front(): call(functools.partial(front_kernel, n, n_dp, heads, 512), number, 'front...  199 us
    pallas_call x2, Pallas kernels, scatter_rows(): call(functools.partial(scatter_kernel, n, rows, width), collective_id, 's...  137 us
    pallas_call x1, Pallas kernels, ffn(): call(functools.partial(ffn_kernel, n, tile, grad_tile), collective_id, 'f...  130 us
    unnamed x6, waiting for transfers between devices  79.3 us
    reduce_scatter x1, waiting for transfers between devices, on_device(): lax.psum_scatter(up_local, 'dp', scatter_dimension=0, tiled=True)  72.3 us
    reduce_scatter x1, waiting for transfers between devices, on_device(): lax.psum_scatter(down_local, 'dp', scatter_dimension=1, tiled=True)  72.1 us
    pallas_call x1, Pallas kernels, gather_rows(): call(functools.partial(gather_kernel, n, rows, count), collective_id, 'ga...  69.7 us
    reduce_scatter x1, waiting for transfers between devices, on_device(): lax.psum_scatter(attend_local.astype(jnp.bfloat16), 'dp', scatter_dimensi...  63.8 us
  transfers between devices with their start and end apart: 6, of which 6 were waited for; matrix products, arithmetic and copies ran while one was open for 3% of the time, Pallas kernels for 0%

profile of v2, /device:TPU:0, one launch (start us, length us, event | category | flops | bytes accessed | tf_op | source)
XLA Modules:
  0.0 1034.1 jit_solution(1858993466384091244)
XLA Ops:
  19.0 198.9 %front.1 = (bf16[1024,2048]{1,0:T(8,128)(2,1)}, bf16[1024,2048]{1,0:T(8,128)(2,1)}, bf16[1024,1536]{1,0:T(8,128)(2,1)}, f32[16,256]{1,0:T(8,128)}, bf16[1024,512...) custom-call(bf16[256,2048]{1,0:T(8,128)(2,1)} %x_own.1, ...), custom_call_target="tpu_custom_call" | custom-call | flops 6442450944 | bytes 1048576 | tf_op jit(solution)/shard_map/front/pallas_call | solution.py:947
  221.1 130.4 %ffn.1 = (f32[256,2048]{1,0:T(8,128)}, bf16[1024,2048]{1,0:T(8,128)(2,1)}, bf16[2048,2048]{1,0:T(8,128)(2,1)}, bf16[2048,2048]{1,0:T(8,128)(2,1)}) custom-call(bf16[256,2048]{1,0:T(8,128)(2,1)} %get-tuple-element.27.own_hidden, f32[4,8,2048]{2,1,0:T(8,128)} %get-tuple-element.26.table, bf16[1024,2048]{1,0:T(8,128)(2,1)} %get-tuple-element.28.d_mlp_hbm, ...), custom_call_target="tpu_custom_call" | custom-call | flops 51539607552 | bytes 1048576 | tf_op jit(solution)/shard_map/ffn/pallas_call | solution.py:486
  351.5 69.1 %scatter_rows.2 = f32[256,2048]{1,0:T(8,128)} custom-call(bf16[1024,2048]{1,0:T(8,128)(2,1)} %get-tuple-element.31.parts_in), custom_call_target="tpu_custom_call" | custom-call | bytes 1048576 | tf_op jit(solution)/shard_map/scatter_rows/pallas_call | solution.py:299
  424.8 4.5 fusion.2
  431.7 69.7 %gather_rows.1 = bf16[1024,2048]{1,0:T(8,128)(2,1)} custom-call(bf16[256,2048]{1,0:T(8,128)(2,1)} %multiply_convert_fusion.3.refs_0_), custom_call_target="tpu_custom_call" | custom-call | bytes 1048576 | tf_op jit(solution)/shard_map/gather_rows/pallas_call | solution.py:261
  504.7 6.4 fusion.11
  511.0 8.1 fusion.22
  519.2 16.0 %multiply_reduce_fusion = (f32[4,1024]{1,0:T(4,128)}, f32[4,1024,1024]{1,2,0:T(8,128)}) fusion(f32[4,1024,1024]{1,2,0:T(8,128)} %fusion.22, f32[4,1024]{1,0:T(4,128)S(1)} %bitcast.119, bf16[1024,4,3,128]{0,3,2,1:T(8,128)(2,1)} %bitcast.104, pred[1024,1024]{0,1:T(8,128)(4,1)} %broadcast_compare_fusion), kind=kOutput, calls=%fused_computation.1 | convolution fusion | flops 1094709248 | bytes 36732928 | tf_op jit(solution)/shard_map/qhd,khd->hqk/dot_general | solution.py:1001
  535.2 9.8 fusion.17
  545.1 10.6 %multiply_convert_fusion = bf16[4,1024,1024]{1,2,0:T(8,128)(2,1)} fusion(f32[4,1024,1024]{1,2,0:T(8,128)} %get-tuple-element.87, f32[4,1024,1024]{1,2,0:T(8,128)S(1)} %bitcast.102, f32[4,1024]{1,0:T(4,128)} %get-tuple-element.86), kind=kLoop, calls=%fused_computation | loop fusion | flops 12582912 | bytes 41959424 | tf_op jit(solution)/shard_map/convert_element_type | solution.py:1009
  555.7 6.8 fusion.21
  569.7 8.4 convolution_convert_fusion.1.parts_in
  578.1 68.2 %scatter_rows.3 = f32[256,2048]{1,0:T(8,128)} custom-call(bf16[1024,2048]{1,0:T(8,128)(2,1)} %convolution_convert_fusion.1.parts_in), custom_call_target="tpu_custom_call" | custom-call | bytes 1048576 | tf_op jit(solution)/shard_map/scatter_rows/pallas_call | solution.py:299
  649.3 4.0 copy.56
  654.6 5.9 convolution_convert_fusion.2
  660.5 11.5 %convolution_convert_fusion = bf16[2048,1536]{1,0:T(8,128)(2,1)} fusion(bf16[1024,2048]{1,0:T(8,128)(2,1)} %get-tuple-element.38, bf16[1024,1536]{0,1:T(8,128)(2,1)} %bitcast.111), kind=kOutput, calls=%fused_computation.5 | convolution fusion | flops 6445596672 | bytes 13631488 | tf_op jit(solution)/shard_map/dot_general | solution.py:28
  673.4 8.7 all-gather.1
  685.3 78.2 %reduce-scatter.16.cloned.1.call-done = f32[3072,4]{1,0:T(8,128)} async-done(((f32[12288,4]{1,0:T(8,128)}), f32[3072,4]{1,0:T(8,128)}) %reduce-scatter.16.cloned.1.call-update) | async-done | bytes 49168
  765.4 9.2 all-gather
  776.8 19.1 %psum.7 = f32[8,4,256]{2,1,0:T(4,128)} all-reduce(f32[8,4,256]{2,1,0:T(4,128)S(1)} %all_to_all.14), channel_id=1, replica_groups=mesh['dp'=8,'tensor'=4] {'tensor'}, use_global_device_ids=true, to_apply=%region_12.13 | all-reduce | flops 8192 | bytes 65536 | tf_op jit(solution)/shard_map/psum | solution.py:1165
  804.6 4.5 reduce-scatter.10.cloned.1.call-done
  810.9 63.8 %reduce-scatter.8.cloned.1.call-done = bf16[256,1536]{1,0:T(8,128)(2,1)} async-done(((bf16[2048,1536]{1,0:T(8,128)(2,1)}), bf16[256,1536]{1,0:T(8,128)(2,1)}) %reduce-scatter.8.cloned.1.call-update) | async-done | bytes 786448 | tf_op jit(solution)/shard_map/reduce_scatter | solution.py:1135
  877.1 72.1 %reduce-scatter.14.cloned.1.call-done = bf16[2048,256]{1,0:T(8,128)(2,1)} async-done(((bf16[2048,2048]{1,0:T(8,128)(2,1)}), bf16[2048,256]{1,0:T(8,128)(2,1)}) %reduce-scatter.14.cloned.1.call-update) | async-done | bytes 1048592 | tf_op jit(solution)/shard_map/reduce_scatter | solution.py:1117
  952.0 72.3 %reduce-scatter.12.cloned.1.call-done = bf16[256,2048]{1,0:T(8,128)(2,1)} async-done(((bf16[2048,2048]{1,0:T(8,128)(2,1)}), bf16[256,2048]{1,0:T(8,128)(2,1)}) %reduce-scatter.12.cloned.1.call-update) | async-done | bytes 1048592 | tf_op jit(solution)/shard_map/reduce_scatter | solution.py:1120
  (133 shorter events, 58.5 us)
Async XLA Ops:
  7.2 756.4 %reduce-scatter.16.cloned.1.call-start = ((), (), s32[]{:S(2)}) async-start(), calls=%async_computation.10 | async-start | bytes 7864320
  351.5 70.3 %copy-start.4 = (f32[256,2048]{1,0:T(8,128)S(1)}, f32[256,2048]{1,0:T(8,128)}, u32[]{:S(2)}) copy-start(f32[256,2048]{1,0:T(8,128)} %get-tuple-element.25) | copy-start | bytes 6291460
  351.5 73.3 %copy-start.12 = (bf16[256,2048]{1,0:T(8,128)(2,1)S(1)}, bf16[256,2048]{1,0:T(8,128)(2,1)}, u32[]{:S(2)}) copy-start(bf16[256,2048]{1,0:T(8,128)(2,1)} %cot_own.1) | copy-start | bytes 3145732
  420.6 4.2 copy-start.6
  420.6 4.2 copy-start.7
  504.6 6.4 copy-start.1
  511.0 8.2 copy-start.8
  511.0 8.1 copy-start.14
  519.2 16.1 %copy-start.9 = (bf16[1024,512]{0,1:T(8,128)(2,1)S(1)}, bf16[1024,512]{0,1:T(8,128)(2,1)}, u32[]{:S(2)}) copy-start(bf16[1024,512]{0,1:T(8,128)(2,1)} %copy-done.8) | copy-start | bytes 3145732
  519.2 25.9 %slice-start = ((s8[16777216]{0:T(1024)(128)(4,1)}), s8[4194304]{0:T(1024)(128)(4,1)S(1)}, s32[]{:S(2)}) async-start(s8[16777216]{0:T(1024)(128)(4,1)} %bitcast.101), calls=%async_computation.11 | async-start | bytes 8388608
  519.2 25.9 %slice-start.1 = ((s8[16777216]{0:T(1024)(128)(4,1)}), s8[4194304]{0:T(1024)(128)(4,1)S(1)}, s32[]{:S(2)}) async-start(s8[16777216]{0:T(1024)(128)(4,1)} %bitcast.101), calls=%async_computation.12 | async-start | bytes 8388608
  519.2 25.9 %slice-start.2 = ((s8[16777216]{0:T(1024)(128)(4,1)}), s8[4194304]{0:T(1024)(128)(4,1)S(1)}, s32[]{:S(2)}) async-start(s8[16777216]{0:T(1024)(128)(4,1)} %bitcast.101), calls=%async_computation.13 | async-start | bytes 8388608
  535.2 9.8 slice-start.3
  555.6 6.8 copy-start
  562.4 4.9 copy-start.10
  562.4 7.3 slice-start.4
  578.1 68.3 %copy-start.5 = (bf16[256,2048]{1,0:T(8,128)(2,1)S(1)}, bf16[256,2048]{1,0:T(8,128)(2,1)}, u32[]{:S(2)}) copy-start(bf16[256,2048]{1,0:T(8,128)(2,1)} %x_own.1) | copy-start | bytes 3145732
  646.3 2.5 copy-start.15
  653.4 155.8 %reduce-scatter.10.cloned.1.call-start = ((), (), s32[]{:S(2)}) async-start(), calls=%async_computation.7 | async-start | bytes 2359296 | tf_op jit(solution)/shard_map/reduce_scatter | solution.py:1127
  660.5 214.2 %reduce-scatter.8.cloned.1.call-start = ((), (), s32[]{:S(2)}) async-start(), calls=%async_computation.6 | async-start | bytes 7077888 | tf_op jit(solution)/shard_map/reduce_scatter | solution.py:1135
  672.1 277.2 %reduce-scatter.14.cloned.1.call-start = ((), (), s32[]{:S(2)}) async-start(), calls=%async_computation.9 | async-start | bytes 9437184 | tf_op jit(solution)/shard_map/reduce_scatter | solution.py:1117
  672.6 351.7 %reduce-scatter.12.cloned.1.call-start = ((), (), s32[]{:S(2)}) async-start(), calls=%async_computation.8 | async-start | bytes 9437184 | tf_op jit(solution)/shard_map/reduce_scatter | solution.py:1120
  672.7 9.5 copy-start.2
  795.8 8.1 all-to-all-start
  (8 other events, 14.9 us)
Sparse Core Ops, SparseCore 0:
  653.5 110.0 reduce-scatter.15
  767.4 41.7 reduce-scatter.9
  812.9 61.7 reduce-scatter.7
  878.0 71.2 reduce-scatter.13
  953.0 71.2 reduce-scatter.11

commit v3 on v2

--- a/solution.py
+++ b/solution.py
@@ -12,24 +12,11 @@
 MASKED = -1e30
 
 
-def normalize(values):
-    return values * lax.rsqrt(jnp.mean(values * values, axis=-1, keepdims=True) + 1e-06)
-
-
-def modulate_rows(values, scale_part, shift_part):
-    return normalize(values) * (1.0 + scale_part) + shift_part
-
-
-def gelu_exact(values):
-    return jax.nn.gelu(values, approximate=False)
-
-
 def dot(a, b, dims=(((1,), (0,)), ((), ()))):
     return lax.dot_general(a, b, dims, preferred_element_type=jnp.float32)
 
 
 ROWS_ROWS = (((0,), (0,)), ((), ()))
-COLS_COLS = (((1,), (1,)), ((), ()))
 
 
 MESH = pl.DeviceIdType.MESH
@@ -126,6 +113,8 @@
         self.pieces = part.shape[1] // width
 
     def columns(self, c):
+        if isinstance(c, int):
+            return pl.ds(c * self.width, self.width)
         return pl.ds(pl.multiple_of(c * self.width, self.width), self.width)
 
     def copy(self, j, slot, c, step):
@@ -187,6 +176,26 @@
         def _():
             self.copy(i, n, c, -1).wait_recv()
             out[:, columns] += self.got[rows_of(n, self.rows), columns].astype(out.dtype)
+
+    def own_value(self, c):
+        i, n = self.i, self.n
+
+        @pl.when(i > 0)
+        def _():
+            self.copy(i, i, c, 1).wait_recv()
+
+        @pl.when(i < n - 1)
+        def _():
+            self.copy(i, n, c, -1).wait_recv()
+
+        return self.own_total(c)
+
+    def own_total(self, c):
+        i, n, columns = self.i, self.n, self.columns(c)
+        total = self.part[rows_of(i, self.rows), columns].astype(jnp.float32)
+        left = self.got[rows_of(i, self.rows), columns].astype(jnp.float32)
+        right = self.got[rows_of(n, self.rows), columns].astype(jnp.float32)
+        return total + jnp.where(i > 0, left, 0.0) + jnp.where(i < n - 1, right, 0.0)
 
     def all_sent(self):
         def one(j, carry):
@@ -227,90 +236,6 @@
         cost_estimate=pl.CostEstimate(flops=flops, bytes_accessed=1 << 20, transcendentals=0),
         name=name,
     )
-
-
-def gather_kernel(n, rows, count, *refs):
-    own, full = refs[:count], refs[count : 2 * count]
-    to_left, to_right, arrived, local = refs[2 * count :]
-    i = lax.axis_index("tensor")
-    copies = [
-        pltpu.make_async_copy(own[a], full[a].at[rows_of(i, rows)], local.at[a])
-        for a in range(count)
-    ]
-    for copy in copies:
-        copy.start()
-    greet_line(n, i)
-    lines = [
-        LineGather(n, i, rows, own[a], full[a], to_left.at[a], to_right.at[a], arrived.at[a])
-        for a in range(count)
-    ]
-    for line in lines:
-        line.start()
-        for s in range(1, n):
-            line.step(s)
-    for line in lines:
-        line.finish()
-    for copy in copies:
-        copy.wait()
-
-
-def gather_rows(n, arrays, collective_id):
-    count = len(arrays)
-    rows, width = arrays[0].shape
-    sems = [DMA((count, n))] * 3 + [DMA((count,))]
-    return call(
-        functools.partial(gather_kernel, n, rows, count),
-        collective_id,
-        "gather_rows",
-        [HBM] * count,
-        [jax.ShapeDtypeStruct((n * rows, width), a.dtype) for a in arrays],
-        [HBM] * count,
-        sems,
-    )(*arrays)
-
-
-def scatter_kernel(n, rows, width, parts_in, out, part, got, sent, arrived, local):
-    i = lax.axis_index("tensor")
-    copy = pltpu.make_async_copy(parts_in, part, local)
-    copy.start()
-    greet_line(n, i)
-    copy.wait()
-    line = LineScatter(n, i, rows, width, part, got, sent, arrived)
-    for t in range(n - 1, 0, -1):
-        for j in (t, n - 1 - t):
-            for c in range(line.pieces):
-                if j == t:
-                    pl.when(i == 0)(functools.partial(line.at_end, j, c))
-                else:
-                    pl.when(i == n - 1)(functools.partial(line.at_end, j, c))
-    for t in range(n - 1, 1, -1):
-        for near in (True, False):
-            for c in range(line.pieces):
-                line.pass_on(t, c, near)
-    for c in range(line.pieces):
-        line.own(c, out)
-    line.all_sent()
-
-
-def scatter_rows(n, parts, collective_id, pieces=4):
-    total, columns = parts.shape
-    rows = total // n
-    width = columns // pieces
-    return call(
-        functools.partial(scatter_kernel, n, rows, width),
-        collective_id,
-        "scatter_rows",
-        [HBM],
-        jax.ShapeDtypeStruct((rows, columns), jnp.float32),
-        VMEM,
-        [
-            pltpu.VMEM((total, columns), jnp.bfloat16),
-            pltpu.VMEM((total + rows, columns), jnp.bfloat16),
-            DMA((n, pieces)),
-            DMA((n + 1, pieces)),
-            DMA,
-        ],
-    )(parts)
 
 
 def ffn_kernel(
@@ -644,10 +569,10 @@
     merge_full,
     up_full,
     down_full,
+    noise_all,
     x_full,
     attend,
     merge,
-    noise_all,
     terms,
     terms_all,
     columns,
@@ -964,13 +889,13 @@
             sds((n * merge_w.shape[0], n_dp * merge_w.shape[1]), low),
             sds((n_dp * k_rows, up_w.shape[1]), low),
             sds((down_w.shape[0], n_dp * down_w.shape[1]), low),
+            sds((n_dp, 8, k_rows), f32),
         ],
-        [HBM] + [VMEM] * 9 + [HBM] * 4,
+        [HBM] + [VMEM] * 9 + [HBM] * 4 + [VMEM],
         [
             pltpu.VMEM((total, width), low),
             pltpu.VMEM((n_dp * k_rows, wide), low),
             pltpu.VMEM((n * merge_w.shape[0], n_dp * merge_w.shape[1]), low),
-            pltpu.VMEM((n_dp, 8, k_rows), f32),
             pltpu.VMEM((n_dp, 8, own_cols), f32),
             pltpu.VMEM((n_dp, 8, own_cols), f32),
             pltpu.VMEM((n * 8, own_cols), f32),
@@ -990,31 +915,716 @@
     )(x, cot, noise, mod_w, chosen, bias, attend_w, merge_w, up_w, down_w)
 
 
-def attention_backward(packed, grad_out, attended, lse, image_of, heads, score_scale):
-    tokens = packed.shape[0]
-    areas = lse.shape[0] // heads
-    split = packed.reshape(tokens, heads, 3, HEAD_DIM)
-    queries, keys, values = split[:, :, 0], split[:, :, 1], split[:, :, 2]
-    grads = grad_out.reshape(tokens, heads, HEAD_DIM)
-    logs = lse.reshape(areas, heads, -1).transpose(1, 0, 2).reshape(heads, tokens)
-    scores = (
-        jnp.einsum("qhd,khd->hqk", queries, keys, preferred_element_type=jnp.float32)
-        * score_scale
+class PlaneScatter:
+    def __init__(self, n_dp, d, theirs, own, swapped, landed, sems):
+        self.chips, self.d = n_dp // 2, d
+        self.chip, self.side = d // 2, lax.rem(d, 2)
+        self.theirs, self.own, self.swapped, self.landed, self.sems = theirs, own, swapped, landed, sems
+
+    def remote(self, source, target, sent, came, device):
+        return pltpu.make_async_remote_copy(
+            src_ref=source,
+            dst_ref=target,
+            send_sem=sent,
+            recv_sem=came,
+            device_id=(device, lax.axis_index("tensor")),
+            device_id_type=MESH,
+        )
+
+    def swap(self, m):
+        return self.remote(
+            self.theirs(m), self.swapped.at[m], self.sems.at[0, m], self.sems.at[1, m], self.d ^ 1
+        )
+
+    def send(self, m):
+        return self.remote(
+            self.own.at[m],
+            self.landed.at[self.chip],
+            self.sems.at[2, m],
+            self.sems.at[3, self.chip],
+            2 * m + self.side,
+        )
+
+    def come(self, m):
+        return self.remote(
+            self.own.at[m],
+            self.landed.at[m],
+            self.sems.at[2, m],
+            self.sems.at[3, m],
+            2 * m + self.side,
+        )
+
+    def keep(self):
+        return pltpu.make_async_copy(
+            self.own.at[self.chip], self.landed.at[self.chip], self.sems.at[2, self.chip]
+        )
+
+    def swap_all(self):
+        def one(m, carry):
+            self.swap(m).start()
+            return carry
+
+        lax.fori_loop(0, self.chips, one, 0)
+
+    def add_and_send(self):
+        _, height, wide = self.own.shape
+        chunk = math.gcd(height, 64 if wide > 512 else 256)
+
+        def one(k, carry):
+            m = self.chip ^ (self.chips - 1 - k)
+            self.swap(m).wait_recv()
+
+            def add(c, inner):
+                at = pl.ds(pl.multiple_of(c * chunk, chunk), chunk)
+                total = self.own[m, at, :].astype(jnp.float32) + self.swapped[m, at, :].astype(
+                    jnp.float32
+                )
+                self.own[m, at, :] = total.astype(self.own.dtype)
+                return inner
+
+            lax.fori_loop(0, height // chunk, add, 0)
+
+            @pl.when(m != self.chip)
+            def _():
+                self.send(m).start()
+
+            return carry
+
+        lax.fori_loop(0, self.chips, one, 0)
+        self.keep().start()
+
+    def landed_all(self):
+        for k in range(1, self.chips):
+            self.come(self.chip ^ k).wait_recv()
+        self.keep().wait()
+
+    def finish(self):
+        for m in range(self.chips):
+            self.swap(m).wait_send()
+        for k in range(1, self.chips):
+            self.send(self.chip ^ k).wait_send()
+
+
+def flows(n, pieces, sums, turn):
+    far, rest = turn // ((n - 2) * pieces), lax.rem(turn, (n - 2) * pieces)
+    t, c = n - 1 - rest // pieces, lax.rem(rest, pieces)
+    for near in (True, False):
+
+        @pl.when(far == (0 if near else 1))
+        def _():
+            sums.pass_on(t, c, near)
+
+
+def back_kernel(
+    n,
+    n_dp,
+    heads,
+    tile,
+    d_hidden,
+    cot,
+    middle,
+    attn_out,
+    table,
+    att_rows,
+    qkv,
+    lse,
+    bias,
+    mlp_hbm,
+    merge_hbm,
+    up_hbm,
+    down_hbm,
+    block_out,
+    d_middle,
+    d_qkv,
+    sums_out,
+    merge_grad,
+    up_landed,
+    down_landed,
+    part,
+    got,
+    merge,
+    d_att,
+    d_send,
+    d_attn,
+    d_keys,
+    d_values,
+    up_own,
+    up_swapped,
+    down_own,
+    down_swapped,
+    stage,
+    mlp_sent,
+    mlp_came,
+    up_sems,
+    down_sems,
+    att_sem,
+    merge_sem,
+    load_sem,
+    stage_sem,
+    own_sem,
+):
+    d, i = lax.axis_index("dp"), lax.axis_index("tensor")
+    rows, width = middle.shape
+    low, f32 = jnp.bfloat16, jnp.float32
+    head_cols = heads * HEAD_DIM
+    chips = n_dp // 2
+    k_rows, down_cols = up_own.shape[1], down_own.shape[2]
+    side = lax.rem(d, 2)
+
+    def up_slab(at):
+        return up_hbm.at[pl.ds(pl.multiple_of(at * k_rows, k_rows), k_rows), :]
+
+    def down_slab(at):
+        return down_hbm.at[:, pl.ds(pl.multiple_of(at * down_cols, down_cols), down_cols)]
+
+    load_mlp = pltpu.make_async_copy(mlp_hbm, part, load_sem.at[0])
+    load_mlp.start()
+
+    def load_merge(t, slot):
+        return pltpu.make_async_copy(
+            merge_hbm.at[pl.ds(pl.multiple_of(t * head_cols, head_cols), head_cols), :],
+            merge.at[slot],
+            merge_sem.at[slot],
+        )
+
+    load_merge(0, 0).start()
+    for m in range(chips):
+        pltpu.make_async_copy(up_slab(2 * m + side), up_own.at[m], own_sem.at[0, m]).start()
+        pltpu.make_async_copy(down_slab(2 * m + side), down_own.at[m], own_sem.at[1, m]).start()
+    greet_all(n, n_dp, d, i)
+    up = PlaneScatter(
+        n_dp, d, lambda m: up_slab(2 * m + 1 - side), up_own, up_swapped, up_landed, up_sems
     )
-    same_image = image_of[:, None] == image_of[None, :]
-    scores = jnp.where(same_image[None], scores, MASKED)
-    probs = jnp.exp(scores - logs[:, :, None])
-    grad_probs = jnp.einsum("qhd,khd->hqk", grads, values, preferred_element_type=jnp.float32)
-    inner = jnp.sum(probs * grad_probs, axis=-1, keepdims=True)
-    grad_scores = (probs * (grad_probs - inner)).astype(jnp.bfloat16)
-
-    def product(form, a, b):
-        return jnp.einsum(form, a, b, preferred_element_type=jnp.float32)
-
-    d_queries = product("hqk,khd->qhd", grad_scores, keys) * score_scale
-    d_keys = product("hqk,qhd->khd", grad_scores, queries) * score_scale
-    d_values = product("hqk,qhd->khd", probs.astype(jnp.bfloat16), grads)
-    return jnp.stack([d_queries, d_keys, d_values], axis=2).astype(jnp.bfloat16).reshape(tokens, -1)
+    down = PlaneScatter(
+        n_dp, d, lambda m: down_slab(2 * m + 1 - side), down_own, down_swapped, down_landed, down_sems
+    )
+    up.swap_all()
+    down.swap_all()
+    load_mlp.wait()
+    sums = LineScatter(n, i, rows, tile, part, got, mlp_sent, mlp_came)
+    pieces = sums.pieces
+
+    def ends(k, carry):
+        t, c = n - 1 - k // pieces, lax.rem(k, pieces)
+        pl.when(i == 0)(functools.partial(sums.at_end, t, c))
+        pl.when(i == n - 1)(functools.partial(sums.at_end, n - 1 - t, c))
+        return carry
+
+    lax.fori_loop(0, (n - 1) * pieces, ends, 0)
+
+    tiles = [slice(c * tile, (c + 1) * tile) for c in range(width // tile)]
+    squares = jnp.zeros((rows, 1), f32)
+    for at in tiles:
+        squares += jnp.sum(middle[:, at] * middle[:, at], axis=1, keepdims=True)
+    root = lax.rsqrt(squares * (1.0 / width) + 1e-06)
+    mean = jnp.zeros((rows, 1), f32)
+    for at in tiles:
+        v = middle[:, at] * root
+        dh = d_hidden[:, at]
+        mean += jnp.sum(dh * (1.0 + table[i, 4:5, at]) * v, axis=1, keepdims=True)
+        sums_out[3:4, at] = jnp.sum(dh, axis=0, keepdims=True)
+        sums_out[4:5, at] = jnp.sum(dh * v, axis=0, keepdims=True)
+    mean = mean * (1.0 / width)
+    for at in tiles:
+        v = middle[:, at] * root
+        u = d_hidden[:, at] * (1.0 + table[i, 4:5, at])
+        dm = cot[:, at].astype(f32) + root * (u - v * mean)
+        d_middle[:, at] = dm
+        d_attn[:, at] = (table[i, 2:3, at] * dm).astype(low)
+        sums_out[2:3, at] = jnp.sum(dm * attn_out[:, at], axis=0, keepdims=True)
+
+    def to_heads(t):
+        return pltpu.make_async_remote_copy(
+            src_ref=d_send.at[t],
+            dst_ref=d_att.at[rows_of(i, rows), :],
+            send_sem=att_sem.at[0, t],
+            recv_sem=att_sem.at[1, i],
+            device_id=(d, t),
+            device_id_type=MESH,
+        )
+
+    def from_rows(t):
+        return pltpu.make_async_remote_copy(
+            src_ref=d_send.at[t],
+            dst_ref=d_att.at[rows_of(t, rows), :],
+            send_sem=att_sem.at[0, t],
+            recv_sem=att_sem.at[1, t],
+            device_id=(d, t),
+            device_id_type=MESH,
+        )
+
+    def head_part(t, carry):
+        slot = lax.rem(t, 2)
+
+        @pl.when(t + 1 < n)
+        def _():
+            load_merge(t + 1, 1 - slot).start()
+
+        load_merge(t, slot).wait()
+        d_send[t] = mm_nt(d_attn[...], merge[slot]).astype(low)
+
+        @pl.when(t != i)
+        def _():
+            to_heads(t).start()
+
+        return carry
+
+    lax.fori_loop(0, n, head_part, 0)
+    d_att[rows_of(i, rows), :] = d_send[i]
+    for m in range(chips):
+        pltpu.make_async_copy(up_slab(2 * m + side), up_own.at[m], own_sem.at[0, m]).wait()
+        pltpu.make_async_copy(down_slab(2 * m + side), down_own.at[m], own_sem.at[1, m]).wait()
+    up.add_and_send()
+
+    wide = width // tile
+
+    def square(row, column):
+        return merge_grad.at[
+            pl.ds(pl.multiple_of(row * tile, tile), tile),
+            pl.ds(pl.multiple_of(column * tile, tile), tile),
+        ]
+
+    def merge_one(k, carry):
+        row, column = k // wide, lax.rem(k, wide)
+        slot = lax.rem(k, 2)
+
+        @pl.when(k >= 2)
+        def _():
+            pltpu.make_async_copy(stage.at[slot], square(0, 0), stage_sem.at[slot]).wait()
+
+        a = att_rows[:, pl.ds(pl.multiple_of(row * tile, tile), tile)]
+        b = d_attn[:, pl.ds(pl.multiple_of(column * tile, tile), tile)]
+        stage[slot] = mm_tn(a, b).astype(low)
+        pltpu.make_async_copy(stage.at[slot], square(row, column), stage_sem.at[slot]).start()
+        return carry
+
+    lax.fori_loop(0, wide * wide, merge_one, 0)
+    for slot in range(2):
+        pltpu.make_async_copy(stage.at[slot], square(0, 0), stage_sem.at[slot]).wait()
+    for turn in range(1, n):
+        from_rows(lax.rem(i + turn, n)).wait_recv()
+
+    area = lse.shape[1]
+    areas = n * rows // area
+    d_keys[...] = jnp.zeros_like(d_keys)
+    d_values[...] = jnp.zeros_like(d_values)
+    turns = 2 * max(n - 2, 0) * pieces
+    per_area = -(-turns // areas)
+    scale = HEAD_DIM ** (-0.5)
+
+    def back_area(here_at, carry):
+        here = rows_of(here_at, area)
+        for h in range(heads):
+            first = h * 3 * HEAD_DIM
+            head = slice(h * HEAD_DIM, (h + 1) * HEAD_DIM)
+            q = qkv[here, first : first + HEAD_DIM]
+            g = d_att[here, head]
+            log_row = lse[pl.ds(here_at * heads + h, 1), :]
+            probs, d_probs = [], []
+            inner = jnp.zeros((1, area), f32)
+            for b in range(areas):
+                key = qkv[b * area : (b + 1) * area, first + HEAD_DIM : first + 2 * HEAD_DIM]
+                value = qkv[b * area : (b + 1) * area, first + 2 * HEAD_DIM : first + 3 * HEAD_DIM]
+                scores = mm_nt(key, q) * scale + bias[here_at, b]
+                probs.append(jnp.exp(scores - log_row))
+                d_probs.append(mm_nt(value, g))
+                inner += jnp.sum(probs[b] * d_probs[b], axis=0, keepdims=True)
+            d_query = jnp.zeros((HEAD_DIM, area), f32)
+            for b in range(areas):
+                at = slice(b * area, (b + 1) * area)
+                key = qkv[at, first + HEAD_DIM : first + 2 * HEAD_DIM]
+                d_scores = (probs[b] * (d_probs[b] - inner)).astype(low)
+                d_values[at, head] += mm(probs[b].astype(low), g)
+                d_keys[at, head] += mm(d_scores, q)
+                d_query += mm_tn(key, d_scores)
+            d_qkv[here, first : first + HEAD_DIM] = (d_query * scale).T.astype(low)
+
+        @pl.when(here_at == 0)
+        def _():
+            down.add_and_send()
+
+        for extra in range(per_area):
+            turn = here_at * per_area + extra
+
+            @pl.when(turn < turns)
+            def _():
+                flows(n, pieces, sums, turn)
+
+        return carry
+
+    lax.fori_loop(0, areas, back_area, 0)
+    for h in range(heads):
+        first = h * 3 * HEAD_DIM
+        head = slice(h * HEAD_DIM, (h + 1) * HEAD_DIM)
+        d_qkv[:, first + HEAD_DIM : first + 2 * HEAD_DIM] = (d_keys[:, head] * scale).astype(low)
+        d_qkv[:, first + 2 * HEAD_DIM : first + 3 * HEAD_DIM] = d_values[:, head].astype(low)
+    for c, at in enumerate(tiles):
+        total = sums.own_value(c)
+        block_out[:, at] = (middle[:, at] + table[i, 5:6, at] * total).astype(low)
+        sums_out[5:6, at] = jnp.sum(cot[:, at].astype(f32) * total, axis=0, keepdims=True)
+    sums_out[0:2, :] = jnp.zeros((2, width), f32)
+    sums_out[6:8, :] = jnp.zeros((2, width), f32)
+    for scatter in (up, down):
+        scatter.landed_all()
+        scatter.finish()
+    for turn in range(1, n):
+        to_heads(lax.rem(i + turn, n)).wait_send()
+    sums.all_sent()
+
+
+def back(n, n_dp, operands, shapes, number, tile=512):
+    (rows, width), wide, units, k_rows, down_cols, areas = shapes
+    heads = wide // (3 * HEAD_DIM)
+    total, chips, pieces = n * rows, n_dp // 2, width // tile
+    low, f32 = jnp.bfloat16, jnp.float32
+    sds = jax.ShapeDtypeStruct
+    return call(
+        functools.partial(back_kernel, n, n_dp, heads, tile),
+        number,
+        "back",
+        [VMEM] * 8 + [pl.BlockSpec(memory_space=pltpu.SMEM)] + [HBM] * 4,
+        [
+            sds((rows, width), low),
+            sds((rows, width), f32),
+            sds((total, wide), low),
+            sds((8, width), f32),
+            sds((width, width), low),
+            sds((chips, k_rows, units), low),
+            sds((chips, units, down_cols), low),
+        ],
+        [VMEM] * 4 + [HBM] * 3,
+        [
+            pltpu.VMEM((total, width), low),
+            pltpu.VMEM((total + rows, width), low),
+            pltpu.VMEM((2, heads * HEAD_DIM, width), low),
+            pltpu.VMEM((total, heads * HEAD_DIM), low),
+            pltpu.VMEM((n, rows, heads * HEAD_DIM), low),
+            pltpu.VMEM((rows, width), low),
+            pltpu.VMEM((total, heads * HEAD_DIM), f32),
+            pltpu.VMEM((total, heads * HEAD_DIM), f32),
+            pltpu.VMEM((chips, k_rows, units), low),
+            pltpu.VMEM((chips, k_rows, units), low),
+            pltpu.VMEM((chips, units, down_cols), low),
+            pltpu.VMEM((chips, units, down_cols), low),
+            pltpu.VMEM((2, tile, tile), low),
+            DMA((n, pieces)),
+            DMA((n + 1, pieces)),
+            DMA((4, chips)),
+            DMA((4, chips)),
+            DMA((2, n)),
+            DMA((2,)),
+            DMA((1,)),
+            DMA((2,)),
+            DMA((2, chips)),
+        ],
+        flops=20 * total * total * wide // 3,
+    )(*operands)
+
+
+def last_kernel(
+    n,
+    n_dp,
+    tile,
+    d_qkv,
+    hidden,
+    x_own,
+    d_middle,
+    sums_in,
+    table,
+    chosen,
+    mod_w,
+    merge_hbm,
+    attend_hbm,
+    input_grad,
+    d_mod_all,
+    noise_sum,
+    attend_landed,
+    merge_out,
+    attend,
+    part,
+    got,
+    grad_own,
+    grad_theirs,
+    grad_swapped,
+    merge_own,
+    merge_swapped,
+    merge_landed,
+    merge_part,
+    merge_got,
+    sums_all,
+    shares,
+    shares_all,
+    terms,
+    terms_all,
+    noise_parts,
+    sent,
+    came,
+    merge_sent,
+    merge_came,
+    grad_sems,
+    merge_sems,
+    share_sem,
+    mod_sem,
+    term_sem,
+    noise_sem,
+    load_sem,
+    own_sem,
+):
+    d, i = lax.axis_index("dp"), lax.axis_index("tensor")
+    rows, width = x_own.shape
+    low, f32 = jnp.bfloat16, jnp.float32
+    chips = n_dp // 2
+    side = lax.rem(d, 2)
+    k_rows, own_cols = mod_w.shape
+    merge_cols = merge_own.shape[2]
+    merge_rows = merge_out.shape[0]
+
+    def merge_slab(at):
+        return merge_hbm.at[:, pl.ds(pl.multiple_of(at * merge_cols, merge_cols), merge_cols)]
+
+    load = pltpu.make_async_copy(attend_hbm, attend, load_sem)
+    load.start()
+    for m in range(chips):
+        pltpu.make_async_copy(merge_slab(2 * m + side), merge_own.at[m], own_sem.at[m]).start()
+    greet_all(n, n_dp, d, i)
+    merge = PlaneScatter(
+        n_dp,
+        d,
+        lambda m: merge_slab(2 * m + 1 - side),
+        merge_own,
+        merge_swapped,
+        merge_landed,
+        merge_sems,
+    )
+    grad = PlaneScatter(
+        n_dp, d, lambda m: grad_theirs.at[m], grad_own, grad_swapped, attend_landed, grad_sems
+    )
+    merge.swap_all()
+    sums = LineScatter(n, i, rows, tile, part, got, sent, came)
+    pieces = sums.pieces
+    load.wait()
+
+    def partial_block(q, carry):
+        j = jnp.where(2 * i < n - 1, n - 1 - q, q)
+        here = rows_of(j, rows)
+
+        def one(c, inner):
+            at = pl.ds(pl.multiple_of(c * tile, tile), tile)
+            part[here, at] = mm_nt(d_qkv[here, :], attend[at, :]).astype(low)
+            sums.at_end(j, c)
+            return inner
+
+        lax.fori_loop(0, pieces, one, 0)
+        return carry
+
+    lax.fori_loop(0, n, partial_block, 0)
+    for m in range(chips):
+        pltpu.make_async_copy(merge_slab(2 * m + side), merge_own.at[m], own_sem.at[m]).wait()
+    merge.add_and_send()
+
+    def slab_grad(at):
+        columns = pl.ds(pl.multiple_of(at * k_rows, k_rows), k_rows)
+        return mm_tn(hidden[:, columns], d_qkv[...]).astype(low)
+
+    def for_them(m, carry):
+        grad_theirs[m] = slab_grad(2 * m + 1 - side)
+        grad.swap(m).start()
+        return carry
+
+    def for_us(m, carry):
+        grad_own[m] = slab_grad(2 * m + side)
+        return carry
+
+    lax.fori_loop(0, chips, for_them, 0)
+    lax.fori_loop(0, chips, for_us, 0)
+    grad.add_and_send()
+    turns = 2 * max(n - 2, 0) * pieces
+
+    def pass_by(turn, carry):
+        flows(n, pieces, sums, turn)
+        return carry
+
+    lax.fori_loop(0, turns, pass_by, 0)
+
+    merge.landed_all()
+    merge_sums = LineScatter(
+        n, i, merge_rows, merge_cols, merge_part, merge_got, merge_sent, merge_came
+    )
+
+    def merge_block(q, carry):
+        j = jnp.where(2 * i < n - 1, n - 1 - q, q)
+        here = rows_of(j, merge_rows)
+        total = merge_landed[0, here, :].astype(f32)
+        for m in range(1, chips):
+            total += merge_landed[m, here, :].astype(f32)
+        merge_part[here, :] = total.astype(low)
+        merge_sums.at_end(j, 0)
+        return carry
+
+    lax.fori_loop(0, n, merge_block, 0)
+
+    tiles = [slice(c * tile, (c + 1) * tile) for c in range(width // tile)]
+    squares = jnp.zeros((rows, 1), f32)
+    for at in tiles:
+        v = x_own[:, at].astype(f32)
+        squares += jnp.sum(v * v, axis=1, keepdims=True)
+    root = lax.rsqrt(squares * (1.0 / width) + 1e-06)
+    mean = jnp.zeros((rows, 1), f32)
+    sums_all[...] = sums_in[...]
+    for c, at in enumerate(tiles):
+        v = x_own[:, at].astype(f32) * root
+        dh = sums.own_value(c)
+        mean += jnp.sum(dh * (1.0 + table[i, 1:2, at]) * v, axis=1, keepdims=True)
+        sums_all[0:1, at] = jnp.sum(dh, axis=0, keepdims=True)
+        sums_all[1:2, at] = jnp.sum(dh * v, axis=0, keepdims=True)
+
+    unit = math.gcd(width, own_cols)
+    for number in range(6):
+        for start in range(0, width, unit):
+            at = number * width + start
+            shares[at // own_cols, :, at % own_cols : at % own_cols + unit] = (
+                chosen[i][:, :1] * sums_all[number : number + 1, start : start + unit]
+            )
+
+    def to_line(source, target, sems, turn, whole=False):
+        t = lax.rem(i + turn, n)
+        return pltpu.make_async_remote_copy(
+            src_ref=source if whole else source.at[t],
+            dst_ref=target.at[i],
+            send_sem=sems.at[0, t],
+            recv_sem=sems.at[1, i],
+            device_id=(d, t),
+            device_id_type=MESH,
+        )
+
+    def from_line(source, target, sems, turn, whole=False):
+        t = lax.rem(i + turn, n)
+        return pltpu.make_async_remote_copy(
+            src_ref=source if whole else source.at[t],
+            dst_ref=target.at[t],
+            send_sem=sems.at[0, t],
+            recv_sem=sems.at[1, t],
+            device_id=(d, t),
+            device_id_type=MESH,
+        )
+
+    def to_plane(source, target, sems, flip):
+        return pltpu.make_async_remote_copy(
+            src_ref=source,
+            dst_ref=target.at[d],
+            send_sem=sems.at[0, flip],
+            recv_sem=sems.at[1, flip],
+            device_id=(d ^ flip, i),
+            device_id_type=MESH,
+        )
+
+    def from_plane(source, target, sems, flip):
+        return pltpu.make_async_remote_copy(
+            src_ref=source,
+            dst_ref=target.at[d ^ flip],
+            send_sem=sems.at[0, flip],
+            recv_sem=sems.at[1, flip],
+            device_id=(d ^ flip, i),
+            device_id_type=MESH,
+        )
+
+    for turn in range(1, n):
+        to_line(shares, shares_all, share_sem, turn).start()
+    mean = mean * (1.0 / width)
+    for c, at in enumerate(tiles):
+        v = x_own[:, at].astype(f32) * root
+        u = sums.own_total(c) * (1.0 + table[i, 1:2, at])
+        input_grad[:, at] = (d_middle[:, at] + root * (u - v * mean)).astype(low)
+    shares_all[i] = shares[i]
+    for turn in range(1, n):
+        from_line(shares, shares_all, share_sem, turn).wait_recv()
+    d_mod_all[d] = jnp.sum(shares_all[...], axis=0).astype(low).astype(f32)
+    own_mod = d_mod_all.at[d]
+    for flip in range(1, n_dp):
+        to_plane(own_mod, d_mod_all, mod_sem, flip).start()
+    for t in range(n - 1, 1, -1):
+        for near in (True, False):
+            merge_sums.pass_on(t, 0, near)
+    for flip in range(1, n_dp):
+        from_plane(own_mod, d_mod_all, mod_sem, flip).wait_recv()
+    flat = d_mod_all[...].reshape(n_dp * 8, own_cols).astype(low)
+    terms[...] = mm_nt(flat, mod_w[...]).reshape(n_dp, 8, k_rows)
+    for turn in range(1, n):
+        to_line(terms, terms_all, term_sem, turn, True).start()
+    terms_all[i] = terms[...]
+    for turn in range(1, n):
+        from_line(terms, terms_all, term_sem, turn, True).wait_recv()
+    noise_parts[...] = jnp.sum(terms_all[...], axis=0)
+    for flip in range(1, n_dp):
+        to_plane(noise_parts.at[d ^ flip], noise_sum, noise_sem, flip).start()
+    noise_sum[d] = noise_parts[d]
+    merge_out[...] = merge_sums.own_value(0)
+    for flip in range(1, n_dp):
+        from_plane(noise_parts.at[d ^ flip], noise_sum, noise_sem, flip).wait_recv()
+    grad.landed_all()
+    grad.finish()
+    merge.finish()
+    for turn in range(1, n):
+        to_line(shares, shares_all, share_sem, turn).wait_send()
+        to_line(terms, terms_all, term_sem, turn, True).wait_send()
+    for flip in range(1, n_dp):
+        to_plane(own_mod, d_mod_all, mod_sem, flip).wait_send()
+        to_plane(noise_parts.at[d ^ flip], noise_sum, noise_sem, flip).wait_send()
+    sums.all_sent()
+    merge_sums.all_sent()
+
+
+def last(n, n_dp, operands, shapes, number, tile=512):
+    (rows, width), wide, k_rows, own_cols, (merge_rows, merge_cols) = shapes
+    total, chips, pieces = n * rows, n_dp // 2, width // tile
+    low, f32 = jnp.bfloat16, jnp.float32
+    sds = jax.ShapeDtypeStruct
+    return call(
+        functools.partial(last_kernel, n, n_dp, tile),
+        number,
+        "last",
+        [VMEM] * 8 + [HBM] * 2,
+        [
+            sds((rows, width), low),
+            sds((n_dp, 8, own_cols), f32),
+            sds((n_dp, 8, k_rows), f32),
+            sds((chips, k_rows, wide), low),
+            sds((merge_rows, merge_cols), f32),
+        ],
+        [VMEM] * 3 + [HBM] + [VMEM],
+        [
+            pltpu.VMEM((width, wide), low),
+            pltpu.VMEM((total, width), low),
+            pltpu.VMEM((total + rows, width), low),
+            pltpu.VMEM((chips, k_rows, wide), low),
+            pltpu.VMEM((chips, k_rows, wide), low),
+            pltpu.VMEM((chips, k_rows, wide), low),
+            pltpu.VMEM((chips, n * merge_rows, merge_cols), low),
+            pltpu.VMEM((chips, n * merge_rows, merge_cols), low),
+            pltpu.VMEM((chips, n * merge_rows, merge_cols), low),
+            pltpu.VMEM((n * merge_rows, merge_cols), low),
+            pltpu.VMEM(((n + 1) * merge_rows, merge_cols), low),
+            pltpu.VMEM((8, width), f32),
+            pltpu.VMEM((n, 8, own_cols), f32),
+            pltpu.VMEM((n, 8, own_cols), f32),
+            pltpu.VMEM((n_dp, 8, k_rows), f32),
+            pltpu.VMEM((n, n_dp, 8, k_rows), f32),
+            pltpu.VMEM((n_dp, 8, k_rows), f32),
+            DMA((n, pieces)),
+            DMA((n + 1, pieces)),
+            DMA((n, 1)),
+            DMA((n + 1, 1)),
+            DMA((4, chips)),
+            DMA((4, chips)),
+            DMA((2, n)),
+            DMA((2, n_dp)),
+            DMA((2, n)),
+            DMA((2, n_dp)),
+            DMA,
+            DMA((chips,)),
+        ],
+        flops=4 * total * width * wide,
+    )(*operands)
 
 
 def on_device(
@@ -1030,8 +1640,6 @@
 ):
     n = lax.axis_size("tensor")
     n_dp = lax.axis_size("dp")
-    place = lax.axis_index("tensor")
-    dp_place = lax.axis_index("dp")
     rows, width = block_input.shape
     tokens = n * rows
     images = image_sizes.shape[1]
@@ -1043,7 +1651,6 @@
     def image_at(places):
         return sum((places >= end).astype(jnp.int32) for end in ends)
 
-    image_of = image_at(jnp.arange(tokens, dtype=jnp.int32))
     block_images = image_at(jnp.arange(n, dtype=jnp.int32) * rows)
     chosen = (block_images[:, None] == jnp.arange(8, dtype=jnp.int32)[None, :]) & (
         jnp.arange(8) < images
@@ -1055,15 +1662,12 @@
     noise_low = jax.nn.silu(noise_embed.astype(jnp.float32)).astype(jnp.bfloat16)
     noise_slabs = noise_low.astype(jnp.float32).reshape(images, n_dp, k_rows).transpose(1, 0, 2)
     noise_slabs = jnp.pad(noise_slabs, ((0, 0), (0, 8 - images), (0, 0)))
-    noise_low_cols = lax.dynamic_slice_in_dim(
-        lax.all_gather(noise_low, "dp", axis=0, tiled=True), dp_place * k_rows, k_rows, 1
-    )
     (
         cot_full,
         hidden_first,
         packed,
         lse,
-        attended,
+        _,
         att_rows,
         attn_out,
         middle,
@@ -1073,6 +1677,7 @@
         merge_full,
         up_full,
         down_full,
+        noise_all,
     ) = front(
         n,
         n_dp,
@@ -1088,82 +1693,69 @@
         down_weight,
         0,
     )
-    heads_local = packed.shape[1] // (3 * HEAD_DIM)
-    score_scale = HEAD_DIM ** (-0.5)
-    own_table = lax.dynamic_index_in_dim(table, place, 0, keepdims=False)
-    shift_first, scale_first, gate_first, shift_second, scale_second, gate_second = [
-        own_table[number : number + 1] for number in range(6)
-    ]
-    inputs = block_input.astype(jnp.float32)
-    grad_rows = cotangent.astype(jnp.float32)
-    own_image = lax.dynamic_index_in_dim(block_images, place, 0, keepdims=False)
-
-    def rows_back(values, scale_part):
-        return jax.vjp(modulate_rows, values, jnp.broadcast_to(scale_part, values.shape), jnp.zeros_like(values))[1]
-
-    back_first = rows_back(inputs, scale_first)
-    back_second = rows_back(middle, scale_second)
     d_hidden_second, mlp_part, up_local, down_local = ffn(
-        n, hidden_second, table, cot_full, up_full, down_full, 2
+        n, hidden_second, table, cot_full, up_full, down_full, 1
     )
-    mlp_out = scatter_rows(n, mlp_part, 3)
-    block_output = (middle + gate_second * mlp_out).astype(jnp.bfloat16)
-    d_gate_second = grad_rows * mlp_out
-    d_mid_norm, d_scale_second, d_shift_second = back_second(d_hidden_second)
-    d_middle = grad_rows + d_mid_norm
-    d_gate_first = d_middle * attn_out
-    d_attn = gather_rows(n, [(gate_first * d_middle).astype(jnp.bfloat16)], 4)[0]
-
-    down_part = lax.psum_scatter(
-        down_local, "dp", scatter_dimension=1, tiled=True
-    ).astype(jnp.float32)
-    up_part = lax.psum_scatter(
-        up_local, "dp", scatter_dimension=0, tiled=True
-    ).astype(jnp.float32)
-
-    own_heads = heads_local * HEAD_DIM
-    merge_own = lax.dynamic_slice_in_dim(merge_full, place * own_heads, own_heads, 0)
-    merge_local = dot(attended, d_attn, ROWS_ROWS)
-    merge_part = lax.psum_scatter(
-        merge_local.astype(jnp.bfloat16), "dp", scatter_dimension=1, tiled=True
-    ).astype(jnp.float32)
-    d_attended = dot(d_attn, merge_own, COLS_COLS).astype(jnp.bfloat16)
-    d_qkv = attention_backward(
-        packed, d_attended, attended, lse, image_of, heads_local, score_scale
+    units = up_full.shape[1]
+    wide = packed.shape[1]
+    (
+        block_output,
+        d_middle,
+        d_qkv,
+        row_sums,
+        merge_local,
+        up_landed,
+        down_landed,
+    ) = back(
+        n,
+        n_dp,
+        (
+            d_hidden_second,
+            cotangent,
+            middle,
+            attn_out,
+            table,
+            att_rows,
+            packed,
+            lse,
+            bias,
+            mlp_part,
+            merge_full,
+            up_local,
+            down_local,
+        ),
+        (block_input.shape, wide, units, k_rows, down_weight.shape[1], bias.shape[0]),
+        2,
     )
-    attend_local = dot(hidden_first, d_qkv, ROWS_ROWS)
-    attend_part = lax.psum_scatter(
-        attend_local.astype(jnp.bfloat16), "dp", scatter_dimension=0, tiled=True
-    ).astype(jnp.float32)
-    d_hidden_first = scatter_rows(
-        n, dot(d_qkv, attend_full, COLS_COLS).astype(jnp.bfloat16), 5
+    input_grad, d_mod_all, noise_sums, attend_landed, merge_part = last(
+        n,
+        n_dp,
+        (
+            d_qkv,
+            hidden_first,
+            block_input,
+            d_middle,
+            row_sums,
+            table,
+            chosen,
+            modulate_weight,
+            merge_local,
+            attend_full,
+        ),
+        (block_input.shape, wide, k_rows, modulate_weight.shape[1], merge_weight.shape),
+        3,
     )
-    d_in_norm, d_scale_first, d_shift_first = back_first(d_hidden_first)
-    input_grad = (d_middle + d_in_norm).astype(jnp.bfloat16)
-
-    token_grads = [
-        d_shift_first,
-        d_scale_first,
-        d_gate_first,
-        d_shift_second,
-        d_scale_second,
-        d_gate_second,
-    ]
-    image_rows = [
-        jnp.concatenate(
-            [jnp.where(own_image == j, jnp.sum(part, axis=0, keepdims=True), 0.0) for part in token_grads], axis=1
-        )
-        for j in range(images)
-    ]
-    d_mod_terms = jnp.concatenate(image_rows, axis=0)
-    d_mod_cols = lax.psum_scatter(
-        d_mod_terms, "tensor", scatter_dimension=1, tiled=True
-    ).astype(jnp.bfloat16)
-    d_mod_all = lax.all_gather(d_mod_cols, "dp", axis=0, tiled=True)
-    modulate_part = dot(noise_low_cols, d_mod_all, ROWS_ROWS)
-    noise_terms = dot(d_mod_all, modulate_weight, COLS_COLS)
-    noise_cols = lax.psum(noise_terms, "tensor")
-    noise_sum = lax.all_to_all(noise_cols, "dp", split_axis=0, concat_axis=1, tiled=True)
+
+    def chip_sum(landed):
+        return jnp.sum(landed.astype(jnp.float32), axis=0)
+
+    up_part, down_part, attend_part = map(chip_sum, (up_landed, down_landed, attend_landed))
+    modulate_part = dot(
+        noise_all.reshape(n_dp * 8, k_rows).astype(jnp.bfloat16),
+        d_mod_all.reshape(n_dp * 8, -1).astype(jnp.bfloat16),
+        ROWS_ROWS,
+    )
+    noise_sum = noise_sums[:, :images].transpose(1, 0, 2).reshape(images, width)
     silu_back = jax.vjp(jax.nn.silu, noise_embed.astype(jnp.float32))[1]
     noise_grad = silu_back(noise_sum)[0]
     return (

time: 1040 us -> 622 us (0.60)
  waiting for transfers between devices: 295 us -> 0 us
  matrix products: 79.9 us -> 2.27 us
  Pallas kernels: 536 us -> 598 us
  blocking collectives: 36.9 us -> 0 us
  other arithmetic: 45.3 us -> 11.2 us
  between operations: 19.6 us -> 3.31 us
  local copies, waits for them, and re-layouts: 17.8 us -> 6.65 us
    reduce_scatter x4 -> x0, waiting for transfers between devices: 213 us -> none  [the longest x1 72.3 us: on_device(): lax.psum_scatter(up_local, 'dp', scatter_dimension=0, tiled=True)]
    unnamed x6 -> x0, waiting for transfers between devices: 79.3 us -> none
    pallas_call x3 -> x2, Pallas kernels: 207 us -> 269 us  [the longest x1 135 us: last(): call(functools.partial(last_kernel, n, n_dp, tile), number, 'last', [VMEM...]
    dot_general x5 -> x0, matrix products: 43.4 us -> none  [the longest x3 19.3 us: product(): return jnp.einsum(form, a, b, preferred_element_type=jnp.float32)]
    dot_general x6 -> x1, matrix products: 36.5 us -> 2.27 us  [dot(): return lax.dot_general(a, b, dims, preferred_element_type=jnp.float32)]
    convert_element_type x7 -> x0, other arithmetic: 24.6 us -> none  [the longest x1 10.6 us: attention_backward(): grad_scores = (probs * (grad_probs - inner)).astype(jnp.bfloat16)]
    psum x1 -> x0, blocking collectives: 19.1 us -> none  [on_device(): noise_cols = lax.psum(noise_terms, 'tensor')]
    all_gather x2 -> x0, blocking collectives: 17.9 us -> none  [the longest x1 9.21 us: on_device(): d_mod_all = lax.all_gather(d_mod_cols, 'dp', axis=0, tiled=True)]
  transfers between devices with their start and end apart: 6 -> 0, of which waited for: 6 -> 0; matrix products, arithmetic and copies ran while one was open for 3% -> 0% of each run, Pallas kernels for 0% -> 0%
where the time goes in v3:
time: 622 us
  Pallas kernels  598 us (96%)
  other arithmetic  11.2 us (2%)
  local copies, waits for them, and re-layouts  6.65 us (1%)
    pallas_call x1, Pallas kernels, front(): call(functools.partial(front_kernel, n, n_dp, heads, 512), number, 'front...  199 us
    pallas_call x1, Pallas kernels, last(): call(functools.partial(last_kernel, n, n_dp, tile), number, 'last', [VMEM...  135 us
    pallas_call x1, Pallas kernels, back(): call(functools.partial(back_kernel, n, n_dp, heads, tile), number, 'back'...  134 us
    pallas_call x1, Pallas kernels, ffn(): call(functools.partial(ffn_kernel, n, tile, grad_tile), collective_id, 'f...  130 us

profile of v3, /device:TPU:0, one launch (start us, length us, event | category | flops | bytes accessed | tf_op | source)
XLA Modules:
  0.0 621.7 jit_solution(5977593529248586160)
XLA Ops:
  0.6 1.4 fusion.13
  4.6 0.7 fusion.12
  5.3 0.1 fusion.9
  5.4 0.6 compare_select_fusion.bias
  6.0 0.7 broadcast_in_dim.8.chosen
  6.7 0.7 fusion.4
  7.4 0.6 pad_convert_fusion.noise
  8.1 199.0 %front.1 = (bf16[1024,2048]{1,0:T(8,128)(2,1)}, bf16[1024,2048]{1,0:T(8,128)(2,1)}, bf16[1024,1536]{1,0:T(8,128)(2,1)}, f32[16,256]{1,0:T(8,128)}, bf16[1024,512...) custom-call(bf16[256,2048]{1,0:T(8,128)(2,1)} %x_own.3, ...), custom_call_target="tpu_custom_call" | custom-call | flops 6442450944 | bytes 1048576 | tf_op jit(solution)/shard_map/front/pallas_call | solution.py:872
  207.1 130.4 %ffn.1 = (f32[256,2048]{1,0:T(8,128)}, bf16[1024,2048]{1,0:T(8,128)(2,1)}, bf16[2048,2048]{1,0:T(8,128)(2,1)}, bf16[2048,2048]{1,0:T(8,128)(2,1)}) custom-call(bf16[256,2048]{1,0:T(8,128)(2,1)} %get-tuple-element.38.own_hidden, f32[4,8,2048]{2,1,0:T(8,128)} %get-tuple-element.39.table, bf16[1024,2048]{1,0:T(8,128)(2,1)} %get-tuple-element.40.d_mlp_hbm, ...), custom_call_target="tpu_custom_call" | custom-call | flops 51539607552 | bytes 1048576 | tf_op jit(solution)/shard_map/ffn/pallas_call | solution.py:411
  337.5 133.6 %back.1 = (bf16[256,2048]{1,0:T(8,128)(2,1)}, f32[256,2048]{1,0:T(8,128)}, bf16[1024,1536]{1,0:T(8,128)(2,1)}, f32[8,2048]{1,0:T(8,128)}, bf16[2048,2048]{1,0:T(...) custom-call(f32[256,2048]{1,0:T(8,128)} %get-tuple-element.43.d_hidden, bf16[256,2048]{1,0:T(8,128)(2,1)} %cot.1, ...), custom_call_target="tpu_custom_call" | custom-call | flops 10737418240 | bytes 1048576 | tf_op jit(solution)/shard_map/back/pallas_call | solution.py:1281
  471.1 0.0 copy-start.5
  471.1 135.3 %last.1 = (bf16[256,2048]{1,0:T(8,128)(2,1)}, f32[8,8,3072]{2,1,0:T(8,128)}, f32[8,8,256]{2,1,0:T(8,128)}, bf16[4,256,1536]{2,1,0:T(8,128)(2,1)}, f32[512,256]{1,0:T(8,128)}) custom-call(bf16[1024,1536]{1,0:T(8,128)(2,1)} %get-tuple-element.54.d_qkv, bf16[1024,2048]{1,0:T(8,128)(2,1)} %get-tuple-element.55.hidden, bf16[256,2048]{1,0:T(8,128)(2,1)} %x_own.3, ...), custom_call_target="tpu_custom_call" | custom-call | flops 12884901888 | bytes 1048576 | tf_op jit(solution)/shard_map/last/pallas_call | solution.py:1582
  606.4 1.0 slice.29
  607.4 0.7 fusion.6
  608.0 3.6 convert_reduce_fusion.2
  611.7 2.1 convert_reduce_fusion.1
  613.8 0.8 copy-done
  614.6 2.0 convert_reduce_fusion
  616.7 0.0 copy-done.6
  616.7 2.3 convolution_bitcast_fusion
  618.9 0.0 copy-done.2
  618.9 1.0 copy.20
  619.9 1.0 copy.21
  620.9 0.8 copy.22
  (13 shorter events, 0.0 us)
Async XLA Ops:
  471.1 136.3 %copy-start.5 = (bf16[4,2048]{1,0:T(4,128)(2,1)S(1)}, bf16[4,2048]{1,0:T(4,128)(2,1)}, u32[]{:S(2)}) copy-start(bf16[4,2048]{1,0:T(4,128)(2,1)} %param.11) | copy-start | bytes 49156
  606.4 5.3 copy-start.1
  611.7 2.9 copy-start
  614.6 2.0 copy-start.6
  614.6 2.0 copy-start.7
  616.7 2.3 copy-start.2
  616.7 3.3 copy-start.3
  618.9 1.9 copy-start.4

commit v4 on v3

--- a/solution.py
+++ b/solution.py
@@ -665,44 +665,65 @@
         n, i, rows, cot_own, cot_full, cot_sem.at[0], cot_sem.at[1], cot_sem.at[2]
     )
     x_line.start()
-    attend_g.start()
-    merge_line.start()
     noise_all[d] = noise[d]
     x_full[rows_of(i, rows), :] = x_own[...]
     for flip in range(1, n_dp):
         from_plane(noise_all, noise_sem, flip).wait_recv()
-    images = noise_all[...].reshape(n_dp * 8, k_rows).astype(low)
+    pictures = noise.shape[1]
+    images = noise_all[...].reshape(n_dp * pictures, k_rows).astype(low)
     for c in range(own_cols // tile):
         terms[:, :, c * tile : (c + 1) * tile] = mm(
             images, mod_w[:, c * tile : (c + 1) * tile]
-        ).reshape(n_dp, 8, tile)
+        ).reshape(n_dp, pictures, tile)
     for flip in range(1, n_dp):
         to_plane(terms, terms_all, terms_sem, flip).start()
+    attend_g.start()
     terms_all[d] = terms[d]
     for flip in range(1, n_dp):
         from_plane(terms_all, terms_sem, flip).wait_recv()
-    columns[pl.ds(pl.multiple_of(i * 8, 8), 8), :] = jnp.sum(terms_all[...], axis=0)
-    own_columns = columns.at[pl.ds(pl.multiple_of(i * 8, 8), 8)]
-    column_line = LineGather(
-        n, i, 8, own_columns, columns, column_sem.at[0], column_sem.at[1], column_sem.at[2]
-    )
-    column_line.start()
-    for s in range(1, n):
-        column_line.step(s)
+    columns[i] = jnp.sum(terms_all[...], axis=0)
+
+    def to_line(turn):
+        t = lax.rem(i + turn, n)
+        return pltpu.make_async_remote_copy(
+            src_ref=columns.at[i],
+            dst_ref=columns.at[i],
+            send_sem=column_sem.at[0, t],
+            recv_sem=column_sem.at[1, i],
+            device_id=(d, t),
+            device_id_type=MESH,
+        )
+
+    def from_line(turn):
+        t = lax.rem(i + turn, n)
+        return pltpu.make_async_remote_copy(
+            src_ref=columns.at[t],
+            dst_ref=columns.at[t],
+            send_sem=column_sem.at[0, t],
+            recv_sem=column_sem.at[1, t],
+            device_id=(d, t),
+            device_id_type=MESH,
+        )
+
+    for turn in range(1, n):
+        to_line(turn).start()
+    merge_line.start()
+    x_line.step(1)
+    for turn in range(1, n):
+        from_line(turn).wait_recv()
     unit = math.gcd(width, own_cols)
 
     def fill(j, carry):
         for number in range(6):
             for start in range(0, width, unit):
                 at = number * width + start
-                part = columns[at // own_cols * 8 : at // own_cols * 8 + 8, pl.ds(at % own_cols, unit)]
+                part = columns[at // own_cols, :, at % own_cols : at % own_cols + unit]
                 table[j, number : number + 1, start : start + unit] = jnp.sum(
                     part * chosen[j][:, :1], axis=0, keepdims=True
                 )
         return carry
 
     lax.fori_loop(0, n, fill, 0)
-    x_line.step(1)
     attend_g.relay()
     merge_line.step(1)
     for copy in copies:
@@ -851,8 +872,10 @@
     for flip in range(1, n_dp):
         to_plane(noise, noise_all, noise_sem, flip).wait_send()
         to_plane(terms, terms_all, terms_sem, flip).wait_send()
-    for line in (merge_line, x_line, column_line, cot_line):
+    for line in (merge_line, x_line, cot_line):
         line.finish()
+    for turn in range(1, n):
+        to_line(turn).wait_send()
     for turn in range(1, n):
         to_owner(lax.rem(i + turn, n)).wait_send()
     for weight in weights:
@@ -889,16 +912,16 @@
             sds((n * merge_w.shape[0], n_dp * merge_w.shape[1]), low),
             sds((n_dp * k_rows, up_w.shape[1]), low),
             sds((down_w.shape[0], n_dp * down_w.shape[1]), low),
-            sds((n_dp, 8, k_rows), f32),
+            sds(noise.shape, f32),
         ],
         [HBM] + [VMEM] * 9 + [HBM] * 4 + [VMEM],
         [
             pltpu.VMEM((total, width), low),
             pltpu.VMEM((n_dp * k_rows, wide), low),
             pltpu.VMEM((n * merge_w.shape[0], n_dp * merge_w.shape[1]), low),
-            pltpu.VMEM((n_dp, 8, own_cols), f32),
-            pltpu.VMEM((n_dp, 8, own_cols), f32),
-            pltpu.VMEM((n * 8, own_cols), f32),
+            pltpu.VMEM((n_dp, noise.shape[1], own_cols), f32),
+            pltpu.VMEM((n_dp, noise.shape[1], own_cols), f32),
+            pltpu.VMEM((n, noise.shape[1], own_cols), f32),
             DMA((2, n_dp)),
             DMA((2, n_dp)),
             DMA((3, n)),
@@ -916,10 +939,11 @@
 
 
 class PlaneScatter:
-    def __init__(self, n_dp, d, theirs, own, swapped, landed, sems):
-        self.chips, self.d = n_dp // 2, d
+    def __init__(self, n_dp, d, theirs, own, swapped, via, landed, sems):
+        self.chips, self.d, self.square = n_dp // 2, d, n_dp == 8
         self.chip, self.side = d // 2, lax.rem(d, 2)
-        self.theirs, self.own, self.swapped, self.landed, self.sems = theirs, own, swapped, landed, sems
+        self.theirs, self.own, self.swapped, self.via = theirs, own, swapped, via
+        self.landed, self.sems = landed, sems
 
     def remote(self, source, target, sent, came, device):
         return pltpu.make_async_remote_copy(
@@ -936,27 +960,34 @@
             self.theirs(m), self.swapped.at[m], self.sems.at[0, m], self.sems.at[1, m], self.d ^ 1
         )
 
-    def send(self, m):
+    def half(self, ref, which):
+        height = self.own.shape[1] // 2
+        return ref.at[pl.ds(which * height, height), :]
+
+    def step(self, k):
+        slab, which, peer = ((1, 0, 1), (3, 0, 1), (2, 1, 2), (3, 1, 2), (2, 0, 2), (1, 1, 1))[k]
+        target = self.via if slab == 3 else self.landed.at[1 if k < 4 else 2]
+        return self.remote(
+            self.half(self.own.at[self.chip ^ slab], which),
+            self.half(target, which),
+            self.sems.at[2, k],
+            self.sems.at[3, k],
+            2 * (self.chip ^ peer) + self.side,
+        )
+
+    def send(self, m, slot, sem):
         return self.remote(
             self.own.at[m],
-            self.landed.at[self.chip],
+            self.landed.at[slot],
             self.sems.at[2, m],
-            self.sems.at[3, self.chip],
+            self.sems.at[3, sem],
             2 * m + self.side,
         )
 
-    def come(self, m):
-        return self.remote(
-            self.own.at[m],
-            self.landed.at[m],
-            self.sems.at[2, m],
-            self.sems.at[3, m],
-            2 * m + self.side,
-        )
-
     def keep(self):
+        slot = 0 if self.square else self.chip
         return pltpu.make_async_copy(
-            self.own.at[self.chip], self.landed.at[self.chip], self.sems.at[2, self.chip]
+            self.own.at[self.chip], self.landed.at[slot], self.sems.at[2, 6 if self.square else self.chip]
         )
 
     def swap_all(self):
@@ -966,43 +997,71 @@
 
         lax.fori_loop(0, self.chips, one, 0)
 
+    def add(self, target, source):
+        height, wide = target.shape
+        chunk = math.gcd(height, 64 if wide > 512 else 256)
+
+        def one(c, carry):
+            at = pl.ds(pl.multiple_of(c * chunk, chunk), chunk)
+            total = target[at, :].astype(jnp.float32) + source[at, :].astype(jnp.float32)
+            target[at, :] = total.astype(target.dtype)
+            return carry
+
+        lax.fori_loop(0, height // chunk, one, 0)
+
     def add_and_send(self):
-        _, height, wide = self.own.shape
-        chunk = math.gcd(height, 64 if wide > 512 else 256)
-
         def one(k, carry):
             m = self.chip ^ (self.chips - 1 - k)
             self.swap(m).wait_recv()
-
-            def add(c, inner):
-                at = pl.ds(pl.multiple_of(c * chunk, chunk), chunk)
-                total = self.own[m, at, :].astype(jnp.float32) + self.swapped[m, at, :].astype(
-                    jnp.float32
-                )
-                self.own[m, at, :] = total.astype(self.own.dtype)
-                return inner
-
-            lax.fori_loop(0, height // chunk, add, 0)
-
-            @pl.when(m != self.chip)
-            def _():
-                self.send(m).start()
+            self.add(self.own.at[m], self.swapped.at[m])
+            if not self.square:
+
+                @pl.when(m != self.chip)
+                def _():
+                    self.send(m, self.chip, self.chip).start()
 
             return carry
 
         lax.fori_loop(0, self.chips, one, 0)
+        if self.square:
+            for k in (1, 3, 0, 2):
+                self.step(k).start()
         self.keep().start()
 
+    def relay(self):
+        if self.square:
+            for k, slab, which in ((1, 2, 0), (3, 1, 1)):
+                self.step(k).wait_recv()
+                self.step(k).wait_send()
+                self.add(self.half(self.own.at[self.chip ^ slab], which), self.half(self.via, which))
+                self.step(4 if k == 1 else 5).start()
+
     def landed_all(self):
-        for k in range(1, self.chips):
-            self.come(self.chip ^ k).wait_recv()
+        if self.square:
+            for k in (0, 2, 4, 5):
+                self.step(k).wait_recv()
+        else:
+            for k in range(1, self.chips):
+                self.send(self.chip ^ k, self.chip ^ k, self.chip ^ k).wait_recv()
         self.keep().wait()
 
     def finish(self):
         for m in range(self.chips):
             self.swap(m).wait_send()
-        for k in range(1, self.chips):
-            self.send(self.chip ^ k).wait_send()
+        if self.square:
+            for k in (0, 2, 4, 5):
+                self.step(k).wait_send()
+        else:
+            for k in range(1, self.chips):
+                self.send(self.chip ^ k, self.chip, self.chip).wait_send()
+
+
+def plane_slots(n_dp):
+    return 3 if n_dp == 8 else n_dp // 2
+
+
+def scatter_sems(n_dp):
+    return DMA((4, max(7, n_dp // 2)))
 
 
 def flows(n, pieces, sums, turn):
@@ -1050,8 +1109,10 @@
     d_values,
     up_own,
     up_swapped,
+    up_via,
     down_own,
     down_swapped,
+    down_via,
     stage,
     mlp_sent,
     mlp_came,
@@ -1080,9 +1141,12 @@
     load_mlp = pltpu.make_async_copy(mlp_hbm, part, load_sem.at[0])
     load_mlp.start()
 
-    def load_merge(t, slot):
+    some = merge.shape[1]
+    shares = head_cols // some
+
+    def load_merge(k, slot):
         return pltpu.make_async_copy(
-            merge_hbm.at[pl.ds(pl.multiple_of(t * head_cols, head_cols), head_cols), :],
+            merge_hbm.at[pl.ds(pl.multiple_of(k * some, some), some), :],
             merge.at[slot],
             merge_sem.at[slot],
         )
@@ -1093,10 +1157,17 @@
         pltpu.make_async_copy(down_slab(2 * m + side), down_own.at[m], own_sem.at[1, m]).start()
     greet_all(n, n_dp, d, i)
     up = PlaneScatter(
-        n_dp, d, lambda m: up_slab(2 * m + 1 - side), up_own, up_swapped, up_landed, up_sems
+        n_dp, d, lambda m: up_slab(2 * m + 1 - side), up_own, up_swapped, up_via, up_landed, up_sems
     )
     down = PlaneScatter(
-        n_dp, d, lambda m: down_slab(2 * m + 1 - side), down_own, down_swapped, down_landed, down_sems
+        n_dp,
+        d,
+        lambda m: down_slab(2 * m + 1 - side),
+        down_own,
+        down_swapped,
+        down_via,
+        down_landed,
+        down_sems,
     )
     up.swap_all()
     down.swap_all()
@@ -1110,7 +1181,7 @@
         pl.when(i == n - 1)(functools.partial(sums.at_end, n - 1 - t, c))
         return carry
 
-    lax.fori_loop(0, (n - 1) * pieces, ends, 0)
+    lax.fori_loop(0, min(n - 1, 1) * pieces, ends, 0)
 
     tiles = [slice(c * tile, (c + 1) * tile) for c in range(width // tile)]
     squares = jnp.zeros((rows, 1), f32)
@@ -1154,14 +1225,18 @@
         )
 
     def head_part(t, carry):
-        slot = lax.rem(t, 2)
-
-        @pl.when(t + 1 < n)
-        def _():
-            load_merge(t + 1, 1 - slot).start()
-
-        load_merge(t, slot).wait()
-        d_send[t] = mm_nt(d_attn[...], merge[slot]).astype(low)
+        for share in range(shares):
+            k = t * shares + share
+            slot = lax.rem(k, 2)
+
+            @pl.when(k + 1 < n * shares)
+            def _():
+                load_merge(k + 1, 1 - slot).start()
+
+            load_merge(k, slot).wait()
+            d_send[t, :, share * some : (share + 1) * some] = mm_nt(
+                d_attn[...], merge[slot]
+            ).astype(low)
 
         @pl.when(t != i)
         def _():
@@ -1170,6 +1245,7 @@
         return carry
 
     lax.fori_loop(0, n, head_part, 0)
+    lax.fori_loop(min(n - 1, 1) * pieces, (n - 1) * pieces, ends, 0)
     d_att[rows_of(i, rows), :] = d_send[i]
     for m in range(chips):
         pltpu.make_async_copy(up_slab(2 * m + side), up_own.at[m], own_sem.at[0, m]).wait()
@@ -1177,10 +1253,11 @@
     up.add_and_send()
 
     wide = width // tile
+    short = stage.shape[1]
 
     def square(row, column):
         return merge_grad.at[
-            pl.ds(pl.multiple_of(row * tile, tile), tile),
+            pl.ds(pl.multiple_of(row * short, short), short),
             pl.ds(pl.multiple_of(column * tile, tile), tile),
         ]
 
@@ -1192,15 +1269,16 @@
         def _():
             pltpu.make_async_copy(stage.at[slot], square(0, 0), stage_sem.at[slot]).wait()
 
-        a = att_rows[:, pl.ds(pl.multiple_of(row * tile, tile), tile)]
+        a = att_rows[:, pl.ds(pl.multiple_of(row * short, short), short)]
         b = d_attn[:, pl.ds(pl.multiple_of(column * tile, tile), tile)]
         stage[slot] = mm_tn(a, b).astype(low)
         pltpu.make_async_copy(stage.at[slot], square(row, column), stage_sem.at[slot]).start()
         return carry
 
-    lax.fori_loop(0, wide * wide, merge_one, 0)
+    lax.fori_loop(0, width // short * wide, merge_one, 0)
     for slot in range(2):
         pltpu.make_async_copy(stage.at[slot], square(0, 0), stage_sem.at[slot]).wait()
+    down.add_and_send()
     for turn in range(1, n):
         from_rows(lax.rem(i + turn, n)).wait_recv()
 
@@ -1241,7 +1319,7 @@
 
         @pl.when(here_at == 0)
         def _():
-            down.add_and_send()
+            up.relay()
 
         for extra in range(per_area):
             turn = here_at * per_area + extra
@@ -1264,6 +1342,7 @@
         sums_out[5:6, at] = jnp.sum(cot[:, at].astype(f32) * total, axis=0, keepdims=True)
     sums_out[0:2, :] = jnp.zeros((2, width), f32)
     sums_out[6:8, :] = jnp.zeros((2, width), f32)
+    down.relay()
     for scatter in (up, down):
         scatter.landed_all()
         scatter.finish()
@@ -1289,14 +1368,14 @@
             sds((total, wide), low),
             sds((8, width), f32),
             sds((width, width), low),
-            sds((chips, k_rows, units), low),
-            sds((chips, units, down_cols), low),
+            sds((plane_slots(n_dp), k_rows, units), low),
+            sds((plane_slots(n_dp), units, down_cols), low),
         ],
         [VMEM] * 4 + [HBM] * 3,
         [
             pltpu.VMEM((total, width), low),
             pltpu.VMEM((total + rows, width), low),
-            pltpu.VMEM((2, heads * HEAD_DIM, width), low),
+            pltpu.VMEM((2, math.gcd(256, heads * HEAD_DIM), width), low),
             pltpu.VMEM((total, heads * HEAD_DIM), low),
             pltpu.VMEM((n, rows, heads * HEAD_DIM), low),
             pltpu.VMEM((rows, width), low),
@@ -1304,13 +1383,15 @@
             pltpu.VMEM((total, heads * HEAD_DIM), f32),
             pltpu.VMEM((chips, k_rows, units), low),
             pltpu.VMEM((chips, k_rows, units), low),
+            pltpu.VMEM((k_rows, units), low),
             pltpu.VMEM((chips, units, down_cols), low),
             pltpu.VMEM((chips, units, down_cols), low),
-            pltpu.VMEM((2, tile, tile), low),
+            pltpu.VMEM((units, down_cols), low),
+            pltpu.VMEM((2, tile // 2, tile), low),
             DMA((n, pieces)),
             DMA((n + 1, pieces)),
-            DMA((4, chips)),
-            DMA((4, chips)),
+            scatter_sems(n_dp),
+            scatter_sems(n_dp),
             DMA((2, n)),
             DMA((2,)),
             DMA((1,)),
@@ -1346,8 +1427,10 @@
     grad_own,
     grad_theirs,
     grad_swapped,
+    grad_via,
     merge_own,
     merge_swapped,
+    merge_via,
     merge_landed,
     merge_part,
     merge_got,
@@ -1378,6 +1461,7 @@
     k_rows, own_cols = mod_w.shape
     merge_cols = merge_own.shape[2]
     merge_rows = merge_out.shape[0]
+    images = chosen.shape[1]
 
     def merge_slab(at):
         return merge_hbm.at[:, pl.ds(pl.multiple_of(at * merge_cols, merge_cols), merge_cols)]
@@ -1393,11 +1477,12 @@
         lambda m: merge_slab(2 * m + 1 - side),
         merge_own,
         merge_swapped,
+        merge_via,
         merge_landed,
         merge_sems,
     )
     grad = PlaneScatter(
-        n_dp, d, lambda m: grad_theirs.at[m], grad_own, grad_swapped, attend_landed, grad_sems
+        n_dp, d, lambda m: grad_theirs.at[m], grad_own, grad_swapped, grad_via, attend_landed, grad_sems
     )
     merge.swap_all()
     sums = LineScatter(n, i, rows, tile, part, got, sent, came)
@@ -1417,10 +1502,11 @@
         lax.fori_loop(0, pieces, one, 0)
         return carry
 
-    lax.fori_loop(0, n, partial_block, 0)
+    partial_block(0, 0)
     for m in range(chips):
         pltpu.make_async_copy(merge_slab(2 * m + side), merge_own.at[m], own_sem.at[m]).wait()
     merge.add_and_send()
+    lax.fori_loop(1, n, partial_block, 0)
 
     def slab_grad(at):
         columns = pl.ds(pl.multiple_of(at * k_rows, k_rows), k_rows)
@@ -1438,6 +1524,7 @@
     lax.fori_loop(0, chips, for_them, 0)
     lax.fori_loop(0, chips, for_us, 0)
     grad.add_and_send()
+    merge.relay()
     turns = 2 * max(n - 2, 0) * pieces
 
     def pass_by(turn, carry):
@@ -1446,22 +1533,7 @@
 
     lax.fori_loop(0, turns, pass_by, 0)
 
-    merge.landed_all()
-    merge_sums = LineScatter(
-        n, i, merge_rows, merge_cols, merge_part, merge_got, merge_sent, merge_came
-    )
-
-    def merge_block(q, carry):
-        j = jnp.where(2 * i < n - 1, n - 1 - q, q)
-        here = rows_of(j, merge_rows)
-        total = merge_landed[0, here, :].astype(f32)
-        for m in range(1, chips):
-            total += merge_landed[m, here, :].astype(f32)
-        merge_part[here, :] = total.astype(low)
-        merge_sums.at_end(j, 0)
-        return carry
-
-    lax.fori_loop(0, n, merge_block, 0)
+    grad.relay()
 
     tiles = [slice(c * tile, (c + 1) * tile) for c in range(width // tile)]
     squares = jnp.zeros((rows, 1), f32)
@@ -1530,6 +1602,24 @@
 
     for turn in range(1, n):
         to_line(shares, shares_all, share_sem, turn).start()
+
+    merge.landed_all()
+    merge_sums = LineScatter(
+        n, i, merge_rows, merge_cols, merge_part, merge_got, merge_sent, merge_came
+    )
+
+    def merge_block(q, carry):
+        j = jnp.where(2 * i < n - 1, n - 1 - q, q)
+        here = rows_of(j, merge_rows)
+        total = merge_landed[0, here, :].astype(f32)
+        for m in range(1, merge_landed.shape[0]):
+            total += merge_landed[m, here, :].astype(f32)
+        merge_part[here, :] = total.astype(low)
+        merge_sums.at_end(j, 0)
+        return carry
+
+    lax.fori_loop(0, n, merge_block, 0)
+
     mean = mean * (1.0 / width)
     for c, at in enumerate(tiles):
         v = x_own[:, at].astype(f32) * root
@@ -1547,8 +1637,8 @@
             merge_sums.pass_on(t, 0, near)
     for flip in range(1, n_dp):
         from_plane(own_mod, d_mod_all, mod_sem, flip).wait_recv()
-    flat = d_mod_all[...].reshape(n_dp * 8, own_cols).astype(low)
-    terms[...] = mm_nt(flat, mod_w[...]).reshape(n_dp, 8, k_rows)
+    flat = d_mod_all[...].reshape(n_dp * images, own_cols).astype(low)
+    terms[...] = mm_nt(flat, mod_w[...]).reshape(n_dp, images, k_rows)
     for turn in range(1, n):
         to_line(terms, terms_all, term_sem, turn, True).start()
     terms_all[i] = terms[...]
@@ -1575,7 +1665,7 @@
 
 
 def last(n, n_dp, operands, shapes, number, tile=512):
-    (rows, width), wide, k_rows, own_cols, (merge_rows, merge_cols) = shapes
+    (rows, width), wide, k_rows, own_cols, (merge_rows, merge_cols), images = shapes
     total, chips, pieces = n * rows, n_dp // 2, width // tile
     low, f32 = jnp.bfloat16, jnp.float32
     sds = jax.ShapeDtypeStruct
@@ -1586,9 +1676,9 @@
         [VMEM] * 8 + [HBM] * 2,
         [
             sds((rows, width), low),
-            sds((n_dp, 8, own_cols), f32),
-            sds((n_dp, 8, k_rows), f32),
-            sds((chips, k_rows, wide), low),
+            sds((n_dp, images, own_cols), f32),
+            sds((n_dp, images, k_rows), f32),
+            sds((plane_slots(n_dp), k_rows, wide), low),
             sds((merge_rows, merge_cols), f32),
         ],
         [VMEM] * 3 + [HBM] + [VMEM],
@@ -1599,23 +1689,25 @@
             pltpu.VMEM((chips, k_rows, wide), low),
             pltpu.VMEM((chips, k_rows, wide), low),
             pltpu.VMEM((chips, k_rows, wide), low),
-            pltpu.VMEM((chips, n * merge_rows, merge_cols), low),
+            pltpu.VMEM((k_rows, wide), low),
             pltpu.VMEM((chips, n * merge_rows, merge_cols), low),
             pltpu.VMEM((chips, n * merge_rows, merge_cols), low),
             pltpu.VMEM((n * merge_rows, merge_cols), low),
+            pltpu.VMEM((plane_slots(n_dp), n * merge_rows, merge_cols), low),
+            pltpu.VMEM((n * merge_rows, merge_cols), low),
             pltpu.VMEM(((n + 1) * merge_rows, merge_cols), low),
             pltpu.VMEM((8, width), f32),
-            pltpu.VMEM((n, 8, own_cols), f32),
-            pltpu.VMEM((n, 8, own_cols), f32),
-            pltpu.VMEM((n_dp, 8, k_rows), f32),
-            pltpu.VMEM((n, n_dp, 8, k_rows), f32),
-            pltpu.VMEM((n_dp, 8, k_rows), f32),
+            pltpu.VMEM((n, images, own_cols), f32),
+            pltpu.VMEM((n, images, own_cols), f32),
+            pltpu.VMEM((n_dp, images, k_rows), f32),
+            pltpu.VMEM((n, n_dp, images, k_rows), f32),
+            pltpu.VMEM((n_dp, images, k_rows), f32),
             DMA((n, pieces)),
             DMA((n + 1, pieces)),
             DMA((n, 1)),
             DMA((n + 1, 1)),
-            DMA((4, chips)),
-            DMA((4, chips)),
+            scatter_sems(n_dp),
+            scatter_sems(n_dp),
             DMA((2, n)),
             DMA((2, n_dp)),
             DMA((2, n)),
@@ -1652,16 +1744,13 @@
         return sum((places >= end).astype(jnp.int32) for end in ends)
 
     block_images = image_at(jnp.arange(n, dtype=jnp.int32) * rows)
-    chosen = (block_images[:, None] == jnp.arange(8, dtype=jnp.int32)[None, :]) & (
-        jnp.arange(8) < images
-    )[None]
-    chosen = jnp.broadcast_to(chosen.astype(jnp.float32)[:, :, None], (n, 8, 128))
+    chosen = block_images[:, None] == jnp.arange(images, dtype=jnp.int32)[None, :]
+    chosen = jnp.broadcast_to(chosen.astype(jnp.float32)[:, :, None], (n, images, 128))
     area = min(256, tokens)
     area_images = image_at(jnp.arange(tokens // area, dtype=jnp.int32) * area)
     bias = jnp.where(area_images[:, None] == area_images[None, :], 0.0, MASKED)
     noise_low = jax.nn.silu(noise_embed.astype(jnp.float32)).astype(jnp.bfloat16)
     noise_slabs = noise_low.astype(jnp.float32).reshape(images, n_dp, k_rows).transpose(1, 0, 2)
-    noise_slabs = jnp.pad(noise_slabs, ((0, 0), (0, 8 - images), (0, 0)))
     (
         cot_full,
         hidden_first,
@@ -1742,7 +1831,14 @@
             merge_local,
             attend_full,
         ),
-        (block_input.shape, wide, k_rows, modulate_weight.shape[1], merge_weight.shape),
+        (
+            block_input.shape,
+            wide,
+            k_rows,
+            modulate_weight.shape[1],
+            merge_weight.shape,
+            images,
+        ),
         3,
     )
 
@@ -1751,11 +1847,11 @@
 
     up_part, down_part, attend_part = map(chip_sum, (up_landed, down_landed, attend_landed))
     modulate_part = dot(
-        noise_all.reshape(n_dp * 8, k_rows).astype(jnp.bfloat16),
-        d_mod_all.reshape(n_dp * 8, -1).astype(jnp.bfloat16),
+        noise_all.reshape(n_dp * images, k_rows).astype(jnp.bfloat16),
+        d_mod_all.reshape(n_dp * images, -1).astype(jnp.bfloat16),
         ROWS_ROWS,
     )
-    noise_sum = noise_sums[:, :images].transpose(1, 0, 2).reshape(images, width)
+    noise_sum = noise_sums.transpose(1, 0, 2).reshape(images, width)
     silu_back = jax.vjp(jax.nn.silu, noise_embed.astype(jnp.float32))[1]
     noise_grad = silu_back(noise_sum)[0]
     return (

time: 622 us -> 562 us (0.904)
  Pallas kernels: 598 us -> 539 us
    pallas_call x1, Pallas kernels: 134 us -> 107 us  [back(): call(functools.partial(back_kernel, n, n_dp, heads, tile), number, 'back'...]
    pallas_call x1, Pallas kernels: 135 us -> 110 us  [last(): call(functools.partial(last_kernel, n, n_dp, tile), number, 'last', [VMEM...]
    pallas_call x1, Pallas kernels: 199 us -> 192 us  [front(): call(functools.partial(front_kernel, n, n_dp, heads, 512), number, 'front...]
where the time goes in v4:
time: 562 us
  Pallas kernels  539 us (96%)
  other arithmetic  11.3 us (2%)
    pallas_call x1, Pallas kernels, front(): call(functools.partial(front_kernel, n, n_dp, heads, 512), number, 'front...  192 us
    pallas_call x1, Pallas kernels, ffn(): call(functools.partial(ffn_kernel, n, tile, grad_tile), collective_id, 'f...  130 us
    pallas_call x1, Pallas kernels, last(): call(functools.partial(last_kernel, n, n_dp, tile), number, 'last', [VMEM...  110 us
    pallas_call x1, Pallas kernels, back(): call(functools.partial(back_kernel, n, n_dp, heads, tile), number, 'back'...  107 us

profile of v4, /device:TPU:0, one launch (start us, length us, event | category | flops | bytes accessed | tf_op | source)
XLA Modules:
  0.0 561.7 jit_solution(1991467090411303672)
XLA Ops:
  0.6 1.4 fusion.12
  4.6 0.7 fusion.11
  5.3 0.6 compare_select_fusion.bias
  5.9 0.1 fusion.8
  6.0 0.7 broadcast_in_dim.8.chosen
  6.7 0.7 fusion.4
  7.4 0.6 convert_bitcast_fusion.noise
  8.0 192.1 %front.1 = (bf16[1024,2048]{1,0:T(8,128)(2,1)}, bf16[1024,2048]{1,0:T(8,128)(2,1)}, bf16[1024,1536]{1,0:T(8,128)(2,1)}, f32[16,256]{1,0:T(8,128)}, bf16[1024,512...) custom-call(bf16[256,2048]{1,0:T(8,128)(2,1)} %x_own.3, ...), custom_call_target="tpu_custom_call" | custom-call | flops 6442450944 | bytes 1048576 | tf_op jit(solution)/shard_map/front/pallas_call | solution.py:895
  200.2 130.3 %ffn.1 = (f32[256,2048]{1,0:T(8,128)}, bf16[1024,2048]{1,0:T(8,128)(2,1)}, bf16[2048,2048]{1,0:T(8,128)(2,1)}, bf16[2048,2048]{1,0:T(8,128)(2,1)}) custom-call(bf16[256,2048]{1,0:T(8,128)(2,1)} %get-tuple-element.38.own_hidden, f32[4,8,2048]{2,1,0:T(8,128)} %get-tuple-element.39.table, bf16[1024,2048]{1,0:T(8,128)(2,1)} %get-tuple-element.40.d_mlp_hbm, ...), custom_call_target="tpu_custom_call" | custom-call | flops 51539607552 | bytes 1048576 | tf_op jit(solution)/shard_map/ffn/pallas_call | solution.py:411
  330.5 107.1 %back.1 = (bf16[256,2048]{1,0:T(8,128)(2,1)}, f32[256,2048]{1,0:T(8,128)}, bf16[1024,1536]{1,0:T(8,128)(2,1)}, f32[8,2048]{1,0:T(8,128)}, bf16[2048,2048]{1,0:T(...) custom-call(f32[256,2048]{1,0:T(8,128)} %get-tuple-element.43.d_hidden, bf16[256,2048]{1,0:T(8,128)(2,1)} %cot.1, ...), custom_call_target="tpu_custom_call" | custom-call | flops 10737418240 | bytes 1048576 | tf_op jit(solution)/shard_map/back/pallas_call | solution.py:1360
  437.7 0.0 copy-start.5
  437.7 109.7 %last.1 = (bf16[256,2048]{1,0:T(8,128)(2,1)}, f32[8,4,3072]{2,1,0:T(4,128)}, f32[8,4,256]{2,1,0:T(4,128)}, bf16[3,256,1536]{2,1,0:T(8,128)(2,1)}, f32[512,256]{1,0:T(8,128)}) custom-call(bf16[1024,1536]{1,0:T(8,128)(2,1)} %get-tuple-element.54.d_qkv, bf16[1024,2048]{1,0:T(8,128)(2,1)} %get-tuple-element.55.hidden, bf16[256,2048]{1,0:T(8,128)(2,1)} %x_own.3, ...), custom_call_target="tpu_custom_call" | custom-call | flops 12884901888 | bytes 1048576 | tf_op jit(solution)/shard_map/last/pallas_call | solution.py:1672
  547.4 0.0 copy-start.1
  547.4 0.0 copy-done.5
  547.4 1.6 fusion.6
  549.0 3.3 convert_reduce_fusion.2
  552.3 0.0 copy-done.1
  552.3 2.0 convert_reduce_fusion.1
  554.3 0.6 copy-done
  554.9 1.7 convert_reduce_fusion
  556.7 2.3 convolution_bitcast_fusion
  559.0 1.0 copy.24
  560.0 1.0 copy.25
  560.9 0.8 copy.26
  (11 shorter events, 0.0 us)
Async XLA Ops:
  437.7 109.8 %copy-start.5 = (bf16[4,2048]{1,0:T(4,128)(2,1)S(1)}, bf16[4,2048]{1,0:T(4,128)(2,1)}, u32[]{:S(2)}) copy-start(bf16[4,2048]{1,0:T(4,128)(2,1)} %param.11) | copy-start | bytes 49156
  547.4 4.9 copy-start.1
  552.3 2.6 copy-start
  554.9 1.7 copy-start.6
  554.9 1.7 copy-start.7
  556.7 2.3 copy-start.2
  556.7 3.3 copy-start.3
  559.0 1.9 copy-start.4

commit v5 on v4

--- a/solution.py
+++ b/solution.py
@@ -260,6 +260,7 @@
     part,
     got,
     stage,
+    mlp,
     to_left,
     to_right,
     arrived,
@@ -279,8 +280,10 @@
         load.start()
     greet_line(n, i)
     line = LineGather(n, i, rows, own_hidden, hidden, to_left, to_right, arrived)
-    line.start()
-    sums = LineScatter(n, i, rows, tile, part, got, sent, came)
+    first_core = lax.rem(lax.axis_index("dp"), 2) == 0
+    pl.when(first_core)(line.start)
+    piece = tile // 2
+    sums = LineScatter(n, i, rows, piece, part, got, sent, came)
     hidden[rows_of(i, rows), :] = own_hidden[...]
     for load in loads:
         load.wait()
@@ -312,14 +315,15 @@
         def second(c, carry):
             at = pl.ds(pl.multiple_of(c * tile, tile), tile)
             part[here, at] = mm_nt(d_pre[here, :], up[at, :]).astype(jnp.bfloat16)
-            sums.at_end(j, c)
+            for k in range(tile // piece):
+                sums.at_end(j, c * (tile // piece) + k)
             return carry
 
         lax.fori_loop(0, width // tile, second, 0)
 
         def third(c, carry):
             at = pl.ds(pl.multiple_of(c * tile, tile), tile)
-            mlp_part[here, at] = mm(activated[here, :], down[:, at]).astype(jnp.bfloat16)
+            mlp[here, at] = mm(activated[here, :], down[:, at]).astype(jnp.bfloat16)
             return carry
 
         lax.fori_loop(0, width // tile, third, 0)
@@ -337,9 +341,15 @@
         def _():
             one_block(j)
 
+        @pl.when((q == 0) & jnp.logical_not(first_core))
+        def _():
+            line.start()
+
         return carry
 
     lax.fori_loop(0, 2 * n - 1, visit, 0)
+    keep_mlp = pltpu.make_async_copy(mlp, mlp_part, local.at[3])
+    keep_mlp.start()
 
     count = (width // grad_tile) * (units // grad_tile)
     turns = 2 * max(n - 2, 1) * sums.pieces
@@ -401,12 +411,13 @@
         sums.own(c, d_hidden)
     line.finish()
     sums.all_sent()
+    keep_mlp.wait()
 
 
 def ffn(n, own_hidden, table, cotangents, up, down, collective_id, tile=512, grad_tile=512):
     rows, width = own_hidden.shape
     units = up.shape[1]
-    pieces = width // tile
+    pieces = 2 * width // tile
     low = jnp.bfloat16
     return call(
         functools.partial(ffn_kernel, n, tile, grad_tile),
@@ -419,7 +430,7 @@
             jax.ShapeDtypeStruct((width, units), low),
             jax.ShapeDtypeStruct((units, width), low),
         ],
-        [VMEM, VMEM, HBM, HBM],
+        [VMEM, HBM, HBM, HBM],
         [
             pltpu.VMEM((width, units), low),
             pltpu.VMEM((units, width), low),
@@ -430,16 +441,33 @@
             pltpu.VMEM((n * rows, width), low),
             pltpu.VMEM(((n + 1) * rows, width), low),
             pltpu.VMEM((2, grad_tile, grad_tile), low),
+            pltpu.VMEM((n * rows, width), low),
             DMA((n,)),
             DMA((n,)),
             DMA((n,)),
             DMA((n, pieces)),
             DMA((n + 1, pieces)),
-            DMA((3,)),
+            DMA((4,)),
             DMA((2,)),
         ],
         flops=12 * n * rows * width * units,
     )(own_hidden, table, cotangents, up, down)
+
+
+def image_at(sizes, place):
+    end, count = 0, 0
+    for k in range(sizes.shape[1]):
+        end = end + sizes[0, k]
+        count = count + jnp.where(place >= end, 1, 0)
+    return count
+
+
+def image_at(sizes, place):
+    end, count = 0, 0
+    for k in range(sizes.shape[1]):
+        end = end + sizes[0, k]
+        count = count + jnp.where(place >= end, 1, 0)
+    return count
 
 
 class PlaneGather:
@@ -547,19 +575,17 @@
     tile,
     x_own,
     cot_own,
-    noise,
+    noise_own,
     mod_w,
-    chosen,
-    bias,
+    sizes,
     attend_w,
     merge_w,
     up_w,
     down_w,
     cot_full,
-    hidden,
-    qkv,
+    hidden_out,
+    qkv_out,
     lse,
-    attended,
     att_rows,
     attn_out,
     middle,
@@ -573,6 +599,10 @@
     x_full,
     attend,
     merge,
+    noise,
+    hidden,
+    qkv,
+    attended,
     terms,
     terms_all,
     columns,
@@ -623,9 +653,9 @@
         pltpu.make_async_copy(source, target, local.at[k])
         for k, (source, target) in enumerate(
             (
-                (cot_own, cot_full.at[rows_of(i, rows)]),
                 (attend_w, attend_g.slab(0)),
                 (merge_w, merge_slab.at[rows_of(i, merge_rows)]),
+                (cot_own, cot_full.at[rows_of(i, rows)]),
                 (up_w, up_g.slab(0)),
                 (down_w, down_g.slab(0)),
             )
@@ -655,6 +685,9 @@
             device_id_type=MESH,
         )
 
+    for k in range(n_dp):
+        v = noise_own[:, k * k_rows : (k + 1) * k_rows].astype(f32)
+        noise[k] = (v * (1.0 / (1.0 + jnp.exp(-v)))).astype(low).astype(f32)
     for flip in range(1, n_dp):
         to_plane(noise, noise_all, noise_sem, flip).start()
     merge_line = LineGather(
@@ -714,25 +747,29 @@
     unit = math.gcd(width, own_cols)
 
     def fill(j, carry):
+        image = image_at(sizes, j * rows)
         for number in range(6):
             for start in range(0, width, unit):
                 at = number * width + start
-                part = columns[at // own_cols, :, at % own_cols : at % own_cols + unit]
-                table[j, number : number + 1, start : start + unit] = jnp.sum(
-                    part * chosen[j][:, :1], axis=0, keepdims=True
+                here = slice(at % own_cols, at % own_cols + unit)
+                table[j, number : number + 1, start : start + unit] = sum(
+                    columns[at // own_cols, k : k + 1, here] * jnp.where(image == k, 1.0, 0.0)
+                    for k in range(pictures)
                 )
         return carry
 
     lax.fori_loop(0, n, fill, 0)
     attend_g.relay()
     merge_line.step(1)
-    for copy in copies:
+    for copy in copies[:2]:
         copy.wait()
     attend_g.close()
     up_g.start()
     keep_attend = pltpu.make_async_copy(attend, attend_full, out_sem.at[0])
     keep_merge = pltpu.make_async_copy(merge, merge_full, out_sem.at[1])
     keep_attend.start()
+    keep_hidden = pltpu.make_async_copy(hidden, hidden_out, out_sem.at[2])
+    keep_qkv = pltpu.make_async_copy(qkv, qkv_out, out_sem.at[3])
 
     def tiles(count):
         return [slice(c * tile, (c + 1) * tile) for c in range(count // tile)]
@@ -777,9 +814,13 @@
 
     lax.fori_loop(0, 2 * n - 1, visit, 0)
 
+    keep_hidden.start()
+    keep_qkv.start()
+
     area = min(256, n * rows)
     areas = n * rows // area
     owners = area // rows
+    area_images = [image_at(sizes, b * area) for b in range(areas)]
 
     def to_owner(j):
         return pltpu.make_async_remote_copy(
@@ -804,13 +845,17 @@
     def attend_area(turn, carry):
         here_at = lax.rem(i // owners + 1 + turn, areas)
         here = rows_of(here_at, area)
+        image = image_at(sizes, here_at * area)
         for h in range(heads):
             first = h * 3 * HEAD_DIM
             q = qkv[here, first : first + HEAD_DIM]
             parts = []
             for b in range(areas):
                 key = qkv[b * area : (b + 1) * area, first + HEAD_DIM : first + 2 * HEAD_DIM]
-                parts.append(mm_nt(key, q) * HEAD_DIM ** (-0.5) + bias[here_at, b])
+                parts.append(
+                    mm_nt(key, q) * HEAD_DIM ** (-0.5)
+                    + jnp.where(image == area_images[b], 0.0, MASKED)
+                )
             highest = parts[0].max(axis=0, keepdims=True)
             for part in parts[1:]:
                 highest = jnp.maximum(highest, part.max(axis=0, keepdims=True))
@@ -867,8 +912,12 @@
     for s in range(3, n):
         cot_line.step(s)
     down_g.close()
+    for copy in copies[2:]:
+        copy.wait()
     keep_attend.wait()
     keep_merge.wait()
+    keep_hidden.wait()
+    keep_qkv.wait()
     for flip in range(1, n_dp):
         to_plane(noise, noise_all, noise_sem, flip).wait_send()
         to_plane(terms, terms_all, terms_sem, flip).wait_send()
@@ -882,13 +931,14 @@
         weight.finish()
 
 
-def front(n, n_dp, x, cot, noise, mod_w, chosen, bias, attend_w, merge_w, up_w, down_w, number):
+def front(n, n_dp, x, cot, noise, mod_w, sizes, attend_w, merge_w, up_w, down_w, number):
     rows, width = x.shape
     k_rows, own_cols = mod_w.shape
     wide = attend_w.shape[1]
     heads = wide // (3 * HEAD_DIM)
     total = n * rows
-    areas = bias.shape[0]
+    areas = total // min(256, total)
+    pictures = noise.shape[0]
     low, f32 = jnp.bfloat16, jnp.float32
     sds = jax.ShapeDtypeStruct
     count = plane_sems(n_dp)
@@ -896,13 +946,12 @@
         functools.partial(front_kernel, n, n_dp, heads, 512),
         number,
         "front",
-        [VMEM] * 5 + [pl.BlockSpec(memory_space=pltpu.SMEM)] + [VMEM] * 4,
+        [VMEM, HBM, VMEM, VMEM, pl.BlockSpec(memory_space=pltpu.SMEM), VMEM, VMEM, HBM, HBM],
         [
             sds((total, width), low),
             sds((total, width), low),
             sds((total, wide), low),
             sds((areas * heads, total // areas), f32),
-            sds((total, heads * HEAD_DIM), low),
             sds((rows, width), low),
             sds((rows, width), f32),
             sds((rows, width), f32),
@@ -912,16 +961,20 @@
             sds((n * merge_w.shape[0], n_dp * merge_w.shape[1]), low),
             sds((n_dp * k_rows, up_w.shape[1]), low),
             sds((down_w.shape[0], n_dp * down_w.shape[1]), low),
-            sds(noise.shape, f32),
+            sds((n_dp, pictures, k_rows), f32),
         ],
-        [HBM] + [VMEM] * 9 + [HBM] * 4 + [VMEM],
+        [HBM] * 3 + [VMEM] * 6 + [HBM] * 4 + [VMEM],
         [
             pltpu.VMEM((total, width), low),
             pltpu.VMEM((n_dp * k_rows, wide), low),
             pltpu.VMEM((n * merge_w.shape[0], n_dp * merge_w.shape[1]), low),
-            pltpu.VMEM((n_dp, noise.shape[1], own_cols), f32),
-            pltpu.VMEM((n_dp, noise.shape[1], own_cols), f32),
-            pltpu.VMEM((n, noise.shape[1], own_cols), f32),
+            pltpu.VMEM((n_dp, pictures, k_rows), f32),
+            pltpu.VMEM((total, width), low),
+            pltpu.VMEM((total, wide), low),
+            pltpu.VMEM((total, heads * HEAD_DIM), low),
+            pltpu.VMEM((n_dp, pictures, own_cols), f32),
+            pltpu.VMEM((n_dp, pictures, own_cols), f32),
+            pltpu.VMEM((n, pictures, own_cols), f32),
             DMA((2, n_dp)),
             DMA((2, n_dp)),
             DMA((3, n)),
@@ -930,12 +983,12 @@
             DMA((3, n)),
             DMA((4, count)),
             DMA((4, count)),
-            DMA((2,)),
+            DMA((4,)),
             DMA((2, n)),
             DMA((5,)),
         ],
         flops=2 * total * width * wide,
-    )(x, cot, noise, mod_w, chosen, bias, attend_w, merge_w, up_w, down_w)
+    )(x, cot, noise, mod_w, sizes, attend_w, merge_w, up_w, down_w)
 
 
 class PlaneScatter:
@@ -1080,14 +1133,14 @@
     heads,
     tile,
     d_hidden,
-    cot,
     middle,
-    attn_out,
     table,
-    att_rows,
-    qkv,
     lse,
-    bias,
+    sizes,
+    cot_hbm,
+    out_hbm,
+    rows_hbm,
+    qkv_hbm,
     mlp_hbm,
     merge_hbm,
     up_hbm,
@@ -1099,6 +1152,10 @@
     merge_grad,
     up_landed,
     down_landed,
+    cot,
+    attn_out,
+    att_rows,
+    qkv,
     part,
     got,
     merge,
@@ -1140,6 +1197,12 @@
 
     load_mlp = pltpu.make_async_copy(mlp_hbm, part, load_sem.at[0])
     load_mlp.start()
+    load_cot = pltpu.make_async_copy(cot_hbm, cot, load_sem.at[3])
+    load_out = pltpu.make_async_copy(out_hbm, attn_out, load_sem.at[4])
+    load_cot.start()
+    load_out.start()
+    load_rows = pltpu.make_async_copy(rows_hbm, att_rows, load_sem.at[1])
+    load_qkv = pltpu.make_async_copy(qkv_hbm, qkv, load_sem.at[2])
 
     some = merge.shape[1]
     shares = head_cols // some
@@ -1155,6 +1218,8 @@
     for m in range(chips):
         pltpu.make_async_copy(up_slab(2 * m + side), up_own.at[m], own_sem.at[0, m]).start()
         pltpu.make_async_copy(down_slab(2 * m + side), down_own.at[m], own_sem.at[1, m]).start()
+    load_rows.start()
+    load_qkv.start()
     greet_all(n, n_dp, d, i)
     up = PlaneScatter(
         n_dp, d, lambda m: up_slab(2 * m + 1 - side), up_own, up_swapped, up_via, up_landed, up_sems
@@ -1172,7 +1237,8 @@
     up.swap_all()
     down.swap_all()
     load_mlp.wait()
-    sums = LineScatter(n, i, rows, tile, part, got, mlp_sent, mlp_came)
+    piece = tile // 2
+    sums = LineScatter(n, i, rows, piece, part, got, mlp_sent, mlp_came)
     pieces = sums.pieces
 
     def ends(k, carry):
@@ -1196,6 +1262,8 @@
         sums_out[3:4, at] = jnp.sum(dh, axis=0, keepdims=True)
         sums_out[4:5, at] = jnp.sum(dh * v, axis=0, keepdims=True)
     mean = mean * (1.0 / width)
+    load_cot.wait()
+    load_out.wait()
     for at in tiles:
         v = middle[:, at] * root
         u = d_hidden[:, at] * (1.0 + table[i, 4:5, at])
@@ -1252,6 +1320,8 @@
         pltpu.make_async_copy(down_slab(2 * m + side), down_own.at[m], own_sem.at[1, m]).wait()
     up.add_and_send()
 
+    load_rows.wait()
+    load_qkv.wait()
     wide = width // tile
     short = stage.shape[1]
 
@@ -1284,14 +1354,15 @@
 
     area = lse.shape[1]
     areas = n * rows // area
+    area_images = [image_at(sizes, b * area) for b in range(areas)]
     d_keys[...] = jnp.zeros_like(d_keys)
     d_values[...] = jnp.zeros_like(d_values)
     turns = 2 * max(n - 2, 0) * pieces
-    per_area = -(-turns // areas)
     scale = HEAD_DIM ** (-0.5)
 
     def back_area(here_at, carry):
         here = rows_of(here_at, area)
+        image = image_at(sizes, here_at * area)
         for h in range(heads):
             first = h * 3 * HEAD_DIM
             head = slice(h * HEAD_DIM, (h + 1) * HEAD_DIM)
@@ -1303,7 +1374,7 @@
             for b in range(areas):
                 key = qkv[b * area : (b + 1) * area, first + HEAD_DIM : first + 2 * HEAD_DIM]
                 value = qkv[b * area : (b + 1) * area, first + 2 * HEAD_DIM : first + 3 * HEAD_DIM]
-                scores = mm_nt(key, q) * scale + bias[here_at, b]
+                scores = mm_nt(key, q) * scale + jnp.where(image == area_images[b], 0.0, MASKED)
                 probs.append(jnp.exp(scores - log_row))
                 d_probs.append(mm_nt(value, g))
                 inner += jnp.sum(probs[b] * d_probs[b], axis=0, keepdims=True)
@@ -1317,26 +1388,27 @@
                 d_query += mm_tn(key, d_scores)
             d_qkv[here, first : first + HEAD_DIM] = (d_query * scale).T.astype(low)
 
-        @pl.when(here_at == 0)
+        @pl.when(here_at == areas - 1)
         def _():
             up.relay()
 
-        for extra in range(per_area):
-            turn = here_at * per_area + extra
-
-            @pl.when(turn < turns)
-            def _():
-                flows(n, pieces, sums, turn)
-
         return carry
 
+    def pass_by(turn, carry):
+        flows(n, pieces, sums, turn)
+        return carry
+
+    early = min(turns, pieces)
+    lax.fori_loop(0, early, pass_by, 0)
     lax.fori_loop(0, areas, back_area, 0)
+    lax.fori_loop(early, turns, pass_by, 0)
     for h in range(heads):
         first = h * 3 * HEAD_DIM
         head = slice(h * HEAD_DIM, (h + 1) * HEAD_DIM)
         d_qkv[:, first + HEAD_DIM : first + 2 * HEAD_DIM] = (d_keys[:, head] * scale).astype(low)
         d_qkv[:, first + 2 * HEAD_DIM : first + 3 * HEAD_DIM] = d_values[:, head].astype(low)
-    for c, at in enumerate(tiles):
+    for c in range(pieces):
+        at = slice(c * piece, (c + 1) * piece)
         total = sums.own_value(c)
         block_out[:, at] = (middle[:, at] + table[i, 5:6, at] * total).astype(low)
         sums_out[5:6, at] = jnp.sum(cot[:, at].astype(f32) * total, axis=0, keepdims=True)
@@ -1354,14 +1426,14 @@
 def back(n, n_dp, operands, shapes, number, tile=512):
     (rows, width), wide, units, k_rows, down_cols, areas = shapes
     heads = wide // (3 * HEAD_DIM)
-    total, chips, pieces = n * rows, n_dp // 2, width // tile
+    total, chips, pieces = n * rows, n_dp // 2, 2 * width // tile
     low, f32 = jnp.bfloat16, jnp.float32
     sds = jax.ShapeDtypeStruct
     return call(
         functools.partial(back_kernel, n, n_dp, heads, tile),
         number,
         "back",
-        [VMEM] * 8 + [pl.BlockSpec(memory_space=pltpu.SMEM)] + [HBM] * 4,
+        [VMEM] * 4 + [pl.BlockSpec(memory_space=pltpu.SMEM)] + [HBM] * 8,
         [
             sds((rows, width), low),
             sds((rows, width), f32),
@@ -1373,6 +1445,10 @@
         ],
         [VMEM] * 4 + [HBM] * 3,
         [
+            pltpu.VMEM((rows, width), low),
+            pltpu.VMEM((rows, width), f32),
+            pltpu.VMEM((rows, width), low),
+            pltpu.VMEM((total, wide), low),
             pltpu.VMEM((total, width), low),
             pltpu.VMEM((total + rows, width), low),
             pltpu.VMEM((2, math.gcd(256, heads * HEAD_DIM), width), low),
@@ -1394,7 +1470,7 @@
             scatter_sems(n_dp),
             DMA((2, n)),
             DMA((2,)),
-            DMA((1,)),
+            DMA((5,)),
             DMA((2,)),
             DMA((2, chips)),
         ],
@@ -1407,13 +1483,13 @@
     n_dp,
     tile,
     d_qkv,
-    hidden,
-    x_own,
-    d_middle,
     sums_in,
     table,
-    chosen,
-    mod_w,
+    sizes,
+    hidden_hbm,
+    x_hbm,
+    middle_hbm,
+    mod_hbm,
     merge_hbm,
     attend_hbm,
     input_grad,
@@ -1421,6 +1497,10 @@
     noise_sum,
     attend_landed,
     merge_out,
+    hidden,
+    x_own,
+    d_middle,
+    mod_w,
     attend,
     part,
     got,
@@ -1452,22 +1532,39 @@
     noise_sem,
     load_sem,
     own_sem,
+    attend_sem,
 ):
     d, i = lax.axis_index("dp"), lax.axis_index("tensor")
-    rows, width = x_own.shape
+    rows, width = input_grad.shape
     low, f32 = jnp.bfloat16, jnp.float32
     chips = n_dp // 2
     side = lax.rem(d, 2)
     k_rows, own_cols = mod_w.shape
     merge_cols = merge_own.shape[2]
     merge_rows = merge_out.shape[0]
-    images = chosen.shape[1]
+    images = d_mod_all.shape[1]
 
     def merge_slab(at):
         return merge_hbm.at[:, pl.ds(pl.multiple_of(at * merge_cols, merge_cols), merge_cols)]
 
-    load = pltpu.make_async_copy(attend_hbm, attend, load_sem)
-    load.start()
+    load_hidden, load_x, load_middle, load_mod = (
+        pltpu.make_async_copy(source, target, load_sem.at[k])
+        for k, (source, target) in enumerate(
+            (
+                (hidden_hbm, hidden),
+                (x_hbm, x_own),
+                (middle_hbm, d_middle),
+                (mod_hbm, mod_w),
+            )
+        )
+    )
+
+    def load_attend(c):
+        at = pl.ds(pl.multiple_of(c * tile, tile), tile)
+        return pltpu.make_async_copy(attend_hbm.at[at, :], attend.at[at, :], attend_sem.at[c])
+
+    for c in range(width // tile):
+        load_attend(c).start()
     for m in range(chips):
         pltpu.make_async_copy(merge_slab(2 * m + side), merge_own.at[m], own_sem.at[m]).start()
     greet_all(n, n_dp, d, i)
@@ -1485,9 +1582,11 @@
         n_dp, d, lambda m: grad_theirs.at[m], grad_own, grad_swapped, grad_via, attend_landed, grad_sems
     )
     merge.swap_all()
-    sums = LineScatter(n, i, rows, tile, part, got, sent, came)
+    for late in (load_hidden, load_x, load_middle, load_mod):
+        late.start()
+    piece = tile // 2
+    sums = LineScatter(n, i, rows, piece, part, got, sent, came)
     pieces = sums.pieces
-    load.wait()
 
     def partial_block(q, carry):
         j = jnp.where(2 * i < n - 1, n - 1 - q, q)
@@ -1495,11 +1594,17 @@
 
         def one(c, inner):
             at = pl.ds(pl.multiple_of(c * tile, tile), tile)
+
+            @pl.when(q == 0)
+            def _():
+                load_attend(c).wait()
+
             part[here, at] = mm_nt(d_qkv[here, :], attend[at, :]).astype(low)
-            sums.at_end(j, c)
+            for k in range(tile // piece):
+                sums.at_end(j, c * (tile // piece) + k)
             return inner
 
-        lax.fori_loop(0, pieces, one, 0)
+        lax.fori_loop(0, width // tile, one, 0)
         return carry
 
     partial_block(0, 0)
@@ -1521,6 +1626,7 @@
         grad_own[m] = slab_grad(2 * m + side)
         return carry
 
+    load_hidden.wait()
     lax.fori_loop(0, chips, for_them, 0)
     lax.fori_loop(0, chips, for_us, 0)
     grad.add_and_send()
@@ -1535,7 +1641,9 @@
 
     grad.relay()
 
-    tiles = [slice(c * tile, (c + 1) * tile) for c in range(width // tile)]
+    for late in (load_x, load_middle, load_mod):
+        late.wait()
+    tiles = [slice(c * piece, (c + 1) * piece) for c in range(pieces)]
     squares = jnp.zeros((rows, 1), f32)
     for at in tiles:
         v = x_own[:, at].astype(f32)
@@ -1551,12 +1659,15 @@
         sums_all[1:2, at] = jnp.sum(dh * v, axis=0, keepdims=True)
 
     unit = math.gcd(width, own_cols)
+    image = image_at(sizes, i * rows)
     for number in range(6):
         for start in range(0, width, unit):
             at = number * width + start
-            shares[at // own_cols, :, at % own_cols : at % own_cols + unit] = (
-                chosen[i][:, :1] * sums_all[number : number + 1, start : start + unit]
-            )
+            for k in range(images):
+                shares[at // own_cols, k : k + 1, at % own_cols : at % own_cols + unit] = (
+                    sums_all[number : number + 1, start : start + unit]
+                    * jnp.where(image == k, 1.0, 0.0)
+                )
 
     def to_line(source, target, sems, turn, whole=False):
         t = lax.rem(i + turn, n)
@@ -1666,14 +1777,14 @@
 
 def last(n, n_dp, operands, shapes, number, tile=512):
     (rows, width), wide, k_rows, own_cols, (merge_rows, merge_cols), images = shapes
-    total, chips, pieces = n * rows, n_dp // 2, width // tile
+    total, chips, pieces = n * rows, n_dp // 2, 2 * width // tile
     low, f32 = jnp.bfloat16, jnp.float32
     sds = jax.ShapeDtypeStruct
     return call(
         functools.partial(last_kernel, n, n_dp, tile),
         number,
         "last",
-        [VMEM] * 8 + [HBM] * 2,
+        [VMEM] * 3 + [pl.BlockSpec(memory_space=pltpu.SMEM)] + [HBM] * 6,
         [
             sds((rows, width), low),
             sds((n_dp, images, own_cols), f32),
@@ -1683,6 +1794,10 @@
         ],
         [VMEM] * 3 + [HBM] + [VMEM],
         [
+            pltpu.VMEM((total, width), low),
+            pltpu.VMEM((rows, width), low),
+            pltpu.VMEM((rows, width), f32),
+            pltpu.VMEM((k_rows, own_cols), low),
             pltpu.VMEM((width, wide), low),
             pltpu.VMEM((total, width), low),
             pltpu.VMEM((total + rows, width), low),
@@ -1712,8 +1827,9 @@
             DMA((2, n_dp)),
             DMA((2, n)),
             DMA((2, n_dp)),
-            DMA,
+            DMA((4,)),
             DMA((chips,)),
+            DMA((width // tile,)),
         ],
         flops=4 * total * width * wide,
     )(*operands)
@@ -1737,26 +1853,11 @@
     images = image_sizes.shape[1]
     k_rows = modulate_weight.shape[0]
 
-    sizes_row = image_sizes[0]
-    ends = [sum(sizes_row[j] for j in range(last + 1)) for last in range(images)]
-
-    def image_at(places):
-        return sum((places >= end).astype(jnp.int32) for end in ends)
-
-    block_images = image_at(jnp.arange(n, dtype=jnp.int32) * rows)
-    chosen = block_images[:, None] == jnp.arange(images, dtype=jnp.int32)[None, :]
-    chosen = jnp.broadcast_to(chosen.astype(jnp.float32)[:, :, None], (n, images, 128))
-    area = min(256, tokens)
-    area_images = image_at(jnp.arange(tokens // area, dtype=jnp.int32) * area)
-    bias = jnp.where(area_images[:, None] == area_images[None, :], 0.0, MASKED)
-    noise_low = jax.nn.silu(noise_embed.astype(jnp.float32)).astype(jnp.bfloat16)
-    noise_slabs = noise_low.astype(jnp.float32).reshape(images, n_dp, k_rows).transpose(1, 0, 2)
     (
         cot_full,
         hidden_first,
         packed,
         lse,
-        _,
         att_rows,
         attn_out,
         middle,
@@ -1772,10 +1873,9 @@
         n_dp,
         block_input,
         cotangent,
-        noise_slabs,
+        noise_embed,
         modulate_weight,
-        chosen,
-        bias,
+        image_sizes,
         attend_weight,
         merge_weight,
         up_weight,
@@ -1800,20 +1900,20 @@
         n_dp,
         (
             d_hidden_second,
+            middle,
+            table,
+            lse,
+            image_sizes,
             cotangent,
-            middle,
             attn_out,
-            table,
             att_rows,
             packed,
-            lse,
-            bias,
             mlp_part,
             merge_full,
             up_local,
             down_local,
         ),
-        (block_input.shape, wide, units, k_rows, down_weight.shape[1], bias.shape[0]),
+        (block_input.shape, wide, units, k_rows, down_weight.shape[1], lse.shape[0]),
         2,
     )
     input_grad, d_mod_all, noise_sums, attend_landed, merge_part = last(
@@ -1821,12 +1921,12 @@
         n_dp,
         (
             d_qkv,
+            row_sums,
+            table,
+            image_sizes,
             hidden_first,
             block_input,
             d_middle,
-            row_sums,
-            table,
-            chosen,
             modulate_weight,
             merge_local,
             attend_full,
@@ -1843,7 +1943,7 @@
     )
 
     def chip_sum(landed):
-        return jnp.sum(landed.astype(jnp.float32), axis=0)
+        return sum(landed[slot].astype(jnp.float32) for slot in range(landed.shape[0]))
 
     up_part, down_part, attend_part = map(chip_sum, (up_landed, down_landed, attend_landed))
     modulate_part = dot(

time: 562 us -> 545 us (0.970)
  Pallas kernels: 539 us -> 529 us
    pallas_call x1, Pallas kernels: 130 us -> 113 us  [ffn(): call(functools.partial(ffn_kernel, n, tile, grad_tile), collective_id, 'f...]
    pallas_call x1, Pallas kernels: 107 us -> 119 us  [back(): call(functools.partial(back_kernel, n, n_dp, heads, tile), number, 'back'...]
    reduce_sum x3 -> x0, other arithmetic: 6.99 us -> none  [chip_sum(): return jnp.sum(landed.astype(jnp.float32), axis=0)]
    add x1 -> x3, other arithmetic: 0.65 us -> 6.55 us  [chip_sum(): sum((landed[slot].astype(jnp.float32) for slot in range(landed.shape[0])))]
where the time goes in v5:
time: 545 us
  Pallas kernels  529 us (97%)
  other arithmetic  8.12 us (1%)
    pallas_call x1, Pallas kernels, front(): call(functools.partial(front_kernel, n, n_dp, heads, 512), number, 'front...  189 us
    pallas_call x1, Pallas kernels, back(): call(functools.partial(back_kernel, n, n_dp, heads, tile), number, 'back'...  119 us
    pallas_call x1, Pallas kernels, ffn(): call(functools.partial(ffn_kernel, n, tile, grad_tile), collective_id, 'f...  113 us
    pallas_call x1, Pallas kernels, last(): call(functools.partial(last_kernel, n, n_dp, tile), number, 'last', [VMEM...  109 us

profile of v5, /device:TPU:0, one launch (start us, length us, event | category | flops | bytes accessed | tf_op | source)
XLA Modules:
  0.0 544.8 jit_solution(16662653953761634200)
XLA Ops:
  0.6 188.7 %front.1 = (bf16[1024,2048]{1,0:T(8,128)(2,1)}, bf16[1024,2048]{1,0:T(8,128)(2,1)}, bf16[1024,1536]{1,0:T(8,128)(2,1)}, f32[16,256]{1,0:T(8,128)}, bf16[256,2048...) custom-call(bf16[256,2048]{1,0:T(8,128)(2,1)} %x_hbm.1, ...), custom_call_target="tpu_custom_call" | custom-call | flops 6442450944 | bytes 1048576 | tf_op jit(solution)/shard_map/front/pallas_call | solution.py:945
  189.3 112.9 %ffn.1 = (f32[256,2048]{1,0:T(8,128)}, bf16[1024,2048]{1,0:T(8,128)(2,1)}, bf16[2048,2048]{1,0:T(8,128)(2,1)}, bf16[2048,2048]{1,0:T(8,128)(2,1)}) custom-call(bf16[256,2048]{1,0:T(8,128)(2,1)} %get-tuple-element.38.own_hidden, f32[4,8,2048]{2,1,0:T(8,128)} %get-tuple-element.39.table, bf16[1024,2048]{1,0:T(8,128)(2,1)} %get-tuple-element.40.d_mlp_hbm, ...), custom_call_target="tpu_custom_call" | custom-call | flops 51539607552 | bytes 1048576 | tf_op jit(solution)/shard_map/ffn/pallas_call | solution.py:422
  302.2 119.1 %back.1 = (bf16[256,2048]{1,0:T(8,128)(2,1)}, f32[256,2048]{1,0:T(8,128)}, bf16[1024,1536]{1,0:T(8,128)(2,1)}, f32[8,2048]{1,0:T(8,128)}, bf16[2048,2048]{1,0:T(...) custom-call(f32[256,2048]{1,0:T(8,128)} %get-tuple-element.43.d_hidden, ...), custom_call_target="tpu_custom_call" | custom-call | flops 10737418240 | bytes 1048576 | tf_op jit(solution)/shard_map/back/pallas_call | solution.py:1432
  421.3 0.0 copy-start.5
  421.3 108.9 %last.1 = (bf16[256,2048]{1,0:T(8,128)(2,1)}, f32[8,4,3072]{2,1,0:T(4,128)}, f32[8,4,256]{2,1,0:T(4,128)}, bf16[3,256,1536]{2,1,0:T(8,128)(2,1)}, f32[512,256]{1,0:T(8,128)}) custom-call(bf16[1024,1536]{1,0:T(8,128)(2,1)} %get-tuple-element.54.d_qkv, f32[8,2048]{1,0:T(8,128)} %get-tuple-element.55.sums_in, f32[4,8,2048]{2,1,0:T(8,128)} %get-tuple-element.39.table, ...), custom_call_target="tpu_custom_call" | custom-call | flops 12884901888 | bytes 1048576 | tf_op jit(solution)/shard_map/last/pallas_call | solution.py:1783
  530.2 0.0 copy-start.1
  530.2 0.0 copy-done.5
  530.2 1.6 fusion.5
  531.8 3.0 add_bitcast_fusion.2
  534.8 0.0 copy-done.1
  534.8 0.0 copy-start
  534.8 1.9 add_bitcast_fusion.1
  536.7 0.8 copy-done
  537.4 0.0 copy-start.6
  537.4 1.7 add_bitcast_fusion
  539.1 0.0 copy-done.6
  539.1 0.0 copy-done.7
  539.1 2.3 convolution_bitcast_fusion
  541.4 0.0 copy-done.2
  541.4 1.0 copy.24
  542.4 0.6 copy-done.3
  543.0 1.0 copy.25
  544.0 0.0 copy-done.4
  544.0 0.8 copy.26
  (4 shorter events, 0.0 us)
Async XLA Ops:
  421.3 108.9 %copy-start.5 = (bf16[4,2048]{1,0:T(4,128)(2,1)S(1)}, bf16[4,2048]{1,0:T(4,128)(2,1)}, u32[]{:S(2)}) copy-start(bf16[4,2048]{1,0:T(4,128)(2,1)} %noise_own.1) | copy-start | bytes 49156
  530.2 4.6 copy-start.1
  534.8 2.6 copy-start
  537.4 1.7 copy-start.6
  537.4 1.7 copy-start.7
  539.1 2.3 copy-start.2
  541.4 1.6 copy-start.3
  541.4 2.6 copy-start.4

commit v6 on v5

--- a/solution.py
+++ b/solution.py
@@ -586,10 +586,10 @@
     hidden_out,
     qkv_out,
     lse,
-    att_rows,
-    attn_out,
-    middle,
-    hidden_second,
+    rows_out,
+    attn_out_hbm,
+    middle_out,
+    second_out,
     table,
     attend_full,
     merge_full,
@@ -603,6 +603,10 @@
     hidden,
     qkv,
     attended,
+    att_rows,
+    attn_out,
+    middle,
+    hidden_second,
     terms,
     terms_all,
     columns,
@@ -908,6 +912,19 @@
     for at in tiles(width):
         v = middle[:, at] * root
         hidden_second[:, at] = (v * (1.0 + table[i, 4:5, at]) + table[i, 3:4, at]).astype(low)
+    keeps = [
+        pltpu.make_async_copy(source, target, out_sem.at[4 + k])
+        for k, (source, target) in enumerate(
+            (
+                (att_rows, rows_out),
+                (attn_out, attn_out_hbm),
+                (middle, middle_out),
+                (hidden_second, second_out),
+            )
+        )
+    ]
+    for keep in keeps:
+        keep.start()
     down_g.relay()
     for s in range(3, n):
         cot_line.step(s)
@@ -918,6 +935,8 @@
     keep_merge.wait()
     keep_hidden.wait()
     keep_qkv.wait()
+    for keep in keeps:
+        keep.wait()
     for flip in range(1, n_dp):
         to_plane(noise, noise_all, noise_sem, flip).wait_send()
         to_plane(terms, terms_all, terms_sem, flip).wait_send()
@@ -963,7 +982,7 @@
             sds((down_w.shape[0], n_dp * down_w.shape[1]), low),
             sds((n_dp, pictures, k_rows), f32),
         ],
-        [HBM] * 3 + [VMEM] * 6 + [HBM] * 4 + [VMEM],
+        [HBM] * 3 + [VMEM] + [HBM] * 4 + [VMEM] + [HBM] * 4 + [VMEM],
         [
             pltpu.VMEM((total, width), low),
             pltpu.VMEM((n_dp * k_rows, wide), low),
@@ -972,6 +991,10 @@
             pltpu.VMEM((total, width), low),
             pltpu.VMEM((total, wide), low),
             pltpu.VMEM((total, heads * HEAD_DIM), low),
+            pltpu.VMEM((rows, width), low),
+            pltpu.VMEM((rows, width), f32),
+            pltpu.VMEM((rows, width), f32),
+            pltpu.VMEM((rows, width), low),
             pltpu.VMEM((n_dp, pictures, own_cols), f32),
             pltpu.VMEM((n_dp, pictures, own_cols), f32),
             pltpu.VMEM((n, pictures, own_cols), f32),
@@ -983,7 +1006,7 @@
             DMA((3, n)),
             DMA((4, count)),
             DMA((4, count)),
-            DMA((4,)),
+            DMA((8,)),
             DMA((2, n)),
             DMA((5,)),
         ],
@@ -1146,14 +1169,16 @@
     up_hbm,
     down_hbm,
     block_out,
-    d_middle,
-    d_qkv,
+    d_middle_out,
+    d_qkv_out,
     sums_out,
     merge_grad,
     up_landed,
     down_landed,
     cot,
     attn_out,
+    d_middle,
+    d_qkv,
     att_rows,
     qkv,
     part,
@@ -1272,6 +1297,9 @@
         d_attn[:, at] = (table[i, 2:3, at] * dm).astype(low)
         sums_out[2:3, at] = jnp.sum(dm * attn_out[:, at], axis=0, keepdims=True)
 
+    keep_middle = pltpu.make_async_copy(d_middle, d_middle_out, load_sem.at[5])
+    keep_middle.start()
+
     def to_heads(t):
         return pltpu.make_async_remote_copy(
             src_ref=d_send.at[t],
@@ -1401,12 +1429,14 @@
     early = min(turns, pieces)
     lax.fori_loop(0, early, pass_by, 0)
     lax.fori_loop(0, areas, back_area, 0)
-    lax.fori_loop(early, turns, pass_by, 0)
     for h in range(heads):
         first = h * 3 * HEAD_DIM
         head = slice(h * HEAD_DIM, (h + 1) * HEAD_DIM)
         d_qkv[:, first + HEAD_DIM : first + 2 * HEAD_DIM] = (d_keys[:, head] * scale).astype(low)
         d_qkv[:, first + 2 * HEAD_DIM : first + 3 * HEAD_DIM] = d_values[:, head].astype(low)
+    keep_qkv = pltpu.make_async_copy(d_qkv, d_qkv_out, load_sem.at[6])
+    keep_qkv.start()
+    lax.fori_loop(early, turns, pass_by, 0)
     for c in range(pieces):
         at = slice(c * piece, (c + 1) * piece)
         total = sums.own_value(c)
@@ -1415,6 +1445,8 @@
     sums_out[0:2, :] = jnp.zeros((2, width), f32)
     sums_out[6:8, :] = jnp.zeros((2, width), f32)
     down.relay()
+    keep_middle.wait()
+    keep_qkv.wait()
     for scatter in (up, down):
         scatter.landed_all()
         scatter.finish()
@@ -1443,10 +1475,12 @@
             sds((plane_slots(n_dp), k_rows, units), low),
             sds((plane_slots(n_dp), units, down_cols), low),
         ],
-        [VMEM] * 4 + [HBM] * 3,
+        [VMEM, HBM, HBM, VMEM] + [HBM] * 3,
         [
             pltpu.VMEM((rows, width), low),
             pltpu.VMEM((rows, width), f32),
+            pltpu.VMEM((rows, width), f32),
+            pltpu.VMEM((total, wide), low),
             pltpu.VMEM((rows, width), low),
             pltpu.VMEM((total, wide), low),
             pltpu.VMEM((total, width), low),
@@ -1470,7 +1504,7 @@
             scatter_sems(n_dp),
             DMA((2, n)),
             DMA((2,)),
-            DMA((5,)),
+            DMA((7,)),
             DMA((2,)),
             DMA((2, chips)),
         ],
@@ -1833,6 +1867,131 @@
         ],
         flops=4 * total * width * wide,
     )(*operands)
+
+
+def final_kernel(
+    noise_own,
+    noise_all,
+    d_mod,
+    noise_sums,
+    up_in,
+    down_in,
+    attend_in,
+    block_in,
+    input_in,
+    merge_in,
+    block_out,
+    input_out,
+    noise_grad,
+    attend_out,
+    merge_out,
+    up_out,
+    down_out,
+    modulate_out,
+    up_slots,
+    down_slots,
+    attend_slots,
+    up_sum,
+    down_sum,
+    attend_sum,
+    modulate,
+    block,
+    inputs,
+    merge,
+    sems,
+):
+    low, f32 = jnp.bfloat16, jnp.float32
+    loads = [
+        pltpu.make_async_copy(source, target, sems.at[0, k])
+        for k, (source, target) in enumerate(
+            (
+                (up_in, up_slots),
+                (down_in, down_slots),
+                (attend_in, attend_slots),
+                (block_in, block),
+                (input_in, inputs),
+                (merge_in, merge),
+            )
+        )
+    ]
+    stores = [
+        pltpu.make_async_copy(source, target, sems.at[1, k])
+        for k, (source, target) in enumerate(
+            (
+                (up_sum, up_out),
+                (down_sum, down_out),
+                (attend_sum, attend_out),
+                (block, block_out),
+                (inputs, input_out),
+                (merge, merge_out),
+                (modulate, modulate_out),
+            )
+        )
+    ]
+    for load in loads:
+        load.start()
+    n_dp, images, k_rows = noise_all.shape
+    left = noise_all[...].reshape(n_dp * images, k_rows).astype(low)
+    right = d_mod[...].reshape(n_dp * images, -1).astype(low)
+    modulate[...] = mm_tn(left, right)
+    stores[6].start()
+    for k in range(n_dp):
+        at = slice(k * k_rows, (k + 1) * k_rows)
+        v = noise_own[:, at].astype(f32)
+        gate = 1.0 / (1.0 + jnp.exp(-v))
+        noise_grad[:, at] = noise_sums[k] * (gate * (1.0 + v * (1.0 - gate)))
+
+    def add(slots, total):
+        count, height, wide = slots.shape
+        chunk = math.gcd(height, 32 if wide > 512 else 256)
+
+        def one(c, carry):
+            at = pl.ds(pl.multiple_of(c * chunk, chunk), chunk)
+            total[at, :] = sum(slots[s, at, :].astype(f32) for s in range(count))
+            return carry
+
+        lax.fori_loop(0, height // chunk, one, 0)
+
+    for k, (slots, total) in enumerate(
+        ((up_slots, up_sum), (down_slots, down_sum), (attend_slots, attend_sum))
+    ):
+        loads[k].wait()
+        add(slots, total)
+        stores[k].start()
+    for k in range(3, 6):
+        loads[k].wait()
+        stores[k].start()
+    for store in stores:
+        store.wait()
+
+
+def final(noise_own, noise_all, d_mod, noise_sums, up, down, attend, block, inputs, merge):
+    sds, f32 = jax.ShapeDtypeStruct, jnp.float32
+    own_cols, k_rows = d_mod.shape[2], noise_all.shape[2]
+    sums = [sds(a.shape[1:], f32) for a in (up, down, attend)]
+    modulate = sds((k_rows, own_cols), f32)
+    return pl.pallas_call(
+        final_kernel,
+        out_shape=[
+            sds(block.shape, block.dtype),
+            sds(inputs.shape, inputs.dtype),
+            sds(noise_own.shape, f32),
+            sums[2],
+            sds(merge.shape, f32),
+            sums[0],
+            sums[1],
+            modulate,
+        ],
+        in_specs=[VMEM] * 4 + [HBM] * 6,
+        out_specs=[HBM, HBM, VMEM] + [HBM] * 5,
+        scratch_shapes=[
+            pltpu.VMEM(a.shape, a.dtype)
+            for a in (up, down, attend, *sums, modulate, block, inputs, merge)
+        ]
+        + [DMA((2, 7))],
+        compiler_params=pltpu.CompilerParams(vmem_limit_bytes=60 * 1024 * 1024),
+        name="final",
+    )(noise_own, noise_all, d_mod, noise_sums, up, down, attend, block, inputs, merge)
 
 
 def on_device(
@@ -1942,27 +2101,19 @@
         3,
     )
 
-    def chip_sum(landed):
-        return sum(landed[slot].astype(jnp.float32) for slot in range(landed.shape[0]))
-
-    up_part, down_part, attend_part = map(chip_sum, (up_landed, down_landed, attend_landed))
-    modulate_part = dot(
-        noise_all.reshape(n_dp * images, k_rows).astype(jnp.bfloat16),
-        d_mod_all.reshape(n_dp * images, -1).astype(jnp.bfloat16),
-        ROWS_ROWS,
-    )
-    noise_sum = noise_sums.transpose(1, 0, 2).reshape(images, width)
-    silu_back = jax.vjp(jax.nn.silu, noise_embed.astype(jnp.float32))[1]
-    noise_grad = silu_back(noise_sum)[0]
-    return (
-        block_output,
-        input_grad,
-        noise_grad,
-        attend_part,
-        merge_part,
-        up_part,
-        down_part,
-        modulate_part,
+    return tuple(
+        final(
+            noise_embed,
+            noise_all,
+            d_mod_all,
+            noise_sums,
+            up_landed,
+            down_landed,
+            attend_landed,
+            block_output,
+            input_grad,
+            merge_part,
+        )
     )
 
 

time: 545 us -> 537 us (0.985)
  other arithmetic: 8.12 us -> 0 us
  Pallas kernels: 529 us -> 536 us
    pallas_call x0 -> x1, Pallas kernels: none -> 9.66 us  [final(): pl.pallas_call(final_kernel, out_shape=[sds(block.shape, block.dtype), sd...]
    add x3 -> x0, other arithmetic: 6.55 us -> none  [chip_sum(): sum((landed[slot].astype(jnp.float32) for slot in range(landed.shape[0])))]
where the time goes in v6:
time: 537 us; the launch traced here: 536 us
  Pallas kernels  536 us (100%)
    pallas_call x1, Pallas kernels, front(): call(functools.partial(front_kernel, n, n_dp, heads, 512), number, 'front...  187 us
    pallas_call x1, Pallas kernels, back(): call(functools.partial(back_kernel, n, n_dp, heads, tile), number, 'back'...  118 us
    pallas_call x1, Pallas kernels, ffn(): call(functools.partial(ffn_kernel, n, tile, grad_tile), collective_id, 'f...  113 us
    pallas_call x1, Pallas kernels, last(): call(functools.partial(last_kernel, n, n_dp, tile), number, 'last', [VMEM...  109 us

profile of v6, /device:TPU:0, one launch (start us, length us, event | category | flops | bytes accessed | tf_op | source)
XLA Modules:
  0.0 536.5 jit_solution(13720294255183479195)
XLA Ops:
  0.6 186.8 %front.1 = (bf16[1024,2048]{1,0:T(8,128)(2,1)}, bf16[1024,2048]{1,0:T(8,128)(2,1)}, bf16[1024,1536]{1,0:T(8,128)(2,1)}, f32[16,256]{1,0:T(8,128)}, bf16[256,2048...) custom-call(bf16[256,2048]{1,0:T(8,128)(2,1)} %x_hbm.1, ...), custom_call_target="tpu_custom_call" | custom-call | flops 6442450944 | bytes 1048576 | tf_op jit(solution)/shard_map/front/pallas_call | solution.py:964
  187.4 112.8 %ffn.1 = (f32[256,2048]{1,0:T(8,128)}, bf16[1024,2048]{1,0:T(8,128)(2,1)}, bf16[2048,2048]{1,0:T(8,128)(2,1)}, bf16[2048,2048]{1,0:T(8,128)(2,1)}) custom-call(bf16[256,2048]{1,0:T(8,128)(2,1)} %get-tuple-element.39.own_hidden, f32[4,8,2048]{2,1,0:T(8,128)} %get-tuple-element.40.table, bf16[1024,2048]{1,0:T(8,128)(2,1)} %get-tuple-element.41.d_mlp_hbm, ...), custom_call_target="tpu_custom_call" | custom-call | flops 51539607552 | bytes 1048576 | tf_op jit(solution)/shard_map/ffn/pallas_call | solution.py:422
  300.2 117.5 %back.1 = (bf16[256,2048]{1,0:T(8,128)(2,1)}, f32[256,2048]{1,0:T(8,128)}, bf16[1024,1536]{1,0:T(8,128)(2,1)}, f32[8,2048]{1,0:T(8,128)}, bf16[2048,2048]{1,0:T(...) custom-call(f32[256,2048]{1,0:T(8,128)} %get-tuple-element.44.d_hidden, ...), custom_call_target="tpu_custom_call" | custom-call | flops 10737418240 | bytes 1048576 | tf_op jit(solution)/shard_map/back/pallas_call | solution.py:1464
  417.7 108.9 %last.1 = (bf16[256,2048]{1,0:T(8,128)(2,1)}, f32[8,4,3072]{2,1,0:T(4,128)}, f32[8,4,256]{2,1,0:T(4,128)}, bf16[3,256,1536]{2,1,0:T(8,128)(2,1)}, f32[512,256]{1,0:T(8,128)}) custom-call(bf16[1024,1536]{1,0:T(8,128)(2,1)} %get-tuple-element.54.d_qkv, f32[8,2048]{1,0:T(8,128)} %get-tuple-element.55.sums_in, f32[4,8,2048]{2,1,0:T(8,128)} %get-tuple-element.40.table, ...), custom_call_target="tpu_custom_call" | custom-call | flops 12884901888 | bytes 1048576 | tf_op jit(solution)/shard_map/last/pallas_call | solution.py:1817
  526.6 9.7 %final.1 = (bf16[256,2048]{1,0:T(8,128)(2,1)}, bf16[256,2048]{1,0:T(8,128)(2,1)}, f32[4,2048]{1,0:T(4,128)}, f32[256,1536]{1,0:T(8,128)}, f32[512,256]{1,0:T(8,1...) custom-call(bf16[4,2048]{1,0:T(4,128)(2,1)} %noise_own.3, ...), custom_call_target="tpu_custom_call" | custom-call | tf_op jit(solution)/shard_map/final/pallas_call | solution.py:1973

commit v7 on v6

--- a/solution.py
+++ b/solution.py
@@ -586,7 +586,7 @@
     hidden_out,
     qkv_out,
     lse,
-    rows_out,
+    attended_out,
     attn_out_hbm,
     middle_out,
     second_out,
@@ -770,7 +770,9 @@
     attend_g.close()
     up_g.start()
     keep_attend = pltpu.make_async_copy(attend, attend_full, out_sem.at[0])
-    keep_merge = pltpu.make_async_copy(merge, merge_full, out_sem.at[1])
+    keep_merge = pltpu.make_async_copy(
+        merge.at[rows_of(i, merge_rows)], merge_full, out_sem.at[1]
+    )
     keep_attend.start()
     keep_hidden = pltpu.make_async_copy(hidden, hidden_out, out_sem.at[2])
     keep_qkv = pltpu.make_async_copy(qkv, qkv_out, out_sem.at[3])
@@ -916,7 +918,7 @@
         pltpu.make_async_copy(source, target, out_sem.at[4 + k])
         for k, (source, target) in enumerate(
             (
-                (att_rows, rows_out),
+                (attended, attended_out),
                 (attn_out, attn_out_hbm),
                 (middle, middle_out),
                 (hidden_second, second_out),
@@ -971,13 +973,13 @@
             sds((total, width), low),
             sds((total, wide), low),
             sds((areas * heads, total // areas), f32),
-            sds((rows, width), low),
+            sds((total, heads * HEAD_DIM), low),
             sds((rows, width), f32),
             sds((rows, width), f32),
             sds((rows, width), low),
             sds((n, 8, width), f32),
             sds((n_dp * k_rows, wide), low),
-            sds((n * merge_w.shape[0], n_dp * merge_w.shape[1]), low),
+            sds((merge_w.shape[0], width), low),
             sds((n_dp * k_rows, up_w.shape[1]), low),
             sds((down_w.shape[0], n_dp * down_w.shape[1]), low),
             sds((n_dp, pictures, k_rows), f32),
@@ -1179,13 +1181,12 @@
     attn_out,
     d_middle,
     d_qkv,
-    att_rows,
+    attended,
     qkv,
     part,
     got,
     merge,
     d_att,
-    d_send,
     d_attn,
     d_keys,
     d_values,
@@ -1200,7 +1201,7 @@
     mlp_came,
     up_sems,
     down_sems,
-    att_sem,
+    line_sem,
     merge_sem,
     load_sem,
     stage_sem,
@@ -1226,20 +1227,11 @@
     load_out = pltpu.make_async_copy(out_hbm, attn_out, load_sem.at[4])
     load_cot.start()
     load_out.start()
-    load_rows = pltpu.make_async_copy(rows_hbm, att_rows, load_sem.at[1])
+    load_rows = pltpu.make_async_copy(rows_hbm, attended, load_sem.at[1])
     load_qkv = pltpu.make_async_copy(qkv_hbm, qkv, load_sem.at[2])
 
-    some = merge.shape[1]
-    shares = head_cols // some
-
-    def load_merge(k, slot):
-        return pltpu.make_async_copy(
-            merge_hbm.at[pl.ds(pl.multiple_of(k * some, some), some), :],
-            merge.at[slot],
-            merge_sem.at[slot],
-        )
-
-    load_merge(0, 0).start()
+    load_merge = pltpu.make_async_copy(merge_hbm, merge, merge_sem)
+    load_merge.start()
     for m in range(chips):
         pltpu.make_async_copy(up_slab(2 * m + side), up_own.at[m], own_sem.at[0, m]).start()
         pltpu.make_async_copy(down_slab(2 * m + side), down_own.at[m], own_sem.at[1, m]).start()
@@ -1272,9 +1264,8 @@
         pl.when(i == n - 1)(functools.partial(sums.at_end, n - 1 - t, c))
         return carry
 
-    lax.fori_loop(0, min(n - 1, 1) * pieces, ends, 0)
-
     tiles = [slice(c * tile, (c + 1) * tile) for c in range(width // tile)]
+    own_rows = rows_of(i, rows)
     squares = jnp.zeros((rows, 1), f32)
     for at in tiles:
         squares += jnp.sum(middle[:, at] * middle[:, at], axis=1, keepdims=True)
@@ -1294,91 +1285,23 @@
         u = d_hidden[:, at] * (1.0 + table[i, 4:5, at])
         dm = cot[:, at].astype(f32) + root * (u - v * mean)
         d_middle[:, at] = dm
-        d_attn[:, at] = (table[i, 2:3, at] * dm).astype(low)
+        d_attn[own_rows, at] = (table[i, 2:3, at] * dm).astype(low)
         sums_out[2:3, at] = jnp.sum(dm * attn_out[:, at], axis=0, keepdims=True)
 
     keep_middle = pltpu.make_async_copy(d_middle, d_middle_out, load_sem.at[5])
     keep_middle.start()
 
-    def to_heads(t):
-        return pltpu.make_async_remote_copy(
-            src_ref=d_send.at[t],
-            dst_ref=d_att.at[rows_of(i, rows), :],
-            send_sem=att_sem.at[0, t],
-            recv_sem=att_sem.at[1, i],
-            device_id=(d, t),
-            device_id_type=MESH,
-        )
-
-    def from_rows(t):
-        return pltpu.make_async_remote_copy(
-            src_ref=d_send.at[t],
-            dst_ref=d_att.at[rows_of(t, rows), :],
-            send_sem=att_sem.at[0, t],
-            recv_sem=att_sem.at[1, t],
-            device_id=(d, t),
-            device_id_type=MESH,
-        )
-
-    def head_part(t, carry):
-        for share in range(shares):
-            k = t * shares + share
-            slot = lax.rem(k, 2)
-
-            @pl.when(k + 1 < n * shares)
-            def _():
-                load_merge(k + 1, 1 - slot).start()
-
-            load_merge(k, slot).wait()
-            d_send[t, :, share * some : (share + 1) * some] = mm_nt(
-                d_attn[...], merge[slot]
-            ).astype(low)
-
-        @pl.when(t != i)
-        def _():
-            to_heads(t).start()
-
-        return carry
-
-    lax.fori_loop(0, n, head_part, 0)
-    lax.fori_loop(min(n - 1, 1) * pieces, (n - 1) * pieces, ends, 0)
-    d_att[rows_of(i, rows), :] = d_send[i]
+    line = LineGather(
+        n, i, rows, d_attn.at[own_rows], d_attn, line_sem.at[0], line_sem.at[1], line_sem.at[2]
+    )
+    line.start()
+    lax.fori_loop(0, (n - 1) * pieces, ends, 0)
     for m in range(chips):
         pltpu.make_async_copy(up_slab(2 * m + side), up_own.at[m], own_sem.at[0, m]).wait()
         pltpu.make_async_copy(down_slab(2 * m + side), down_own.at[m], own_sem.at[1, m]).wait()
-    up.add_and_send()
-
     load_rows.wait()
     load_qkv.wait()
-    wide = width // tile
-    short = stage.shape[1]
-
-    def square(row, column):
-        return merge_grad.at[
-            pl.ds(pl.multiple_of(row * short, short), short),
-            pl.ds(pl.multiple_of(column * tile, tile), tile),
-        ]
-
-    def merge_one(k, carry):
-        row, column = k // wide, lax.rem(k, wide)
-        slot = lax.rem(k, 2)
-
-        @pl.when(k >= 2)
-        def _():
-            pltpu.make_async_copy(stage.at[slot], square(0, 0), stage_sem.at[slot]).wait()
-
-        a = att_rows[:, pl.ds(pl.multiple_of(row * short, short), short)]
-        b = d_attn[:, pl.ds(pl.multiple_of(column * tile, tile), tile)]
-        stage[slot] = mm_tn(a, b).astype(low)
-        pltpu.make_async_copy(stage.at[slot], square(row, column), stage_sem.at[slot]).start()
-        return carry
-
-    lax.fori_loop(0, width // short * wide, merge_one, 0)
-    for slot in range(2):
-        pltpu.make_async_copy(stage.at[slot], square(0, 0), stage_sem.at[slot]).wait()
-    down.add_and_send()
-    for turn in range(1, n):
-        from_rows(lax.rem(i + turn, n)).wait_recv()
+    load_merge.wait()
 
     area = lse.shape[1]
     areas = n * rows // area
@@ -1416,10 +1339,6 @@
                 d_query += mm_tn(key, d_scores)
             d_qkv[here, first : first + HEAD_DIM] = (d_query * scale).T.astype(low)
 
-        @pl.when(here_at == areas - 1)
-        def _():
-            up.relay()
-
         return carry
 
     def pass_by(turn, carry):
@@ -1427,8 +1346,37 @@
         return carry
 
     early = min(turns, pieces)
-    lax.fori_loop(0, early, pass_by, 0)
-    lax.fori_loop(0, areas, back_area, 0)
+
+    def visit(q, carry):
+        s = (q + 1) // 2
+        j = i + s * (1 - 2 * (q % 2))
+
+        @pl.when(q % 2 == 1)
+        def _():
+            line.step(s)
+
+        @pl.when((j >= 0) & (j < n))
+        def _():
+            here = rows_of(j, rows)
+            d_att[here, :] = mm_nt(d_attn[here, :], merge[...]).astype(low)
+            if area == rows:
+                back_area(j, 0)
+
+        @pl.when(q == 0)
+        def _():
+            up.add_and_send()
+            down.add_and_send()
+
+        @pl.when(q == 2 * (n - 2))
+        def _():
+            up.relay()
+            lax.fori_loop(0, early, pass_by, 0)
+
+        return carry
+
+    lax.fori_loop(0, 2 * n - 1, visit, 0)
+    if area != rows:
+        lax.fori_loop(0, areas, back_area, 0)
     for h in range(heads):
         first = h * 3 * HEAD_DIM
         head = slice(h * HEAD_DIM, (h + 1) * HEAD_DIM)
@@ -1436,6 +1384,32 @@
         d_qkv[:, first + 2 * HEAD_DIM : first + 3 * HEAD_DIM] = d_values[:, head].astype(low)
     keep_qkv = pltpu.make_async_copy(d_qkv, d_qkv_out, load_sem.at[6])
     keep_qkv.start()
+    wide = width // tile
+    short = stage.shape[1]
+
+    def square(row, column):
+        return merge_grad.at[
+            pl.ds(pl.multiple_of(row * short, short), short),
+            pl.ds(pl.multiple_of(column * tile, tile), tile),
+        ]
+
+    def merge_one(k, carry):
+        row, column = k // wide, lax.rem(k, wide)
+        slot = lax.rem(k, 2)
+
+        @pl.when(k >= 2)
+        def _():
+            pltpu.make_async_copy(stage.at[slot], square(0, 0), stage_sem.at[slot]).wait()
+
+        a = attended[:, pl.ds(pl.multiple_of(row * short, short), short)]
+        b = d_attn[:, pl.ds(pl.multiple_of(column * tile, tile), tile)]
+        stage[slot] = mm_tn(a, b).astype(low)
+        pltpu.make_async_copy(stage.at[slot], square(row, column), stage_sem.at[slot]).start()
+        return carry
+
+    lax.fori_loop(0, attended.shape[1] // short * wide, merge_one, 0)
+    for slot in range(2):
+        pltpu.make_async_copy(stage.at[slot], square(0, 0), stage_sem.at[slot]).wait()
     lax.fori_loop(early, turns, pass_by, 0)
     for c in range(pieces):
         at = slice(c * piece, (c + 1) * piece)
@@ -1450,8 +1424,7 @@
     for scatter in (up, down):
         scatter.landed_all()
         scatter.finish()
-    for turn in range(1, n):
-        to_heads(lax.rem(i + turn, n)).wait_send()
+    line.finish()
     sums.all_sent()
 
 
@@ -1471,7 +1444,7 @@
             sds((rows, width), f32),
             sds((total, wide), low),
             sds((8, width), f32),
-            sds((width, width), low),
+            sds((heads * HEAD_DIM, width), low),
             sds((plane_slots(n_dp), k_rows, units), low),
             sds((plane_slots(n_dp), units, down_cols), low),
         ],
@@ -1481,14 +1454,13 @@
             pltpu.VMEM((rows, width), f32),
             pltpu.VMEM((rows, width), f32),
             pltpu.VMEM((total, wide), low),
-            pltpu.VMEM((rows, width), low),
+            pltpu.VMEM((total, heads * HEAD_DIM), low),
             pltpu.VMEM((total, wide), low),
             pltpu.VMEM((total, width), low),
             pltpu.VMEM((total + rows, width), low),
-            pltpu.VMEM((2, math.gcd(256, heads * HEAD_DIM), width), low),
+            pltpu.VMEM((heads * HEAD_DIM, width), low),
             pltpu.VMEM((total, heads * HEAD_DIM), low),
-            pltpu.VMEM((n, rows, heads * HEAD_DIM), low),
-            pltpu.VMEM((rows, width), low),
+            pltpu.VMEM((total, width), low),
             pltpu.VMEM((total, heads * HEAD_DIM), f32),
             pltpu.VMEM((total, heads * HEAD_DIM), f32),
             pltpu.VMEM((chips, k_rows, units), low),
@@ -1502,8 +1474,8 @@
             DMA((n + 1, pieces)),
             scatter_sems(n_dp),
             scatter_sems(n_dp),
-            DMA((2, n)),
-            DMA((2,)),
+            DMA((3, n)),
+            DMA,
             DMA((7,)),
             DMA((2,)),
             DMA((2, chips)),
@@ -1530,7 +1502,7 @@
     d_mod_all,
     noise_sum,
     attend_landed,
-    merge_out,
+    merge_landed,
     hidden,
     x_own,
     d_middle,
@@ -1545,9 +1517,6 @@
     merge_own,
     merge_swapped,
     merge_via,
-    merge_landed,
-    merge_part,
-    merge_got,
     sums_all,
     shares,
     shares_all,
@@ -1556,8 +1525,6 @@
     noise_parts,
     sent,
     came,
-    merge_sent,
-    merge_came,
     grad_sems,
     merge_sems,
     share_sem,
@@ -1575,7 +1542,6 @@
     side = lax.rem(d, 2)
     k_rows, own_cols = mod_w.shape
     merge_cols = merge_own.shape[2]
-    merge_rows = merge_out.shape[0]
     images = d_mod_all.shape[1]
 
     def merge_slab(at):
@@ -1748,23 +1714,6 @@
     for turn in range(1, n):
         to_line(shares, shares_all, share_sem, turn).start()
 
-    merge.landed_all()
-    merge_sums = LineScatter(
-        n, i, merge_rows, merge_cols, merge_part, merge_got, merge_sent, merge_came
-    )
-
-    def merge_block(q, carry):
-        j = jnp.where(2 * i < n - 1, n - 1 - q, q)
-        here = rows_of(j, merge_rows)
-        total = merge_landed[0, here, :].astype(f32)
-        for m in range(1, merge_landed.shape[0]):
-            total += merge_landed[m, here, :].astype(f32)
-        merge_part[here, :] = total.astype(low)
-        merge_sums.at_end(j, 0)
-        return carry
-
-    lax.fori_loop(0, n, merge_block, 0)
-
     mean = mean * (1.0 / width)
     for c, at in enumerate(tiles):
         v = x_own[:, at].astype(f32) * root
@@ -1777,9 +1726,6 @@
     own_mod = d_mod_all.at[d]
     for flip in range(1, n_dp):
         to_plane(own_mod, d_mod_all, mod_sem, flip).start()
-    for t in range(n - 1, 1, -1):
-        for near in (True, False):
-            merge_sums.pass_on(t, 0, near)
     for flip in range(1, n_dp):
         from_plane(own_mod, d_mod_all, mod_sem, flip).wait_recv()
     flat = d_mod_all[...].reshape(n_dp * images, own_cols).astype(low)
@@ -1793,9 +1739,9 @@
     for flip in range(1, n_dp):
         to_plane(noise_parts.at[d ^ flip], noise_sum, noise_sem, flip).start()
     noise_sum[d] = noise_parts[d]
-    merge_out[...] = merge_sums.own_value(0)
     for flip in range(1, n_dp):
         from_plane(noise_parts.at[d ^ flip], noise_sum, noise_sem, flip).wait_recv()
+    merge.landed_all()
     grad.landed_all()
     grad.finish()
     merge.finish()
@@ -1806,7 +1752,6 @@
         to_plane(own_mod, d_mod_all, mod_sem, flip).wait_send()
         to_plane(noise_parts.at[d ^ flip], noise_sum, noise_sem, flip).wait_send()
     sums.all_sent()
-    merge_sums.all_sent()
 
 
 def last(n, n_dp, operands, shapes, number, tile=512):
@@ -1824,9 +1769,9 @@
             sds((n_dp, images, own_cols), f32),
             sds((n_dp, images, k_rows), f32),
             sds((plane_slots(n_dp), k_rows, wide), low),
-            sds((merge_rows, merge_cols), f32),
+            sds((plane_slots(n_dp), merge_rows, merge_cols), low),
         ],
-        [VMEM] * 3 + [HBM] + [VMEM],
+        [VMEM] * 3 + [HBM] * 2,
         [
             pltpu.VMEM((total, width), low),
             pltpu.VMEM((rows, width), low),
@@ -1839,12 +1784,9 @@
             pltpu.VMEM((chips, k_rows, wide), low),
             pltpu.VMEM((chips, k_rows, wide), low),
             pltpu.VMEM((k_rows, wide), low),
-            pltpu.VMEM((chips, n * merge_rows, merge_cols), low),
-            pltpu.VMEM((chips, n * merge_rows, merge_cols), low),
-            pltpu.VMEM((n * merge_rows, merge_cols), low),
-            pltpu.VMEM((plane_slots(n_dp), n * merge_rows, merge_cols), low),
-            pltpu.VMEM((n * merge_rows, merge_cols), low),
-            pltpu.VMEM(((n + 1) * merge_rows, merge_cols), low),
+            pltpu.VMEM((chips, merge_rows, merge_cols), low),
+            pltpu.VMEM((chips, merge_rows, merge_cols), low),
+            pltpu.VMEM((merge_rows, merge_cols), low),
             pltpu.VMEM((8, width), f32),
             pltpu.VMEM((n, images, own_cols), f32),
             pltpu.VMEM((n, images, own_cols), f32),
@@ -1853,8 +1795,6 @@
             pltpu.VMEM((n_dp, images, k_rows), f32),
             DMA((n, pieces)),
             DMA((n + 1, pieces)),
-            DMA((n, 1)),
-            DMA((n + 1, 1)),
             scatter_sems(n_dp),
             scatter_sems(n_dp),
             DMA((2, n)),
@@ -1891,13 +1831,14 @@
     up_slots,
     down_slots,
     attend_slots,
+    merge_slots,
     up_sum,
     down_sum,
     attend_sum,
+    merge_sum,
     modulate,
     block,
     inputs,
-    merge,
     sems,
 ):
     low, f32 = jnp.bfloat16, jnp.float32
@@ -1908,9 +1849,9 @@
                 (up_in, up_slots),
                 (down_in, down_slots),
                 (attend_in, attend_slots),
+                (merge_in, merge_slots),
                 (block_in, block),
                 (input_in, inputs),
-                (merge_in, merge),
             )
         )
     ]
@@ -1921,9 +1862,9 @@
                 (up_sum, up_out),
                 (down_sum, down_out),
                 (attend_sum, attend_out),
+                (merge_sum, merge_out),
                 (block, block_out),
                 (inputs, input_out),
-                (merge, merge_out),
                 (modulate, modulate_out),
             )
         )
@@ -1953,12 +1894,17 @@
         lax.fori_loop(0, height // chunk, one, 0)
 
     for k, (slots, total) in enumerate(
-        ((up_slots, up_sum), (down_slots, down_sum), (attend_slots, attend_sum))
+        (
+            (up_slots, up_sum),
+            (down_slots, down_sum),
+            (attend_slots, attend_sum),
+            (merge_slots, merge_sum),
+        )
     ):
         loads[k].wait()
         add(slots, total)
         stores[k].start()
-    for k in range(3, 6):
+    for k in range(4, 6):
         loads[k].wait()
         stores[k].start()
     for store in stores:
@@ -1968,7 +1914,7 @@
 def final(noise_own, noise_all, d_mod, noise_sums, up, down, attend, block, inputs, merge):
     sds, f32 = jax.ShapeDtypeStruct, jnp.float32
     own_cols, k_rows = d_mod.shape[2], noise_all.shape[2]
-    sums = [sds(a.shape[1:], f32) for a in (up, down, attend)]
+    sums = [sds(a.shape[1:], f32) for a in (up, down, attend, merge)]
     modulate = sds((k_rows, own_cols), f32)
     return pl.pallas_call(
         final_kernel,
@@ -1977,7 +1923,7 @@
             sds(inputs.shape, inputs.dtype),
             sds(noise_own.shape, f32),
             sums[2],
-            sds(merge.shape, f32),
+            sums[3],
             sums[0],
             sums[1],
             modulate,
@@ -1986,7 +1932,7 @@
         out_specs=[HBM, HBM, VMEM] + [HBM] * 5,
         scratch_shapes=[
             pltpu.VMEM(a.shape, a.dtype)
-            for a in (up, down, attend, *sums, modulate, block, inputs, merge)
+            for a in (up, down, attend, merge, *sums, modulate, block, inputs)
         ]
         + [DMA((2, 7))],
         compiler_params=pltpu.CompilerParams(vmem_limit_bytes=60 * 1024 * 1024),
@@ -2017,7 +1963,7 @@
         hidden_first,
         packed,
         lse,
-        att_rows,
+        attended,
         attn_out,
         middle,
         hidden_second,
@@ -2065,7 +2011,7 @@
             image_sizes,
             cotangent,
             attn_out,
-            att_rows,
+            attended,
             packed,
             mlp_part,
             merge_full,
@@ -2075,7 +2021,7 @@
         (block_input.shape, wide, units, k_rows, down_weight.shape[1], lse.shape[0]),
         2,
     )
-    input_grad, d_mod_all, noise_sums, attend_landed, merge_part = last(
+    input_grad, d_mod_all, noise_sums, attend_landed, merge_landed = last(
         n,
         n_dp,
         (
@@ -2112,7 +2058,7 @@
             attend_landed,
             block_output,
             input_grad,
-            merge_part,
+            merge_landed,
         )
     )
 

time: 537 us -> 528 us (0.983)
  Pallas kernels: 536 us -> 527 us
    pallas_call x1, Pallas kernels: 109 us -> 101 us  [last(): call(functools.partial(last_kernel, n, n_dp, tile), number, 'last', [VMEM...]
where the time goes in v7:
time: 528 us
  Pallas kernels  527 us (100%)
    pallas_call x1, Pallas kernels, front(): call(functools.partial(front_kernel, n, n_dp, heads, 512), number, 'front...  187 us
    pallas_call x1, Pallas kernels, back(): call(functools.partial(back_kernel, n, n_dp, heads, tile), number, 'back'...  116 us
    pallas_call x1, Pallas kernels, ffn(): call(functools.partial(ffn_kernel, n, tile, grad_tile), collective_id, 'f...  113 us
    pallas_call x1, Pallas kernels, last(): call(functools.partial(last_kernel, n, n_dp, tile), number, 'last', [VMEM...  101 us

profile of v7, /device:TPU:0, one launch (start us, length us, event | category | flops | bytes accessed | tf_op | source)
XLA Modules:
  0.0 527.6 jit_solution(7249001642373584948)
XLA Ops:
  0.6 186.8 %front.1 = (bf16[1024,2048]{1,0:T(8,128)(2,1)}, bf16[1024,2048]{1,0:T(8,128)(2,1)}, bf16[1024,1536]{1,0:T(8,128)(2,1)}, f32[16,256]{1,0:T(8,128)}, bf16[1024,512...) custom-call(bf16[256,2048]{1,0:T(8,128)(2,1)} %x_hbm.1, ...), custom_call_target="tpu_custom_call" | custom-call | flops 6442450944 | bytes 1048576 | tf_op jit(solution)/shard_map/front/pallas_call | solution.py:966
  187.4 112.7 %ffn.1 = (f32[256,2048]{1,0:T(8,128)}, bf16[1024,2048]{1,0:T(8,128)(2,1)}, bf16[2048,2048]{1,0:T(8,128)(2,1)}, bf16[2048,2048]{1,0:T(8,128)(2,1)}) custom-call(bf16[256,2048]{1,0:T(8,128)(2,1)} %get-tuple-element.39.own_hidden, f32[4,8,2048]{2,1,0:T(8,128)} %get-tuple-element.40.table, bf16[1024,2048]{1,0:T(8,128)(2,1)} %get-tuple-element.41.d_mlp_hbm, ...), custom_call_target="tpu_custom_call" | custom-call | flops 51539607552 | bytes 1048576 | tf_op jit(solution)/shard_map/ffn/pallas_call | solution.py:422
  300.2 116.5 %back.1 = (bf16[256,2048]{1,0:T(8,128)(2,1)}, f32[256,2048]{1,0:T(8,128)}, bf16[1024,1536]{1,0:T(8,128)(2,1)}, f32[8,2048]{1,0:T(8,128)}, bf16[512,2048]{1,0:T(8...) custom-call(f32[256,2048]{1,0:T(8,128)} %get-tuple-element.44.d_hidden, ...), custom_call_target="tpu_custom_call" | custom-call | flops 10737418240 | bytes 1048576 | tf_op jit(solution)/shard_map/back/pallas_call | solution.py:1437
  416.6 100.7 %last.1 = (bf16[256,2048]{1,0:T(8,128)(2,1)}, f32[8,4,3072]{2,1,0:T(4,128)}, f32[8,4,256]{2,1,0:T(4,128)}, bf16[3,256,1536]{2,1,0:T(8,128)(2,1)}, bf16[3,512,256]{2,1,0:T(8,128)(2,1)}) custom-call(bf16[1024,1536]{1,0:T(8,128)(2,1)} %get-tuple-element.54.d_qkv, f32[8,2048]{1,0:T(8,128)} %get-tuple-element.55.sums_in, f32[4,8,2048]{2,1,0:T(8,128)} %get-tuple-element.40.table, ...), custom_call_target="tpu_custom_call" | custom-call | flops 12884901888 | bytes 1048576 | tf_op jit(solution)/shard_map/last/pallas_call | solution.py:1762
  517.4 10.0 %final.1 = (bf16[256,2048]{1,0:T(8,128)(2,1)}, bf16[256,2048]{1,0:T(8,128)(2,1)}, f32[4,2048]{1,0:T(4,128)}, f32[256,1536]{1,0:T(8,128)}, f32[512,256]{1,0:T(8,1...) custom-call(bf16[4,2048]{1,0:T(4,128)(2,1)} %noise_own.3, ...), custom_call_target="tpu_custom_call" | custom-call | tf_op jit(solution)/shard_map/final/pallas_call | solution.py:1919

commit v8 on v7

--- a/solution.py
+++ b/solution.py
@@ -1294,8 +1294,13 @@
     line = LineGather(
         n, i, rows, d_attn.at[own_rows], d_attn, line_sem.at[0], line_sem.at[1], line_sem.at[2]
     )
-    line.start()
-    lax.fori_loop(0, (n - 1) * pieces, ends, 0)
+    first_core = side == 0
+
+    def send_rows():
+        line.start()
+        lax.fori_loop(0, (n - 1) * pieces, ends, 0)
+
+    pl.when(first_core)(send_rows)
     for m in range(chips):
         pltpu.make_async_copy(up_slab(2 * m + side), up_own.at[m], own_sem.at[0, m]).wait()
         pltpu.make_async_copy(down_slab(2 * m + side), down_own.at[m], own_sem.at[1, m]).wait()
@@ -1361,6 +1366,10 @@
             d_att[here, :] = mm_nt(d_attn[here, :], merge[...]).astype(low)
             if area == rows:
                 back_area(j, 0)
+
+        @pl.when((q == 0) & jnp.logical_not(first_core))
+        def _():
+            send_rows()
 
         @pl.when(q == 0)
         def _():

time: 528 us -> 524 us (level)
    pallas_call x1, Pallas kernels: 116 us -> 106 us  [back(): call(functools.partial(back_kernel, n, n_dp, heads, tile), number, 'back'...]
    pallas_call x1, Pallas kernels: 101 us -> 107 us  [last(): call(functools.partial(last_kernel, n, n_dp, tile), number, 'last', [VMEM...]
where the time goes in v8:
time: 524 us
  Pallas kernels  523 us (100%)
    pallas_call x1, Pallas kernels, front(): call(functools.partial(front_kernel, n, n_dp, heads, 512), number, 'front...  187 us
    pallas_call x1, Pallas kernels, ffn(): call(functools.partial(ffn_kernel, n, tile, grad_tile), collective_id, 'f...  113 us
    pallas_call x1, Pallas kernels, last(): call(functools.partial(last_kernel, n, n_dp, tile), number, 'last', [VMEM...  107 us
    pallas_call x1, Pallas kernels, back(): call(functools.partial(back_kernel, n, n_dp, heads, tile), number, 'back'...  106 us

profile of v8, /device:TPU:0, one launch (start us, length us, event | category | flops | bytes accessed | tf_op | source)
XLA Modules:
  0.0 524.0 jit_solution(14063459883772956390)
XLA Ops:
  0.6 186.8 %front.1 = (bf16[1024,2048]{1,0:T(8,128)(2,1)}, bf16[1024,2048]{1,0:T(8,128)(2,1)}, bf16[1024,1536]{1,0:T(8,128)(2,1)}, f32[16,256]{1,0:T(8,128)}, bf16[1024,512...) custom-call(bf16[256,2048]{1,0:T(8,128)(2,1)} %x_hbm.1, ...), custom_call_target="tpu_custom_call" | custom-call | flops 6442450944 | bytes 1048576 | tf_op jit(solution)/shard_map/front/pallas_call | solution.py:966
  187.4 112.7 %ffn.1 = (f32[256,2048]{1,0:T(8,128)}, bf16[1024,2048]{1,0:T(8,128)(2,1)}, bf16[2048,2048]{1,0:T(8,128)(2,1)}, bf16[2048,2048]{1,0:T(8,128)(2,1)}) custom-call(bf16[256,2048]{1,0:T(8,128)(2,1)} %get-tuple-element.39.own_hidden, f32[4,8,2048]{2,1,0:T(8,128)} %get-tuple-element.40.table, bf16[1024,2048]{1,0:T(8,128)(2,1)} %get-tuple-element.41.d_mlp_hbm, ...), custom_call_target="tpu_custom_call" | custom-call | flops 51539607552 | bytes 1048576 | tf_op jit(solution)/shard_map/ffn/pallas_call | solution.py:422
  300.2 106.3 %back.1 = (bf16[256,2048]{1,0:T(8,128)(2,1)}, f32[256,2048]{1,0:T(8,128)}, bf16[1024,1536]{1,0:T(8,128)(2,1)}, f32[8,2048]{1,0:T(8,128)}, bf16[512,2048]{1,0:T(8...) custom-call(f32[256,2048]{1,0:T(8,128)} %get-tuple-element.44.d_hidden, ...), custom_call_target="tpu_custom_call" | custom-call | flops 10737418240 | bytes 1048576 | tf_op jit(solution)/shard_map/back/pallas_call | solution.py:1446
  406.5 107.3 %last.1 = (bf16[256,2048]{1,0:T(8,128)(2,1)}, f32[8,4,3072]{2,1,0:T(4,128)}, f32[8,4,256]{2,1,0:T(4,128)}, bf16[3,256,1536]{2,1,0:T(8,128)(2,1)}, bf16[3,512,256]{2,1,0:T(8,128)(2,1)}) custom-call(bf16[1024,1536]{1,0:T(8,128)(2,1)} %get-tuple-element.54.d_qkv, f32[8,2048]{1,0:T(8,128)} %get-tuple-element.55.sums_in, f32[4,8,2048]{2,1,0:T(8,128)} %get-tuple-element.40.table, ...), custom_call_target="tpu_custom_call" | custom-call | flops 12884901888 | bytes 1048576 | tf_op jit(solution)/shard_map/last/pallas_call | solution.py:1771
  513.8 10.0 %final.1 = (bf16[256,2048]{1,0:T(8,128)(2,1)}, bf16[256,2048]{1,0:T(8,128)(2,1)}, f32[4,2048]{1,0:T(4,128)}, f32[256,1536]{1,0:T(8,128)}, f32[512,256]{1,0:T(8,1...) custom-call(bf16[4,2048]{1,0:T(4,128)(2,1)} %noise_own.3, ...), custom_call_target="tpu_custom_call" | custom-call | tf_op jit(solution)/shard_map/final/pallas_call | solution.py:1928

commit v9 on v8

--- a/solution.py
+++ b/solution.py
@@ -300,8 +300,10 @@
 
         lax.fori_loop(0, width // tile, gated, 0)
 
+        wide = math.gcd(units, 2 * tile)
+
         def first(c, carry):
-            at = pl.ds(pl.multiple_of(c * tile, tile), tile)
+            at = pl.ds(pl.multiple_of(c * wide, wide), wide)
             pre = mm(hidden[here, :], up[:, at])
             d_act = mm_nt(d_mlp[here, :], down[at, :])
             cdf = 0.5 * (1.0 + lax.erf(pre * (0.5**0.5)))
@@ -310,7 +312,7 @@
             d_pre[here, at] = (d_act * (cdf + pre * density)).astype(jnp.bfloat16)
             return carry
 
-        lax.fori_loop(0, units // tile, first, 0)
+        lax.fori_loop(0, units // wide, first, 0)
 
         def second(c, carry):
             at = pl.ds(pl.multiple_of(c * tile, tile), tile)
@@ -321,12 +323,14 @@
 
         lax.fori_loop(0, width // tile, second, 0)
 
+        broad = math.gcd(width, 2 * tile)
+
         def third(c, carry):
-            at = pl.ds(pl.multiple_of(c * tile, tile), tile)
+            at = pl.ds(pl.multiple_of(c * broad, broad), broad)
             mlp[here, at] = mm(activated[here, :], down[:, at]).astype(jnp.bfloat16)
             return carry
 
-        lax.fori_loop(0, width // tile, third, 0)
+        lax.fori_loop(0, width // broad, third, 0)
 
     def visit(q, carry):
         s = (q + 1) // 2

time: 524 us -> 524 us (level)
  no operation moved by 1% of the time
where the time goes in v9:
time: 524 us
  Pallas kernels  523 us (100%)
    pallas_call x1, Pallas kernels, front(): call(functools.partial(front_kernel, n, n_dp, heads, 512), number, 'front...  187 us
    pallas_call x1, Pallas kernels, ffn(): call(functools.partial(ffn_kernel, n, tile, grad_tile), collective_id, 'f...  113 us
    pallas_call x1, Pallas kernels, last(): call(functools.partial(last_kernel, n, n_dp, tile), number, 'last', [VMEM...  107 us
    pallas_call x1, Pallas kernels, back(): call(functools.partial(back_kernel, n, n_dp, heads, tile), number, 'back'...  106 us

profile of v9, /device:TPU:0, one launch (start us, length us, event | category | flops | bytes accessed | tf_op | source)
XLA Modules:
  0.0 523.9 jit_solution(13832845915848454071)
XLA Ops:
  0.6 186.8 %front.1 = (bf16[1024,2048]{1,0:T(8,128)(2,1)}, bf16[1024,2048]{1,0:T(8,128)(2,1)}, bf16[1024,1536]{1,0:T(8,128)(2,1)}, f32[16,256]{1,0:T(8,128)}, bf16[1024,512...) custom-call(bf16[256,2048]{1,0:T(8,128)(2,1)} %x_hbm.1, ...), custom_call_target="tpu_custom_call" | custom-call | flops 6442450944 | bytes 1048576 | tf_op jit(solution)/shard_map/front/pallas_call | solution.py:970
  187.4 113.1 %ffn.1 = (f32[256,2048]{1,0:T(8,128)}, bf16[1024,2048]{1,0:T(8,128)(2,1)}, bf16[2048,2048]{1,0:T(8,128)(2,1)}, bf16[2048,2048]{1,0:T(8,128)(2,1)}) custom-call(bf16[256,2048]{1,0:T(8,128)(2,1)} %get-tuple-element.39.own_hidden, f32[4,8,2048]{2,1,0:T(8,128)} %get-tuple-element.40.table, bf16[1024,2048]{1,0:T(8,128)(2,1)} %get-tuple-element.41.d_mlp_hbm, ...), custom_call_target="tpu_custom_call" | custom-call | flops 51539607552 | bytes 1048576 | tf_op jit(solution)/shard_map/ffn/pallas_call | solution.py:426
  300.6 105.7 %back.1 = (bf16[256,2048]{1,0:T(8,128)(2,1)}, f32[256,2048]{1,0:T(8,128)}, bf16[1024,1536]{1,0:T(8,128)(2,1)}, f32[8,2048]{1,0:T(8,128)}, bf16[512,2048]{1,0:T(8...) custom-call(f32[256,2048]{1,0:T(8,128)} %get-tuple-element.44.d_hidden, ...), custom_call_target="tpu_custom_call" | custom-call | flops 10737418240 | bytes 1048576 | tf_op jit(solution)/shard_map/back/pallas_call | solution.py:1450
  406.3 107.4 %last.1 = (bf16[256,2048]{1,0:T(8,128)(2,1)}, f32[8,4,3072]{2,1,0:T(4,128)}, f32[8,4,256]{2,1,0:T(4,128)}, bf16[3,256,1536]{2,1,0:T(8,128)(2,1)}, bf16[3,512,256]{2,1,0:T(8,128)(2,1)}) custom-call(bf16[1024,1536]{1,0:T(8,128)(2,1)} %get-tuple-element.54.d_qkv, f32[8,2048]{1,0:T(8,128)} %get-tuple-element.55.sums_in, f32[4,8,2048]{2,1,0:T(8,128)} %get-tuple-element.40.table, ...), custom_call_target="tpu_custom_call" | custom-call | flops 12884901888 | bytes 1048576 | tf_op jit(solution)/shard_map/last/pallas_call | solution.py:1775
  513.7 10.0 %final.1 = (bf16[256,2048]{1,0:T(8,128)(2,1)}, bf16[256,2048]{1,0:T(8,128)(2,1)}, f32[4,2048]{1,0:T(4,128)}, f32[256,1536]{1,0:T(8,128)}, f32[512,256]{1,0:T(8,1...) custom-call(bf16[4,2048]{1,0:T(4,128)(2,1)} %noise_own.3, ...), custom_call_target="tpu_custom_call" | custom-call | tf_op jit(solution)/shard_map/final/pallas_call | solution.py:1932
